TPU v7x, 32 devices: a whole 2x2x4 slice. The times are simulated.
32 devices in a mesh: dp: 8 (over z, y), fsdp: 4 (over x, core).
Axes of the slice: x: 2, y: 2, z: 4, core: 2. Of those that a mesh axis runs over, the one named last changes fastest.
Arguments:
- tokens: bfloat16 [8192, 2048], P(('dp', 'fsdp')), may hold values from -6 to 6
- widths: int32 [8], P('dp'), may hold values from 0 to 3, as said below
- cotangent: bfloat16 [8192, 2048], P(('dp', 'fsdp')), may hold values from -6 to 6
- in_weight: float32 [2048, 8512], P(('dp', 'fsdp')), may hold values from -0.125 to 0.125
- in_first: float32 [2048, 8512], P(('dp', 'fsdp')), may hold values from -0.0029296875 to 0.0029296875
- in_second: float32 [2048, 8512], P(('dp', 'fsdp')), may hold values from 3.8685798e-08 to 1.5474319e-07
- out_weight: float32 [4096, 2048], P(('dp', 'fsdp')), may hold values from -0.09375 to 0.09375
- out_first: float32 [4096, 2048], P(('dp', 'fsdp')), may hold values from -0.0029296875 to 0.0029296875
- out_second: float32 [4096, 2048], P(('dp', 'fsdp')), may hold values from 3.8685798e-08 to 1.5474319e-07
- vectors: float32 [28096], replicated, may hold values from -8 to 3
- vector_first: float32 [28096], replicated, may hold values from -0.0078125 to 0.0078125
- vector_second: float32 [28096], replicated, may hold values from 1.5474319e-07 to 6.1897276e-07
Outputs:
- layer_out: bfloat16 [8192, 2048], P(('dp', 'fsdp'))
- token_grad: bfloat16 [8192, 2048], P(('dp', 'fsdp'))
- in_grad: float32 [2048, 8512], P(('dp', 'fsdp'))
- out_grad: float32 [4096, 2048], P(('dp', 'fsdp'))
- vector_grad: float32 [28096], replicated
- grad_norm: float32 [], replicated
- in_moment: float32 [2048, 8512], P(('dp', 'fsdp'))
- in_square: float32 [2048, 8512], P(('dp', 'fsdp'))
- in_master: float32 [2048, 8512], P(('dp', 'fsdp'))
- in_rounded: bfloat16 [2048, 8512], P(('dp', 'fsdp'))
- out_moment: float32 [4096, 2048], P(('dp', 'fsdp'))
- out_square: float32 [4096, 2048], P(('dp', 'fsdp'))
- out_master: float32 [4096, 2048], P(('dp', 'fsdp'))
- out_rounded: bfloat16 [4096, 2048], P(('dp', 'fsdp'))
- vector_moment: float32 [28096], replicated
- vector_square: float32 [28096], replicated
- vector_master: float32 [28096], replicated
Inputs may be any that keep to these rules, and one draw needn't show every extreme that they name: `widths`: every width index 0, 1, 2 and 3 occurs in every draw.
All inputs are finite; a program needn't handle non-finite values.
Results may differ from a plain program's by a relative error of at most 0.0087.
The roundings to bfloat16 on the way count: a program that leaves them out, or rounds other values in their place, can miss the bound.
Values may be sent and summed in bfloat16 or wider, within the bound.
A program may use at most 232 MiB of HBM per device.

v0:
```python
from functools import partial

import jax
import jax.numpy as jnp
from jax import lax
from jax.sharding import PartitionSpec as P

D = 2048
HEADS = 64
HEAD_DIM = 64
STATE = 128
CONV = 4
SPAN = 256
STEP = 10
INNER = 4096
XBC = 4352


norm_eps = 1e-05
clip_norm = 1.0
beta_first = 0.5
beta_second = 0.5
adam_eps = 1e-08
weight_decay = 0.1
rate_in_proj = 0.03
rate_out_proj = 0.02
rate_vectors = 0.5
highest = lax.Precision.HIGHEST


def passed_along(value, axis, steps):
    count = lax.axis_size(axis)
    initial, last = (max(0, -steps), min(count, count - steps))
    return lax.ppermute(value, axis, [(source, source + steps) for source in range(initial, last)])


def carried_in(part, axis, combine, identity):
    place = lax.axis_index(axis)
    gathered = jax.tree.map(lambda a: lax.all_gather(a, axis), part)
    state = jax.tree.map(lambda a, e: jnp.zeros_like(a) + jnp.asarray(e, a.dtype), part, identity)

    def one(lap, state):
        return combine(
            state, jax.tree.map(lambda a: lax.dynamic_index_in_dim(a, lap, 0, False), gathered)
        )

    return lax.fori_loop(0, place, one, state)


def carried_in_2(x, axis, combine, identity):
    peers, here = (lax.axis_size(axis), lax.axis_index(axis))
    everything = jax.tree.map(
        lambda part, kind: lax.all_gather(part.astype(kind), axis),
        x,
        jax.tree.map(lambda a: jnp.bfloat16 if a.dtype == jnp.float32 else a.dtype, x),
    )
    start = jax.tree.map(
        lambda part, zero: jnp.broadcast_to(jnp.asarray(zero, part.dtype), part.shape), x, identity
    )

    def lap(k, before):
        at = peers - 1 - k
        reached = at > here
        new = combine(
            before, jax.tree.map(lambda part, own: part[at].astype(own.dtype), everything, x)
        )
        return jax.tree.map(lambda a, b: jnp.where(reached, a, b), new, before)

    return lax.fori_loop(0, peers, lap, start)


def shortened(x):
    return jax.tree.map(lambda a: a.astype(jnp.bfloat16) if a.dtype == jnp.float32 else a, x)


def unpack(vectors):
    offset = D + INNER
    taps_end = offset + CONV * XBC
    heads_start = taps_end + XBC
    norm_gain = vectors[:D]
    gate_gain = vectors[D:offset]
    filter_taps = vectors[offset:taps_end].reshape(CONV, XBC)
    filter_bias = vectors[taps_end:heads_start]
    step_bias = vectors[heads_start : heads_start + HEADS]
    decay_log = vectors[heads_start + HEADS : heads_start + 2 * HEADS]
    skip_gain = vectors[heads_start + 2 * HEADS : heads_start + 3 * HEADS]
    return (norm_gain, gate_gain, filter_taps, filter_bias, step_bias, decay_log, skip_gain)


def rms_scale(values, gain_vector):
    return (
        values
        * lax.rsqrt(jnp.mean(values * values, axis=-1, keepdims=True) + norm_eps)
        * gain_vector[None, :]
    )


def causal_filter(signal, previous, filter_taps, filter_bias):
    padded = jnp.concatenate([previous, signal], axis=0)
    length = signal.shape[0]
    summed = filter_bias[None, :] + filter_taps[0][None, :] * padded[0:length]
    for offset in range(1, CONV):
        summed = summed + filter_taps[offset][None, :] * padded[offset : offset + length]
    return summed


def span_apply(carry_state, values, step_sizes, key_rows, query_rows, decay_rates):
    block_rows = values.shape[0]
    log_sums = jnp.cumsum(step_sizes * decay_rates[None, :], axis=0)
    weighted = values * step_sizes[:, :, None]
    causal = jnp.arange(block_rows)[:, None] >= jnp.arange(block_rows)[None, :]
    log_heads = log_sums.T
    differences = log_heads[:, :, None] - log_heads[:, None, :]
    decays = jnp.exp(jnp.where(causal[None], differences, 0.0)) * causal[None].astype(jnp.float32)
    intersection = jnp.dot(query_rows, key_rows.T, precision=highest)
    mixing = decays * intersection[None]
    within = jnp.einsum("hij,jhp->ihp", mixing, weighted, precision=highest)
    carried = (
        jnp.einsum("in,hpn->ihp", query_rows, carry_state, precision=highest)
        * jnp.exp(log_sums)[:, :, None]
    )
    tail_decay = jnp.exp(log_sums[-1][None, :] - log_sums)
    renewed = carry_state * jnp.exp(log_sums[-1])[:, None, None] + jnp.einsum(
        "jhp,jn->hpn", weighted * tail_decay[:, :, None], key_rows, precision=highest
    )
    return (renewed, within + carried)


def select_columns(matrix, heads_on):
    inner_on = heads_on * HEAD_DIM
    return jnp.concatenate(
        [
            matrix[:, :inner_on],
            matrix[:, INNER : INNER + inner_on],
            matrix[:, 2 * INNER : 2 * INNER + 2 * STATE + heads_on],
        ],
        axis=1,
    )


def spread_columns(matrix, heads_on):
    inner_on = heads_on * HEAD_DIM
    row_count = matrix.shape[0]
    inner_gap = jnp.zeros((row_count, INNER - inner_on), jnp.float32)
    head_gap = jnp.zeros((row_count, HEADS - heads_on), jnp.float32)
    return jnp.concatenate(
        [
            matrix[:, :inner_on],
            inner_gap,
            matrix[:, inner_on : 2 * inner_on],
            inner_gap,
            matrix[:, 2 * inner_on :],
            head_gap,
        ],
        axis=1,
    )


def project_in(normed_low, weight_in, heads_on):
    return spread_columns(
        jnp.dot(
            normed_low, select_columns(weight_in, heads_on), preferred_element_type=jnp.float32
        ),
        heads_on,
    )


def project_in_back(grad_low, weight_in, heads_on):
    grad_on = select_columns(grad_low, heads_on)
    return lax.dot_general(
        grad_on,
        select_columns(weight_in, heads_on),
        (((1,), (1,)), ((), ())),
        preferred_element_type=jnp.float32,
    )


def project_out(gated_low, weight_out, heads_on):
    inner_on = heads_on * HEAD_DIM
    return jnp.dot(
        gated_low[:, :inner_on], weight_out[:inner_on], preferred_element_type=jnp.float32
    )


def project_out_back(cotangent, weight_out, heads_on):
    inner_on = heads_on * HEAD_DIM
    row_count = cotangent.shape[0]
    propagated = lax.dot_general(
        cotangent,
        weight_out[:inner_on],
        (((1,), (1,)), ((), ())),
        preferred_element_type=jnp.float32,
    )
    return jnp.concatenate(
        [propagated, jnp.zeros((row_count, INNER - inner_on), jnp.float32)], axis=1
    )


def row_term(left, right, count):
    piece = lax.slice_in_dim(left, 0, count, axis=1)
    return lax.dot_general(
        piece, right, (((0,), (0,)), ((), ())), preferred_element_type=jnp.float32
    )


def prepare(mixed_part, rim_rows, step_raw, vectors, head_mask):
    norm_gain, gate_gain, filter_taps, filter_bias, step_bias, decay_log, skip_gain = unpack(
        vectors
    )
    length = mixed_part.shape[0]
    activated = jax.nn.silu(causal_filter(mixed_part, rim_rows, filter_taps, filter_bias))
    values = activated[:, :INNER].reshape(length, HEADS, HEAD_DIM) * head_mask[None, :, None]
    key_rows = activated[:, INNER : INNER + STATE]
    query_rows = activated[:, INNER + STATE :]
    step_sizes = jax.nn.softplus(step_raw + step_bias[None, :])
    decay_rates = -jnp.exp(decay_log)
    return (values, step_sizes, key_rows, query_rows, decay_rates)


def local_scan(values, step_sizes, key_rows, query_rows, decay_rates):
    length = values.shape[0]
    blocks = length // SPAN

    def advance(carry_state, pieces):
        return span_apply(carry_state, pieces[0], pieces[1], pieces[2], pieces[3], decay_rates)

    last_state, outputs = lax.scan(
        advance,
        jnp.zeros((HEADS, HEAD_DIM, STATE), jnp.float32),
        (
            values.reshape(blocks, SPAN, HEADS, HEAD_DIM),
            step_sizes.reshape(blocks, SPAN, HEADS),
            key_rows.reshape(blocks, SPAN, STATE),
            query_rows.reshape(blocks, SPAN, STATE),
        ),
    )
    log_sums = jnp.cumsum(step_sizes * decay_rates[None, :], axis=0)
    return (outputs.reshape(length, HEADS, HEAD_DIM), jnp.exp(log_sums[-1]), last_state, log_sums)


def finish(
    partial_out,
    log_sums,
    query_rows,
    entering,
    values,
    gate_part,
    vectors,
    head_mask,
    channel_count,
):
    norm_gain, gate_gain, filter_taps, filter_bias, step_bias, decay_log, skip_gain = unpack(
        vectors
    )
    length = values.shape[0]
    carried = (
        jnp.einsum("tn,hpn->thp", query_rows, entering, precision=highest)
        * jnp.exp(log_sums)[:, :, None]
    )
    combined = partial_out + carried + skip_gain[None, :, None] * values
    gated = combined.reshape(length, INNER) * jax.nn.silu(gate_part)
    inverse_rms = lax.rsqrt(
        jnp.sum(gated * gated, axis=-1, keepdims=True) / channel_count + norm_eps
    )
    return gated * inverse_rms * gate_gain[None, :]


def join_forward(earlier, later):
    return (earlier[0] * later[0], earlier[1] * later[0][:, None, None] + later[1])


def join_backward(earlier, later):
    return (earlier[0] * later[0], later[1] + later[0][:, None, None] * earlier[1])


def adamw(weight, moment, square, gradient, step_rate):
    moment_new = beta_first * moment + (1.0 - beta_first) * gradient
    square_new = beta_second * square + (1.0 - beta_second) * gradient * gradient
    moment_hat = moment_new / (1.0 - beta_first**STEP)
    square_hat = square_new / (1.0 - beta_second**STEP)
    weight_new = weight - step_rate * (
        moment_hat / (jnp.sqrt(square_hat) + adam_eps) + weight_decay * weight
    )
    return (moment_new, square_new, weight_new)


def on_device(
    tokens,
    widths,
    cotangent,
    in_weight,
    in_first,
    in_second,
    out_weight,
    out_first,
    out_second,
    vectors,
    vector_first,
    vector_second,
):
    width_index = widths[0]
    inputs = tokens.astype(jnp.float32)
    length = inputs.shape[0]
    active = HEADS // 8 * jnp.left_shift(jnp.int32(1), width_index)
    head_mask = (jnp.arange(HEADS, dtype=jnp.int32) < active).astype(jnp.float32)
    channel_mask = jnp.repeat(head_mask, HEAD_DIM)
    column_mask = jnp.concatenate(
        [channel_mask, channel_mask, jnp.ones((2 * STATE,), jnp.float32), head_mask]
    )
    channel_count = (active * HEAD_DIM).astype(jnp.float32)
    head_counts = [HEADS // 8 * 2**exponent for exponent in range(4)]
    normed, norm_pull = jax.vjp(
        lambda values, params: rms_scale(values, params[:D]), inputs, vectors
    )
    normed_low = normed.astype(jnp.bfloat16)
    lowered = (in_weight.astype(jnp.bfloat16), out_weight.astype(jnp.bfloat16))
    whole_in, whole_out = (
        lax.all_gather(lowered[0], ("dp", "fsdp"), axis=0, tiled=True),
        lax.all_gather(lowered[1], ("dp", "fsdp"), axis=0, tiled=True),
    )
    projected = lax.switch(
        width_index,
        [partial(project_in, heads_on=head_number) for head_number in head_counts],
        normed_low,
        whole_in,
    )
    gate_part = projected[:, :INNER]
    mixed_part = projected[:, INNER : INNER + XBC]
    step_raw = projected[:, INNER + XBC :]
    rim_rows = passed_along(mixed_part[length - (CONV - 1) :], "fsdp", 1)
    prepared, prepare_pull = jax.vjp(
        partial(prepare, head_mask=head_mask), mixed_part, rim_rows, step_raw, vectors
    )
    values, step_sizes, key_rows, query_rows, decay_rates = prepared
    scanned, scan_pull = jax.vjp(local_scan, values, step_sizes, key_rows, query_rows, decay_rates)
    partial_out, device_decay, device_state, log_sums = scanned
    identity = (jnp.ones((HEADS,), jnp.float32), jnp.zeros((HEADS, HEAD_DIM, STATE), jnp.float32))
    entering = carried_in((device_decay, device_state), "fsdp", join_forward, identity)[1]
    gated_out, finish_pull = jax.vjp(
        partial(finish, head_mask=head_mask, channel_count=channel_count),
        partial_out,
        log_sums,
        query_rows,
        entering,
        values,
        gate_part,
        vectors,
    )
    gated_low = gated_out.astype(jnp.bfloat16)
    added = lax.switch(
        width_index,
        [partial(project_out, heads_on=head_number) for head_number in head_counts],
        gated_low,
        whole_out,
    )
    layer_out = (inputs + added).astype(jnp.bfloat16)
    back_in, back_out = (
        lax.all_gather(lowered[0], ("dp", "fsdp"), axis=0, tiled=True),
        lax.all_gather(lowered[1], ("dp", "fsdp"), axis=0, tiled=True),
    )
    gated_grad = lax.switch(
        width_index,
        [partial(project_out_back, heads_on=head_number) for head_number in head_counts],
        cotangent,
        back_out,
    )
    partial_grad, log_grad, query_grad, local_state, value_grad, gate_grad, vector_part_a = (
        finish_pull(gated_grad)
    )
    leaving = carried_in_2((device_decay, local_state), "fsdp", join_backward, identity)[1]
    decay_grad = jnp.sum(leaving * entering, axis=(1, 2))
    value_more, size_grad, key_grad, query_more, rate_grad = scan_pull(
        (partial_grad, decay_grad, leaving, log_grad)
    )
    mixed_grad, rim_grad, raw_grad, vector_part_b = prepare_pull(
        (value_grad + value_more, size_grad, key_grad, query_grad + query_more, rate_grad)
    )
    rim_back = jax.tree.map(
        lambda part, own: part.astype(own.dtype),
        passed_along(shortened(rim_grad), "fsdp", -1),
        rim_grad,
    )
    mixed_grad = jnp.concatenate(
        [mixed_grad[: length - (CONV - 1)], mixed_grad[length - (CONV - 1) :] + rim_back], axis=0
    )
    projected_grad = (
        jnp.concatenate([gate_grad, mixed_grad, raw_grad], axis=1) * column_mask[None, :]
    ).astype(jnp.bfloat16)
    normed_grad = lax.switch(
        width_index,
        [partial(project_in_back, heads_on=head_number) for head_number in head_counts],
        projected_grad,
        back_in,
    )
    input_grad, vector_part_c = norm_pull(normed_grad)
    token_grad = (cotangent.astype(jnp.float32) + input_grad).astype(jnp.bfloat16)
    rows_in = in_weight.shape[0]
    rows_out = out_weight.shape[0]
    in_raw = lax.psum_scatter(
        row_term(normed_low, projected_grad, rows_in * lax.axis_size(("dp", "fsdp"))),
        ("dp", "fsdp"),
        scatter_dimension=0,
        tiled=True,
    )
    out_raw = lax.psum_scatter(
        row_term(gated_low, cotangent, rows_out * lax.axis_size(("dp", "fsdp"))),
        ("dp", "fsdp"),
        scatter_dimension=0,
        tiled=True,
    )
    vector_term = vector_part_a + vector_part_b + vector_part_c
    shard_squares = jnp.sum(in_raw * in_raw) + jnp.sum(out_raw * out_raw)
    vector_raw = lax.psum(vector_term, ("dp", "fsdp"))
    squares = lax.psum(shard_squares, ("dp", "fsdp"))
    grad_norm = jnp.sqrt(squares + jnp.sum(vector_raw * vector_raw))
    factor = jnp.minimum(1.0, clip_norm / (grad_norm + 1e-06))
    in_grad = in_raw * factor
    out_grad = out_raw * factor
    vector_grad = vector_raw * factor
    in_moment, in_square, in_master = adamw(in_weight, in_first, in_second, in_grad, rate_in_proj)
    out_moment, out_square, out_master = adamw(
        out_weight, out_first, out_second, out_grad, rate_out_proj
    )
    vector_moment, vector_square, vector_master = adamw(
        vectors, vector_first, vector_second, vector_grad, rate_vectors
    )
    return (
        layer_out,
        token_grad,
        in_grad,
        out_grad,
        vector_grad,
        grad_norm,
        in_moment,
        in_square,
        in_master,
        in_master.astype(jnp.bfloat16),
        out_moment,
        out_square,
        out_master,
        out_master.astype(jnp.bfloat16),
        vector_moment,
        vector_square,
        vector_master,
    )


def solution(mesh):
    return jax.shard_map(
        on_device,
        mesh=mesh,
        in_specs=(
            P(("dp", "fsdp"), None),
            P("dp"),
            P(("dp", "fsdp"), None),
            P(("dp", "fsdp"), None),
            P(("dp", "fsdp"), None),
            P(("dp", "fsdp"), None),
            P(("dp", "fsdp"), None),
            P(("dp", "fsdp"), None),
            P(("dp", "fsdp"), None),
            P(),
            P(),
            P(),
        ),
        out_specs=(
            P(("dp", "fsdp"), None),
            P(("dp", "fsdp"), None),
            P(("dp", "fsdp"), None),
            P(("dp", "fsdp"), None),
            P(),
            P(),
            P(("dp", "fsdp"), None),
            P(("dp", "fsdp"), None),
            P(("dp", "fsdp"), None),
            P(("dp", "fsdp"), None),
            P(("dp", "fsdp"), None),
            P(("dp", "fsdp"), None),
            P(("dp", "fsdp"), None),
            P(("dp", "fsdp"), None),
            P(),
            P(),
            P(),
        ),
        check_vma=False,
    )
```

profile of v0, /device:TPU:0, one launch (start us, length us, event | category | flops | bytes accessed | tf_op | source)
XLA Modules:
  0.0 1796.5 jit_solution(16947382660750988759)
XLA Ops:
  14.6 201.9 %all-gather.9.cloned.1.call-done = bf16[2048,8512]{1,0:T(8,128)(2,1)} async-done(((bf16[64,8512]{1,0:T(8,128)(2,1)}), bf16[2048,8512]{1,0:T(8,128)(2,1)}) %all-gather.9.cloned.1.call-update) | async-done | bytes 34865168 | tf_op jit(solution)/shard_map/all_gather | solution.py:318
  216.6 19.4 %conditional.4 = (f32[256,8512]{1,0:T(8,128)}) conditional(s32[]{:T(128)} %bitcast.5, (bf16[2048,8512]{1,0:T(8,128)(2,1)}, bf16[256,2048]{1,0:T(8,128)(2,1)}) %tuple.97, (bf16[2048,8512]{1,0:T(8,128)(2,1)}, bf16[256,2048]{1,0:T(8,128)(2,1)}) %tuple.97, (bf16[2048,8512]{1,0:T(8,128)(2,1)}, ...), branch_computations={%region_1.0_spmd, %region_2.0_spmd, %region_3.0_spmd, %region_4.0_... | conditional | flops 8925478912 | bytes 108003360 | solution.py:321
  217.1 18.7 %fusion.236 = f32[256,8512]{1,0:T(8,128)} fusion(bf16[256,2048]{1,0:T(8,128)(2,1)} %get-tuple-element.425, bf16[2048,8512]{1,0:T(8,128)(2,1)} %get-tuple-element.426), kind=kOutput, calls=%fused_computation.318 | convolution fusion | flops 8925478912 | bytes 44630016 | tf_op jit(solution)/shard_map/cond/branch_3_fun/dot_general | solution.py:161
  246.3 9.7 fusion.107
  266.4 7.2 fusion.152
  275.2 58.6 %all-gather.11.cloned.1.call-done = bf16[4096,2048]{1,0:T(8,128)(2,1)} async-done(((bf16[128,2048]{1,0:T(8,128)(2,1)}), bf16[4096,2048]{1,0:T(8,128)(2,1)}) %all-gather.11.cloned.1.call-update) | async-done | bytes 16777232 | tf_op jit(solution)/shard_map/all_gather | solution.py:319
  333.8 10.4 conditional.6
  333.8 10.2 fusion.238
  351.2 5.9 fusion.170
  357.2 35.3 %all-gather.13.cloned.1.call-done = f32[256,64,128]{2,1,0:T(8,128)} async-done(((f32[64,64,128]{2,1,0:T(8,128)}), f32[256,64,128]{2,1,0:T(8,128)}) %all-gather.13.cloned.1.call-update) | async-done | bytes 8388624 | tf_op jit(solution)/shard_map/all_gather | solution.py:39
  397.4 23.3 %fusion.111 = f32[256,64,64]{0,2,1:T(8,128)} fusion(f32[256,64,64]{0,2,1:T(8,128)S(1)} %fusion.184, f32[256,64,64]{0,2,1:T(8,128)} %fusion.170, f32[256,4096]{0,1:T(8,128)S(1)} %copy-done.6, f32[256,256]{1,0:T(8,128)S(1)} %copy-done.35, f32[256,256]{1,0:T(8,128)S(1)} %copy-done.33, f32[64,256]{1,0:T(8,128)S(1)} %get-tuple-element.617, ...), kind=kOutput, calls=%fused_computation.132 | convolution fusion | flops 3247439872 | bytes 21758464 | tf_op jit(solution)/shard_map/jvp()/while/body/eval_jaxpr/hij,jhp->ihp/dot_general | solution.py:117
  433.5 8.8 multiply_reduce_fusion.6
  448.0 6.6 fusion.155
  454.7 16.0 fusion.241
  471.1 9.8 all-gather.3
  480.9 8.7 fusion.161
  489.6 6.7 fusion.158
  496.3 26.7 %fusion.89 = (f32[64,256]{1,0:T(8,128)}, f32[64,256]{1,0:T(8,128)}, f32[256,256]{1,0:T(8,128)S(1)}) fusion(f32[256,256]{1,0:T(8,128)S(1)} %copy-done.36, f32[256,256]{1,0:T(8,128)S(1)} %copy-done.34, f32[64,256]{1,0:T(8,128)S(1)} %get-tuple-element.617, pred[256,256]{1,0:T(8,128)(4,1)S(1)} %copy-done.54, f32[64,64,256]{2,1,0:T(8,128)S(1)} %bitcast.177, ...), kind=kOutput, calls=%fused_computation.94 | convolution fusion | flops 3269361664 | bytes 9502976 | tf_op jit(solution)/shard_map/transpose(jvp())/while/body/eval_jaxpr/hij,jhp->ihp/dot_general | solution.py:117
  526.4 13.9 while.19
  547.9 18.1 %multiply_reduce_fusion.8 = (f32[256,64]{0,1:T(8,128)S(1)}, f32[256,64]{0,1:T(8,128)}, f32[256,64,64]{0,2,1:T(8,128)}) fusion(f32[256,64,64]{0,2,1:T(8,128)S(1)} %fusion.180, f32[256,64]{0,1:T(8,128)S(1)} %copy.131, f32[64]{0:T(128)S(1)} %compare_convert_fusion, f32[256,4096]{0,1:T(8,128)} %copy.130, f32[64,64,256]{2,1,0:T(8,128)S(1)} %bitcast.178, ...), kind=kOutput, calls=%fused_computation.136 | convolution fusion | flops 3247407104 | bytes 17694976 | tf_op jit(solution)/shard_map/transpose(jvp())/while/body/eval_jaxpr/hij,jhp->ihp/dot_general | solution.py:117
  578.3 9.5 fusion.164
  593.8 7.0 multiply_reduce_fusion.3
  606.0 6.4 pad_add_fusion
  622.2 28.2 %fusion.240 = f32[2048,8512]{1,0:T(8,128)} fusion(bf16[256,2048]{1,0:T(8,128)(2,1)} %fusion.131, bf16[256,8512]{1,0:T(8,128)(2,1)} %fusion.90), kind=kOutput, calls=%fused_computation.322 | convolution fusion | flops 8925478912 | bytes 75137024 | tf_op jit(solution)/shard_map/dot_general | solution.py:201
  652.0 10.0 conditional.5
  652.4 9.6 fusion.237
  663.5 16.8 conditional.7
  663.6 16.5 fusion.239
  687.9 164.1 %reduce-scatter.5.cloned.1.call-done = f32[128,2048]{1,0:T(8,128)} async-done(((f32[4096,2048]{1,0:T(8,128)}), f32[128,2048]{1,0:T(8,128)}) %reduce-scatter.5.cloned.1.call-update) | async-done | bytes 1048592 | tf_op jit(solution)/shard_map/reduce_scatter | solution.py:405
  854.2 742.3 %reduce-scatter.3.cloned.1.call-done = f32[64,8512]{1,0:T(8,128)} async-done(((f32[2048,8512]{1,0:T(8,128)}), f32[64,8512]{1,0:T(8,128)}) %reduce-scatter.3.cloned.1.call-update) | async-done | bytes 2179088 | tf_op jit(solution)/shard_map/reduce_scatter | solution.py:399
  1600.6 131.7 %all-reduce.26.cloned.1.call-done = f32[28096]{0:T(1024)} async-done(((f32[28096]{0:T(1024)}), f32[28096]{0:T(1024)}) %all-reduce.26.cloned.1.call-update) | async-done | bytes 112400 | tf_op jit(solution)/shard_map/psum | solution.py:413
  1733.9 40.9 %psum.14 = f32[]{:T(128)} all-reduce(f32[]{:T(128)S(6)} %add.284), channel_id=1, replica_groups=mesh['dp'=8,'fsdp'=4] {'dp','fsdp'}, use_global_device_ids=true, to_apply=%region_44.45 | all-reduce | flops 1 | bytes 8 | tf_op jit(solution)/shard_map/psum | solution.py:414
  (272 shorter events, 146.6 us)
Async XLA Ops:
  7.2 209.3 %all-gather.9.cloned.1.call-start = ((), (), s32[]{:S(2)}) async-start(), calls=%async_computation.2 | async-start | bytes 36225024 | tf_op jit(solution)/shard_map/all_gather | solution.py:318
  10.2 323.6 %all-gather.11.cloned.1.call-start = ((), (), s32[]{:S(2)}) async-start(), calls=%async_computation.3 | async-start | bytes 17301504 | tf_op jit(solution)/shard_map/all_gather | solution.py:319
  11.1 381.4 %all-gather.13.cloned.1.call-start = ((), (), s32[]{:S(2)}) async-start(), calls=%async_computation.7 | async-start | bytes 10485760 | tf_op jit(solution)/shard_map/all_gather | solution.py:39
  11.8 204.7 %copy-start.46 = (f32[2048]{0:T(1024)}, f32[2048]{0:T(1024)S(1)}, u32[]{:S(2)}) copy-start(f32[2048]{0:T(1024)S(1)} %slice.257) | copy-start | bytes 24580
  12.1 204.4 %copy-start.61 = (f32[256]{0:T(256)}, f32[256]{0:T(256)S(1)}, u32[]{:S(2)}) copy-start(f32[256]{0:T(256)S(1)} %fusion.135) | copy-start | bytes 3076
  12.2 204.4 %copy-start.60 = (f32[256]{0:T(256)}, f32[256]{0:T(256)S(1)}, u32[]{:S(2)}) copy-start(f32[256]{0:T(256)S(1)} %fusion.205) | copy-start | bytes 3076
  12.7 226.3 %copy-start.64 = (f32[64]{0:T(128)}, f32[64]{0:T(128)S(1)}, u32[]{:S(2)}) copy-start(f32[64]{0:T(128)S(1)} %get-tuple-element.604) | copy-start | bytes 772
  12.7 226.3 %copy-start.66 = (f32[64]{0:T(128)}, f32[64]{0:T(128)S(1)}, u32[]{:S(2)}) copy-start(f32[64]{0:T(128)S(1)} %get-tuple-element.605) | copy-start | bytes 772
  236.8 9.4 collective-permute-start
  266.4 67.4 %copy-start.21 = (bf16[256,2048]{1,0:T(8,128)(2,1)S(1)}, bf16[256,2048]{1,0:T(8,128)(2,1)}, u32[]{:S(2)}) copy-start(bf16[256,2048]{1,0:T(8,128)(2,1)} %param.34) | copy-start | bytes 3145732
  273.5 252.8 %all-gather.15.cloned.1.call-start = ((), (), s32[]{:S(2)}) async-start(), calls=%async_computation.8 | async-start | bytes 5242880 | tf_op jit(solution)/shard_map/all_gather | solution.py:53
  397.3 23.4 %copy-start.10 = (f32[256,64,64]{0,2,1:T(8,128)}, f32[256,64,64]{0,2,1:T(8,128)S(1)}, u32[]{:S(2)}) copy-start(f32[256,64,64]{0,2,1:T(8,128)S(1)} %fusion.184) | copy-start | bytes 12582916
  454.7 397.4 %reduce-scatter.5.cloned.1.call-start = ((), (), s32[]{:S(2)}) async-start(), calls=%async_computation.5 | async-start | bytes 34603008 | tf_op jit(solution)/shard_map/reduce_scatter | solution.py:405
  470.7 1125.8 %reduce-scatter.3.cloned.1.call-start = ((), (), s32[]{:S(2)}) async-start(), calls=%async_computation.4 | async-start | bytes 72450048 | tf_op jit(solution)/shard_map/reduce_scatter | solution.py:399
  470.9 18.6 %copy-start.1 = (f32[256,4096]{0,1:T(8,128)S(1)}, f32[256,4096]{0,1:T(8,128)}, u32[]{:S(2)}) copy-start(f32[256,4096]{0,1:T(8,128)} %copy.136) | copy-start | bytes 12582916
  496.3 28.0 %copy-start.8 = (f32[256,64,64]{0,2,1:T(8,128)S(1)}, f32[256,64,64]{0,2,1:T(8,128)}, u32[]{:S(2)}) copy-start(f32[256,64,64]{0,2,1:T(8,128)} %fusion.170) | copy-start | bytes 12582916
  496.3 28.0 %copy-start.11 = (f32[256,64,64]{0,2,1:T(8,128)S(1)}, f32[256,64,64]{0,2,1:T(8,128)}, u32[]{:S(2)}) copy-start(f32[256,64,64]{0,2,1:T(8,128)} %copy-done.10) | copy-start | bytes 12582916
  566.0 12.2 copy-start.55
  566.0 12.3 copy-start
  578.3 15.4 slice-start
  578.3 15.4 slice-start.2
  612.5 3.2 collective-permute-start.1
  650.4 1081.9 %all-reduce.26.cloned.1.call-start = ((), (), s32[]{:S(2)}) async-start(), calls=%async_computation.6 | async-start | bytes 229376 | tf_op jit(solution)/shard_map/psum | solution.py:413
  652.0 10.9 copy-start.30
  663.5 16.9 copy-start.13
  663.5 16.9 copy-start.47
  663.5 18.8 %copy-start.50 = (f32[4352]{0:T(1024)S(1)}, f32[4352]{0:T(1024)}, u32[]{:S(2)}) copy-start(f32[4352]{0:T(1024)} %get-tuple-element.511) | copy-start | bytes 52228
  683.7 1092.4 %copy-start.48 = (f32[28096]{0:T(1024)S(1)}, f32[28096]{0:T(1024)}, u32[]{:S(2)}) copy-start(f32[28096]{0:T(1024)} %param.43) | copy-start | bytes 337156
  683.7 1092.4 %copy-start.49 = (f32[28096]{0:T(1024)S(1)}, f32[28096]{0:T(1024)}, u32[]{:S(2)}) copy-start(f32[28096]{0:T(1024)} %param.42) | copy-start | bytes 337156
  687.9 1090.0 %copy-start.19 = (f32[128,2048]{1,0:T(8,128)S(1)}, f32[128,2048]{1,0:T(8,128)}, u32[]{:S(2)}) copy-start(f32[128,2048]{1,0:T(8,128)} %param.38) | copy-start | bytes 3145732
  687.9 1090.0 %copy-start.28 = (f32[128,2048]{1,0:T(8,128)S(1)}, f32[128,2048]{1,0:T(8,128)}, u32[]{:S(2)}) copy-start(f32[128,2048]{1,0:T(8,128)} %param.40) | copy-start | bytes 3145732
  852.0 925.8 %copy-start.20 = (f32[128,2048]{1,0:T(8,128)S(1)}, f32[128,2048]{1,0:T(8,128)}, u32[]{:S(2)}) copy-start(f32[128,2048]{1,0:T(8,128)} %reduce-scatter.5.cloned.1.call-done) | copy-start | bytes 3145732
  (49 other events, 264.9 us)
Sparse Core Ops, SparseCore 0:
  11.5 205.0 all-gather.8
  220.0 113.7 all-gather.10
  335.9 56.4 all-gather.12
  454.8 40.3 all-gather.14
  497.4 354.6 reduce-scatter.4
  854.3 742.2 reduce-scatter.2
  1603.6 128.6 all-reduce.25
where the time goes:
time: 1800 us
  waiting for transfers between devices  1330 us (74%)
  matrix products  226 us (13%)
  other arithmetic  113 us (6%)
  blocking collectives  55.7 us (3%)
  local copies, waits for them, and re-layouts  42.3 us (2%)
  between operations  20 us (1%)
    reduce_scatter x1, waiting for transfers between devices, on_device(): lax.psum_scatter(row_term(normed_low, projected_grad, rows_in * lax.axis_...  742 us
    all_gather x1, waiting for transfers between devices, on_device(): lax.all_gather(lowered[0], ('dp', 'fsdp'), axis=0, tiled=True)  202 us
    reduce_scatter x1, waiting for transfers between devices, on_device(): lax.psum_scatter(row_term(gated_low, cotangent, rows_out * lax.axis_size(...  164 us
    psum x1, waiting for transfers between devices, on_device(): vector_raw = lax.psum(vector_term, ('dp', 'fsdp'))  132 us
    dot_general x3, matrix products, span_apply(): within = jnp.einsum('hij,jhp->ihp', mixing, weighted, precision=highest)  68.1 us
    all_gather x1, waiting for transfers between devices, on_device(): lax.all_gather(lowered[1], ('dp', 'fsdp'), axis=0, tiled=True)  58.6 us
    dot_general x2, matrix products, row_term(): lax.dot_general(piece, right, (((0,), (0,)), ((), ())), preferred_element...  44.2 us
    psum x1, blocking collectives, on_device(): squares = lax.psum(shard_squares, ('dp', 'fsdp'))  40.9 us
  transfers between devices with their start and end apart: 9, of which 6 were waited for; matrix products, arithmetic and copies ran while one was open for 17% of the time, Pallas kernels for 0%

commit v1 on v0

v1 whole, which is shorter than its diff:
```python
from functools import partial

import jax
import jax.numpy as jnp
from jax import lax
from jax.experimental import pallas as pl
from jax.experimental.pallas import tpu as pltpu
from jax.sharding import PartitionSpec as P

D = 2048
HEADS = 64
HEAD_DIM = 64
STATE = 128
CONV = 4
SPAN = 128
STEP = 10
INNER = 4096
XBC = 4352
PAIR = 2 * HEAD_DIM
GROUP = 4
LANES = GROUP * HEAD_DIM
ROW_TILE = 256
RING_LIMIT = 16

norm_eps = 1e-05
clip_norm = 1.0
beta_first = 0.5
beta_second = 0.5
adam_eps = 1e-08
weight_decay = 0.1
rate_in_proj = 0.03
rate_out_proj = 0.02
rate_vectors = 0.5
highest = lax.Precision.HIGHEST
f32 = jnp.float32
bf16 = jnp.bfloat16
VMEM_BYTES = 56 * 1024 * 1024


def ring_order(count):
    return list(range(0, count, 2)) + list(range(count - 1, 0, -2))


def ring_links(count):
    order = ring_order(count)
    right = [(order[i], order[(i + 1) % count]) for i in range(count)]
    return right, [(b, a) for a, b in right]


def ring_place(axis):
    count = lax.axis_size(axis)
    order = ring_order(count)
    places = [0] * count
    for place, member in enumerate(order):
        places[member] = place
    place = jnp.asarray(places, jnp.int32)[lax.axis_index(axis)]

    def member_at(distance):
        return jnp.asarray(order, jnp.int32)[lax.rem(place + distance + count, count)]

    return member_at


def uses_ring(axis):
    count = lax.axis_size(axis)
    return count % 2 == 0 and 4 <= count <= RING_LIMIT


def gather_rows(block, axis):
    count = lax.axis_size(axis)
    if not uses_ring(axis):
        return lax.all_gather(block, axis, axis=0, tiled=True)
    right, left = ring_links(count)
    member_at = ring_place(axis)
    rows, half = block.shape[0], block.shape[0] // 2
    whole = jnp.zeros((count * rows,) + block.shape[1:], block.dtype)
    columns = (0,) * (block.ndim - 1)

    def put(whole, piece, distance, shift=0):
        return lax.dynamic_update_slice(
            whole, piece, (member_at(distance) * rows + shift,) + columns
        )

    whole = put(whole, block, 0)
    going_right = going_left = block
    for hop in range(1, count // 2):
        going_right = lax.ppermute(going_right, axis, right)
        going_left = lax.ppermute(going_left, axis, left)
        whole = put(whole, going_right, -hop)
        whole = put(whole, going_left, hop)
    first = lax.ppermute(going_right[:half], axis, right)
    second = lax.ppermute(going_left[half:], axis, left)
    whole = put(whole, first, count // 2)
    return put(whole, second, count // 2, half)


def scatter_rows(terms, axis):
    count = lax.axis_size(axis)
    if not uses_ring(axis):
        return lax.psum_scatter(terms.astype(f32), axis, scatter_dimension=0, tiled=True)
    right, left = ring_links(count)
    member_at = ring_place(axis)
    rows = terms.shape[0] // count
    half = rows // 2

    def term(distance):
        return lax.dynamic_slice_in_dim(terms, member_at(distance) * rows, rows, 0).astype(f32)

    far = term(count // 2).astype(bf16)
    going_right = lax.ppermute(far[:half], axis, right)
    going_left = lax.ppermute(far[half:], axis, left)
    for distance in range(count // 2 - 1, 0, -1):
        to_right, to_left = term(distance), term(-distance)
        if distance == count // 2 - 1:
            to_right = jnp.concatenate([to_right[:half] + going_right, to_right[half:]])
            to_left = jnp.concatenate([to_left[:half], to_left[half:] + going_left])
        else:
            to_right, to_left = to_right + going_right, to_left + going_left
        going_right = lax.ppermute(to_right.astype(bf16), axis, right)
        going_left = lax.ppermute(to_left.astype(bf16), axis, left)
    return term(0) + going_right + going_left


def swapped(value, axis, flip):
    count = lax.axis_size(axis)
    return lax.ppermute(value, axis, [(i, i ^ flip) for i in range(count)])


def summed(value, axis):
    count = lax.axis_size(axis)
    if count <= 8:
        parts = [value] + [swapped(value, axis, flip) for flip in range(1, count)]
        while len(parts) > 1:
            parts = [parts[i] + parts[i + 1] for i in range(0, len(parts), 2)]
        return parts[0]
    return summed_in_steps(value, axis)


def summed_in_steps(value, axis):
    flip = 1
    while flip < lax.axis_size(axis):
        value = value + swapped(value, axis, flip)
        flip *= 2
    return value


def placed(parts, axis):
    count = lax.axis_size(axis)
    me = lax.axis_index(axis)
    whole = jnp.zeros((count,) + parts[0].shape, parts[0].dtype)
    for flip, part in enumerate(parts):
        whole = lax.dynamic_update_index_in_dim(whole, part, lax.bitwise_xor(me, flip), 0)
    return whole


def spread(value, axis):
    count = lax.axis_size(axis)
    parts = [value]
    flip = count // 2
    known = {0: value}
    while flip:
        fresh = {k ^ flip: swapped(v, axis, flip) for k, v in known.items()}
        known.update(fresh)
        flip //= 2
    parts = [known[k] for k in range(count)]
    return placed(parts, axis)


def spread_small(value, axis):
    count = lax.axis_size(axis)
    return placed([value] + [swapped(value, axis, k) for k in range(1, count)], axis)


def exchanged(blocks, axis):
    count = lax.axis_size(axis)
    me = lax.axis_index(axis)

    def block_for(flip):
        return lax.dynamic_index_in_dim(blocks, lax.bitwise_xor(me, flip), 0, False)

    return placed(
        [block_for(0)] + [swapped(block_for(k), axis, k) for k in range(1, count)], axis
    )


def halved(blocks, axis):
    count = lax.axis_size(axis)
    me = lax.axis_index(axis)
    held = {
        k: lax.dynamic_index_in_dim(blocks, lax.bitwise_xor(me, k), 0, False)
        for k in range(count)
    }
    flip = 1
    while flip < count:
        kept = {}
        for k in sorted(held):
            if k & flip:
                continue
            arrived = swapped(held[k ^ flip].astype(bf16), axis, flip)
            kept[k] = held[k].astype(f32) + arrived
        held = kept
        flip *= 2
    return held[0]


def dot_rows(a, b):
    return lax.dot_general(a, b, (((1,), (0,)), ((), ())), preferred_element_type=f32)


def dot_lanes(a, b):
    return lax.dot_general(a, b, (((1,), (1,)), ((), ())), preferred_element_type=f32)


def head_lanes(columns, base):
    rows = columns.shape[0]
    full = [
        jnp.broadcast_to(columns[:, base + j : base + j + 1], (rows, PAIR)) for j in range(GROUP)
    ]
    first = lax.broadcasted_iota(jnp.int32, (rows, PAIR), 1) < HEAD_DIM
    lanes = jnp.concatenate(
        [jnp.where(first, full[i], full[i + 1]) for i in range(0, GROUP, 2)], axis=1
    )
    return full, lanes


def stacked_heads(values, block_mask):
    return jnp.concatenate([values] * GROUP, axis=0) * block_mask


def filtered(window, taps, bias, rows):
    pre = bias + taps[CONV - 1 : CONV] * window[8 : 8 + rows]
    for k in range(CONV - 1):
        pre = pre + taps[k : k + 1] * window[5 + k : 5 + k + rows]
    return pre


def scan_forward_kernel(
    x_ref, taps_ref, bias_ref, mask_ref, skip_ref, column_ref, row_ref, key_ref, query_ref,
    key_t_ref, block_ref, y_ref, states_ref, padded, state,
):
    length = x_ref.shape[0]
    rows = SPAN
    mask = mask_ref[...]
    padded[0:8, :] = jnp.zeros((8, LANES), f32)
    padded[8 : 8 + length, :] = x_ref[...] * mask
    state[...] = jnp.zeros_like(state)
    taps, bias, skip = taps_ref[...], bias_ref[...], skip_ref[...]
    causal = lax.broadcasted_iota(jnp.int32, (rows, rows), 0) >= lax.broadcasted_iota(
        jnp.int32, (rows, rows), 1
    )

    def chunk(c, carry):
        start = pl.multiple_of(c * rows, rows)
        here = pl.ds(start, rows)
        pre = filtered(padded[pl.ds(start, rows + 8), :], taps, bias, rows)
        values = pre * jax.nn.sigmoid(pre) * mask
        columns = column_ref[here, :]
        log_full, log_lanes = head_lanes(columns, 0)
        step_lanes = head_lanes(columns, GROUP)[1]
        weighted = step_lanes * values
        weighted_low = weighted.astype(bf16)
        keys, queries, keys_t = key_ref[here, :], query_ref[here, :], key_t_ref[:, here]
        inner = dot_lanes(queries, keys)
        mixing = jnp.concatenate(
            [
                (
                    jnp.where(causal, jnp.exp(log_full[j] - row_ref[j : j + 1, here]), 0.0)
                    * inner
                ).astype(bf16)
                for j in range(GROUP)
            ],
            axis=1,
        )
        state_now = state[...]
        state_low = state_now.astype(bf16)
        states_ref[pl.ds(c, 1)] = state_low[None]
        y = dot_rows(mixing, stacked_heads(weighted_low, block_ref[...]))
        y = y + jnp.exp(log_lanes) * dot_rows(queries, state_low)
        y_ref[here, :] = y + skip * values
        log_last = log_lanes[rows - 1 : rows, :]
        tail = (weighted * jnp.exp(log_last - log_lanes)).astype(bf16)
        state[...] = jnp.exp(log_last) * state_now + dot_rows(keys_t, tail)
        return carry

    lax.fori_loop(0, length // rows, chunk, 0)


def scan_backward_kernel(
    x_ref, taps_ref, bias_ref, mask_ref, skip_ref, column_ref, row_ref, key_ref, query_ref,
    query_t_ref, block_ref, pick_ref, grad_ref, states_ref,
    x_grad_ref, key_grad_ref, query_grad_ref, sums_ref, rest_ref, channel_ref,
    padded, following, state_back, inner_grad,
):
    length = x_ref.shape[0]
    rows = SPAN
    chunks = length // rows
    group = pl.program_id(0)
    mask = mask_ref[...]
    padded[0:8, :] = jnp.zeros((8, LANES), f32)
    padded[8 : 8 + length, :] = x_ref[...] * mask
    following[...] = jnp.zeros_like(following)
    state_back[...] = jnp.zeros_like(state_back)
    channel_ref[...] = jnp.zeros_like(channel_ref)

    @pl.when(group == 0)
    def _():
        key_grad_ref[...] = jnp.zeros_like(key_grad_ref)
        query_grad_ref[...] = jnp.zeros_like(query_grad_ref)
        inner_grad[...] = jnp.zeros_like(inner_grad)

    taps, bias, skip = taps_ref[...], bias_ref[...], skip_ref[...]
    row_at = lax.broadcasted_iota(jnp.int32, (rows, rows), 0)
    lane_at = lax.broadcasted_iota(jnp.int32, (rows, rows), 1)
    causal, causal_t = row_at >= lane_at, lane_at >= row_at

    def chunk(lap, carry):
        c = chunks - 1 - lap
        start = pl.multiple_of(c * rows, rows)
        here = pl.ds(start, rows)
        window = padded[pl.ds(start, rows + 8), :]
        pre = filtered(window, taps, bias, rows)
        gate = jax.nn.sigmoid(pre)
        values = pre * gate * mask
        columns = column_ref[here, :]
        log_full, log_lanes = head_lanes(columns, 0)
        step_lanes = head_lanes(columns, GROUP)[1]
        weighted = step_lanes * values
        weighted_low = weighted.astype(bf16)
        keys, queries, queries_t = key_ref[here, :], query_ref[here, :], query_t_ref[:, here]
        grad_low = grad_ref[here, :]
        grad = grad_low.astype(f32)
        inner, inner_t = dot_lanes(queries, keys), dot_lanes(keys, queries)
        blocks = block_ref[...]
        weighted_blocks = stacked_heads(weighted_low, blocks)
        grad_blocks = stacked_heads(grad_low, blocks)
        mixing_grad = dot_lanes(grad_low, weighted_blocks)
        mixing, mixing_t, inner_sum = [], [], jnp.zeros((rows, rows), f32)
        for j in range(GROUP):
            log_row = row_ref[j : j + 1, here]
            decay = jnp.where(causal, jnp.exp(log_full[j] - log_row), 0.0)
            decay_t = jnp.where(causal_t, jnp.exp(log_row - log_full[j]), 0.0)
            mixing.append((decay * inner).astype(bf16))
            mixing_t.append((decay_t * inner_t).astype(bf16))
            inner_sum = inner_sum + decay * mixing_grad[:, j * rows : (j + 1) * rows]
        inner_grad[pl.ds(c, 1)] = inner_grad[pl.ds(c, 1)] + inner_sum[None]
        y = dot_rows(jnp.concatenate(mixing, axis=1), weighted_blocks)
        state_low = states_ref[pl.ds(c, 1)][0]
        entry = jnp.exp(log_lanes)
        y = y + entry * dot_rows(queries, state_low)
        inside = dot_rows(jnp.concatenate(mixing_t, axis=1), grad_blocks)
        back = state_back[...]
        back_low = back.astype(bf16)
        log_last = log_lanes[rows - 1 : rows, :]
        tail = jnp.exp(log_last - log_lanes)
        outside = tail * dot_rows(keys, back_low)
        entry_grad = (grad * entry).astype(bf16)
        tail_low = (weighted * tail).astype(bf16)
        query_grad_ref[here, :] = query_grad_ref[here, :] + dot_lanes(entry_grad, state_low)
        key_grad_ref[here, :] = key_grad_ref[here, :] + dot_lanes(tail_low, back_low)
        last = jnp.exp(log_last)
        rest_ref[pl.ds(c, 1)] = (
            last * jnp.sum(state_low.astype(f32) * back, axis=0, keepdims=True)
        )[None]
        state_back[...] = last * back + dot_rows(queries_t, entry_grad)
        weighted_grad = inside + outside
        first = grad * y - weighted_low.astype(f32) * inside
        first_high = first.astype(bf16)
        first_rest = (first - first_high.astype(f32)).astype(bf16)
        sums_ref[here, :] = (
            dot_rows(first_high, pick_ref[0])
            + dot_rows(first_rest, pick_ref[0])
            + dot_rows((weighted * outside).astype(bf16), pick_ref[1])
            + dot_rows((values * weighted_grad).astype(bf16), pick_ref[2])
        )
        values_grad = step_lanes * weighted_grad + skip * grad
        pre_grad = values_grad * mask * (gate * (1.0 + pre * (1.0 - gate)))
        channel_ref[CONV : CONV + 1, :] += jnp.sum(pre_grad, axis=0, keepdims=True)
        channel_ref[CONV + 1 : CONV + 2, :] += jnp.sum(grad * values, axis=0, keepdims=True)
        for k in range(CONV):
            channel_ref[k : k + 1, :] += jnp.sum(
                pre_grad * window[5 + k : 5 + k + rows], axis=0, keepdims=True
            )
        ahead = jnp.concatenate([pre_grad, following[...]], axis=0)
        following[...] = pre_grad[0:8]
        x_grad = taps[CONV - 1 : CONV] * ahead[0:rows]
        for k in range(CONV - 1):
            x_grad = x_grad + taps[k : k + 1] * ahead[CONV - 1 - k : CONV - 1 - k + rows]
        x_grad_ref[here, :] = (x_grad * mask).astype(bf16)
        return carry

    lax.fori_loop(0, chunks, chunk, 0)

    @pl.when(group == pl.num_programs(0) - 1)
    def _():
        def finish(c, carry):
            here = pl.ds(pl.multiple_of(c * rows, rows), rows)
            inner_low = inner_grad[pl.ds(c, 1)][0].astype(bf16)
            query_grad_ref[here, :] = query_grad_ref[here, :] + dot_rows(
                inner_low, key_ref[here, :]
            )
            key_grad_ref[here, :] = key_grad_ref[here, :] + lax.dot_general(
                inner_low, query_ref[here, :], (((0,), (0,)), ((), ())),
                preferred_element_type=f32,
            )
            return carry

        lax.fori_loop(0, chunks, finish, 0)


def block_mask():
    row = jnp.arange(GROUP * SPAN)[:, None] // SPAN
    lane = jnp.arange(LANES)[None, :] // HEAD_DIM
    return (row == lane).astype(bf16)


def pick_masks():
    lane = jnp.arange(LANES)[:, None] // HEAD_DIM
    target = jnp.arange(PAIR)[None, :]
    return jnp.stack([(target == lane + GROUP * kind).astype(bf16) for kind in range(3)])


def whole_spec():
    return pl.BlockSpec(memory_space=pltpu.VMEM)


def lane_spec(rows):
    return pl.BlockSpec((rows, LANES), lambda g: (0, g))


def head_specs(length):
    return [
        lane_spec(length),
        lane_spec(CONV),
        lane_spec(1),
        lane_spec(1),
        lane_spec(1),
        pl.BlockSpec((length, PAIR), lambda g: (0, g)),
        pl.BlockSpec((8, length), lambda g: (g, 0)),
        whole_spec(),
        whole_spec(),
        whole_spec(),
        whole_spec(),
    ]


def scan_forward(x, taps, bias, mask, skip, columns, rows, keys, queries, keys_t):
    length, width = x.shape
    chunks = length // SPAN
    return pl.pallas_call(
        scan_forward_kernel,
        grid=(width // LANES,),
        in_specs=head_specs(length),
        out_specs=[
            lane_spec(length),
            pl.BlockSpec((chunks, STATE, LANES), lambda g: (0, 0, g)),
        ],
        out_shape=[
            jax.ShapeDtypeStruct((length, width), f32),
            jax.ShapeDtypeStruct((chunks, STATE, width), bf16),
        ],
        scratch_shapes=[pltpu.VMEM((length + 8, LANES), f32), pltpu.VMEM((STATE, LANES), f32)],
        compiler_params=pltpu.CompilerParams(vmem_limit_bytes=VMEM_BYTES),
        cost_estimate=pl.CostEstimate(
            flops=10_000_000_000, bytes_accessed=12_000_000, transcendentals=4_000_000
        ),
        name="scan_forward",
    )(x, taps, bias, mask, skip, columns, rows, keys, queries, keys_t, block_mask())


def scan_backward(
    x, taps, bias, mask, skip, columns, rows, keys, queries, queries_t, grad, states
):
    length, width = x.shape
    chunks = length // SPAN
    groups = width // LANES
    same = lambda g: (0, 0)
    return pl.pallas_call(
        scan_backward_kernel,
        grid=(groups,),
        in_specs=head_specs(length)
        + [
            whole_spec(),
            lane_spec(length),
            pl.BlockSpec((chunks, STATE, LANES), lambda g: (0, 0, g)),
        ],
        out_specs=[
            lane_spec(length),
            pl.BlockSpec((length, STATE), same),
            pl.BlockSpec((length, STATE), same),
            pl.BlockSpec((length, PAIR), lambda g: (0, g)),
            pl.BlockSpec((chunks, 1, LANES), lambda g: (0, 0, g)),
            lane_spec(8),
        ],
        out_shape=[
            jax.ShapeDtypeStruct((length, width), bf16),
            jax.ShapeDtypeStruct((length, STATE), f32),
            jax.ShapeDtypeStruct((length, STATE), f32),
            jax.ShapeDtypeStruct((length, PAIR * groups), f32),
            jax.ShapeDtypeStruct((chunks, 1, width), f32),
            jax.ShapeDtypeStruct((8, width), f32),
        ],
        scratch_shapes=[
            pltpu.VMEM((length + 8, LANES), f32),
            pltpu.VMEM((8, LANES), f32),
            pltpu.VMEM((STATE, LANES), f32),
            pltpu.VMEM((chunks, SPAN, SPAN), f32),
        ],
        compiler_params=pltpu.CompilerParams(vmem_limit_bytes=VMEM_BYTES),
        cost_estimate=pl.CostEstimate(
            flops=30_000_000_000, bytes_accessed=16_000_000, transcendentals=8_000_000
        ),
        name="scan_backward",
    )(
        x, taps, bias, mask, skip, columns, rows, keys, queries, queries_t, block_mask(),
        pick_masks(), grad, states,
    )


def gate_kernel(
    normed_ref, weight_ref, cotangent_ref, out_ref, y_ref, gain_ref, mask_ref,
    gate_part_ref, gated_grad_ref, stats_ref,
):
    gate_part = dot_rows(normed_ref[...], weight_ref[...]) * mask_ref[...]
    gated_grad = dot_lanes(cotangent_ref[...], out_ref[...])
    gate_part_ref[...] = gate_part
    gated_grad_ref[...] = gated_grad
    gated = y_ref[...] * (gate_part * jax.nn.sigmoid(gate_part))
    squares = jnp.sum(gated * gated, axis=1, keepdims=True)
    products = jnp.sum(gated * gated_grad * gain_ref[...], axis=1, keepdims=True)
    lane = lax.broadcasted_iota(jnp.int32, stats_ref.shape, 1)
    stats_ref[...] = jnp.where(lane == 0, squares, products)


def gate_forward(normed, weight, cotangent, out_weight, y, gain, mask):
    length, width = y.shape
    rows = lambda lanes: pl.BlockSpec((ROW_TILE, lanes), lambda i: (i, 0))
    return pl.pallas_call(
        gate_kernel,
        grid=(length // ROW_TILE,),
        in_specs=[
            rows(D), whole_spec(), rows(D), whole_spec(), rows(width), whole_spec(), whole_spec(),
        ],
        out_specs=[rows(width), rows(width), rows(PAIR)],
        out_shape=[
            jax.ShapeDtypeStruct((length, width), f32),
            jax.ShapeDtypeStruct((length, width), f32),
            jax.ShapeDtypeStruct((length, PAIR), f32),
        ],
        compiler_params=pltpu.CompilerParams(vmem_limit_bytes=VMEM_BYTES),
        cost_estimate=pl.CostEstimate(
            flops=9_000_000_000, bytes_accessed=28_000_000, transcendentals=1_000_000
        ),
        name="gate_forward",
    )(normed, weight, cotangent, out_weight, y, gain, mask)


def norm_back_kernel(
    y_ref, gate_part_ref, gated_grad_ref, scale_ref, gain_ref, mask_ref,
    gated_ref, y_grad_ref, gate_grad_ref, gain_grad_ref,
):
    @pl.when(pl.program_id(0) == 0)
    def _():
        gain_grad_ref[...] = jnp.zeros_like(gain_grad_ref)

    y, gate_part, gated_grad = y_ref[...], gate_part_ref[...], gated_grad_ref[...]
    inverse, pull = scale_ref[:, 0:1], scale_ref[:, 1:2]
    gate = jax.nn.sigmoid(gate_part)
    silu = gate_part * gate
    gated = y * silu
    scaled = gated * inverse
    gain = gain_ref[...]
    gated_ref[...] = (scaled * gain).astype(bf16)
    gain_grad_ref[0:1, :] += jnp.sum(gated_grad * scaled, axis=0, keepdims=True)
    back = inverse * (gated_grad * gain) - gated * pull
    y_grad_ref[...] = (back * silu).astype(bf16)
    gate_grad_ref[...] = (
        back * y * (gate * (1.0 + gate_part * (1.0 - gate))) * mask_ref[...]
    ).astype(bf16)


def norm_back(y, gate_part, gated_grad, scales, gain, mask):
    length, width = y.shape
    rows = lambda lanes: pl.BlockSpec((ROW_TILE, lanes), lambda i: (i, 0))
    return pl.pallas_call(
        norm_back_kernel,
        grid=(length // ROW_TILE,),
        in_specs=[rows(width), rows(width), rows(width), rows(2), whole_spec(), whole_spec()],
        out_specs=[
            rows(width), rows(width), rows(width), pl.BlockSpec((8, width), lambda i: (0, 0)),
        ],
        out_shape=[
            jax.ShapeDtypeStruct((length, width), bf16),
            jax.ShapeDtypeStruct((length, width), bf16),
            jax.ShapeDtypeStruct((length, width), bf16),
            jax.ShapeDtypeStruct((8, width), f32),
        ],
        compiler_params=pltpu.CompilerParams(vmem_limit_bytes=VMEM_BYTES),
        cost_estimate=pl.CostEstimate(
            flops=30_000_000, bytes_accessed=18_000_000, transcendentals=1_000_000
        ),
        name="norm_back",
    )(y, gate_part, gated_grad, scales, gain, mask)


def unpack(vectors):
    offset = D + INNER
    taps_end = offset + CONV * XBC
    heads_start = taps_end + XBC
    norm_gain = vectors[:D]
    gate_gain = vectors[D:offset]
    filter_taps = vectors[offset:taps_end].reshape(CONV, XBC)
    filter_bias = vectors[taps_end:heads_start]
    step_bias = vectors[heads_start : heads_start + HEADS]
    decay_log = vectors[heads_start + HEADS : heads_start + 2 * HEADS]
    skip_gain = vectors[heads_start + 2 * HEADS : heads_start + 3 * HEADS]
    return (norm_gain, gate_gain, filter_taps, filter_bias, step_bias, decay_log, skip_gain)


def adamw(weight, moment, square, gradient, step_rate):
    moment_new = beta_first * moment + (1.0 - beta_first) * gradient
    square_new = beta_second * square + (1.0 - beta_second) * gradient * gradient
    moment_hat = moment_new / (1.0 - beta_first**STEP)
    square_hat = square_new / (1.0 - beta_second**STEP)
    weight_new = weight - step_rate * (
        moment_hat / (jnp.sqrt(square_hat) + adam_eps) + weight_decay * weight
    )
    return (moment_new, square_new, weight_new)


def on_device(
    tokens,
    widths,
    cotangent,
    in_weight,
    in_first,
    in_second,
    out_weight,
    out_first,
    out_second,
    vectors,
    vector_first,
    vector_second,
):
    fsdp = lax.axis_size("fsdp")
    me = lax.axis_index("fsdp")
    heads = HEADS // fsdp
    inner = INNER // fsdp
    shared = 2 * STATE // fsdp
    pairs = HEADS // 2 // fsdp
    rows_in, rows_out = in_weight.shape[0], out_weight.shape[0]
    length = tokens.shape[0] * fsdp
    chunks = length // SPAN
    out_aligned = rows_out == PAIR

    def own_channels(v):
        lead = v.shape[:-1]
        cut = v.reshape(lead + (pairs, fsdp, PAIR))
        return lax.dynamic_index_in_dim(cut, me, len(lead) + 1, False).reshape(lead + (inner,))

    def own_heads(v):
        return lax.dynamic_index_in_dim(v.reshape(pairs, fsdp, 2), me, 1, False).reshape(heads)

    def own_shared(v):
        return lax.dynamic_slice_in_dim(v, me * shared, shared, v.ndim - 1)

    norm_gain, gate_gain, filter_taps, filter_bias, step_bias, decay_log, skip_gain = unpack(
        vectors
    )
    gain_own = own_channels(gate_gain)[None]
    taps_own = own_channels(filter_taps[:, :INNER])
    bias_own = own_channels(filter_bias[:INNER])[None]
    taps_shared = own_shared(filter_taps[:, INNER:])
    bias_shared = own_shared(filter_bias[INNER:])
    step_bias_own, decay_own = own_heads(step_bias), -jnp.exp(own_heads(decay_log))
    skip_own = jnp.repeat(own_heads(skip_gain), HEAD_DIM)[None]

    width_index = widths[0]
    active = HEADS // 8 * jnp.left_shift(jnp.int32(1), width_index)
    head_mask = (jnp.arange(heads, dtype=jnp.int32) < active // fsdp).astype(f32)
    mask = jnp.repeat(head_mask, HEAD_DIM)[None]
    channel_count = (active * HEAD_DIM).astype(f32)

    in_low = in_weight.astype(bf16)
    shared_cut = jnp.concatenate(
        [
            in_low[:, 2 * INNER : 2 * INNER + 2 * STATE]
            .reshape(rows_in, fsdp, shared)
            .transpose(1, 0, 2),
            in_low[:, 2 * INNER + 2 * STATE :]
            .reshape(rows_in, pairs, fsdp, 2)
            .transpose(2, 0, 1, 3)
            .reshape(fsdp, rows_in, heads),
        ],
        axis=2,
    )

    def channel_cut(part):
        return (
            part.reshape(rows_in, pairs, fsdp, PAIR)
            .transpose(2, 0, 1, 3)
            .reshape(fsdp, rows_in, inner)
        )

    def gathered(cut):
        block = exchanged(cut, "fsdp")
        return gather_rows(block.reshape(fsdp * rows_in, cut.shape[2]), "dp")

    weight_shared = gathered(shared_cut)
    weight_x = gathered(channel_cut(in_low[:, INNER : 2 * INNER]))
    weight_gate = gathered(channel_cut(in_low[:, :INNER]))
    out_low = out_weight.astype(bf16)
    if out_aligned:
        weight_out = gather_rows(out_low, "dp")
    else:
        weight_out = lax.dynamic_index_in_dim(
            lax.all_gather(out_low, ("dp", "fsdp"), axis=0, tiled=True).reshape(
                pairs, fsdp, PAIR, D
            ),
            me,
            1,
            False,
        ).reshape(inner, D)

    inputs = tokens.astype(f32)
    inverse_in = lax.rsqrt(jnp.mean(inputs * inputs, axis=-1, keepdims=True) + norm_eps)
    normed_own = (inputs * inverse_in * norm_gain[None, :]).astype(bf16)
    normed = spread(normed_own, "fsdp").reshape(length, D)
    cotangents = spread(cotangent, "fsdp").reshape(length, D)

    small = lax.dot_general(
        weight_shared, normed, (((0,), (1,)), ((), ())), preferred_element_type=f32
    )
    shared_part = small[:shared]
    step_raw = small[shared:] * head_mask[:, None]
    shared_padded = jnp.pad(shared_part, ((0, 0), (CONV - 1, 0)))
    shared_pre = bias_shared[:, None] + sum(
        taps_shared[k][:, None] * shared_padded[:, k : k + length] for k in range(CONV)
    )
    shared_gate = jax.nn.sigmoid(shared_pre)
    shared_all = spread_small((shared_pre * shared_gate).astype(bf16), "fsdp").reshape(
        2 * STATE, length
    )
    keys_t, queries_t = shared_all[:STATE], shared_all[STATE:]
    keys, queries = keys_t.T, queries_t.T
    step_logits = step_raw + step_bias_own[:, None]
    step_sizes = jax.nn.softplus(step_logits)
    upto = (jnp.arange(SPAN)[:, None] <= jnp.arange(SPAN)[None, :]).astype(f32)
    log_sums = jnp.dot(
        (step_sizes * decay_own[:, None]).reshape(heads, chunks, SPAN), upto, precision=highest
    ).reshape(heads, length)
    groups = heads // GROUP
    head_rows = jnp.concatenate(
        [log_sums.reshape(groups, GROUP, length), step_sizes.reshape(groups, GROUP, length)],
        axis=1,
    )
    head_columns = jnp.pad(
        head_rows.transpose(2, 0, 1), ((0, 0), (0, 0), (0, PAIR - 2 * GROUP))
    ).reshape(length, groups * PAIR)
    head_rows = head_rows.reshape(groups * 2 * GROUP, length)

    x_part = jnp.dot(normed, weight_x, preferred_element_type=f32)
    y, states = scan_forward(
        x_part, taps_own, bias_own, mask, skip_own, head_columns, head_rows, keys, queries, keys_t
    )
    gate_part, gated_grad, stats = gate_forward(
        normed, weight_gate, cotangents, weight_out, y, gain_own, mask
    )
    stats = summed(stats[:, :2].T, "fsdp")
    inverse_out = lax.rsqrt(stats[0] / channel_count + norm_eps)
    pull = inverse_out**3 / channel_count * stats[1]
    gated_low, y_grad, gate_grad, gain_grad = norm_back(
        y, gate_part, gated_grad, jnp.stack([inverse_out, pull], axis=1), gain_own, mask
    )

    out_term = lax.dot_general(
        gated_low, cotangents, (((0,), (0,)), ((), ())), preferred_element_type=f32
    ).astype(bf16)
    if out_aligned:
        out_raw = scatter_rows(out_term, "dp")
    else:
        whole_term = jnp.zeros((pairs, fsdp, PAIR, D), f32)
        whole_term = lax.dynamic_update_slice(
            whole_term, out_term.astype(f32).reshape(pairs, 1, PAIR, D), (0, me, 0, 0)
        )
        out_raw = lax.psum_scatter(
            whole_term.reshape(INNER, D), ("dp", "fsdp"), scatter_dimension=0, tiled=True
        )
    added = halved(
        jnp.dot(gated_low, weight_out, preferred_element_type=f32)
        .astype(bf16)
        .reshape(fsdp, tokens.shape[0], D),
        "fsdp",
    )
    layer_out = (inputs + added).astype(bf16)

    def in_term(grad):
        return lax.dot_general(
            normed, grad, (((0,), (0,)), ((), ())), preferred_element_type=f32
        ).astype(bf16)

    gate_raw = scatter_rows(in_term(gate_grad), "dp")

    x_grad, key_grad, query_grad, sums, rest, channel_grad = scan_backward(
        x_part, taps_own, bias_own, mask, skip_own, head_columns, head_rows, keys, queries,
        queries_t, y_grad, states,
    )
    x_raw = scatter_rows(in_term(x_grad), "dp")

    shared_grads = jnp.concatenate([key_grad, query_grad], axis=1).T.astype(bf16)
    arrived = exchanged(shared_grads.reshape(fsdp, shared, length), "fsdp").astype(f32)
    activated_grad = jnp.sum(arrived, axis=0)
    shared_pre_grad = activated_grad * shared_gate * (1.0 + shared_pre * (1.0 - shared_gate))
    shared_ahead = jnp.pad(shared_pre_grad, ((0, 0), (0, CONV - 1)))
    shared_grad = sum(
        taps_shared[k][:, None] * shared_ahead[:, CONV - 1 - k : CONV - 1 - k + length]
        for k in range(CONV)
    )
    taps_shared_grad = jnp.stack(
        [
            jnp.sum(shared_pre_grad * shared_padded[:, k : k + length], axis=1)
            for k in range(CONV)
        ]
    )
    bias_shared_grad = jnp.sum(shared_pre_grad, axis=1)

    sums = (
        sums.reshape(length, groups, PAIR)[:, :, : 3 * GROUP]
        .reshape(length, groups, 3, GROUP)
        .transpose(2, 1, 3, 0)
        .reshape(3, heads, chunks, SPAN)
    )
    before = (jnp.arange(SPAN)[:, None] < jnp.arange(SPAN)[None, :]).astype(f32)
    rest = rest.reshape(chunks, heads, HEAD_DIM).sum(axis=2).T
    log_grad = (
        jnp.dot(sums[0], 1.0 - before, precision=highest)
        + jnp.dot(sums[1], before, precision=highest)
        + rest[:, :, None]
    ).reshape(heads, length)
    step_grad = decay_own[:, None] * log_grad + sums[2].reshape(heads, length)
    raw_grad = step_grad * jax.nn.sigmoid(step_logits)
    step_bias_grad = jnp.sum(raw_grad, axis=1)
    decay_grad = jnp.sum(step_sizes * log_grad, axis=1) * decay_own
    small_grad = jnp.concatenate([shared_grad, raw_grad * head_mask[:, None]], axis=0).astype(bf16)
    small_raw = scatter_rows(
        lax.dot_general(
            normed, small_grad, (((0,), (1,)), ((), ())), preferred_element_type=f32
        ).astype(bf16),
        "dp",
    )

    def in_back(grad, weight, grad_dim=1):
        return lax.dot_general(
            grad, weight, (((grad_dim,), (1,)), ((), ())), preferred_element_type=f32
        )

    normed_grad = halved(
        (
            in_back(gate_grad, weight_gate)
            + in_back(x_grad, weight_x)
            + in_back(small_grad, weight_shared, 0)
        )
        .astype(bf16)
        .reshape(fsdp, tokens.shape[0], D),
        "fsdp",
    )
    pulled = normed_grad * norm_gain[None, :]
    input_grad = inverse_in * pulled - inputs * (
        inverse_in**3 * jnp.mean(pulled * inputs, axis=-1, keepdims=True)
    )
    token_grad = (cotangent.astype(f32) + input_grad).astype(bf16)
    norm_gain_grad = jnp.sum(normed_grad * inputs * inverse_in, axis=0)

    skip_grad = channel_grad[CONV + 1].reshape(heads, HEAD_DIM).sum(axis=1)
    head_row = jnp.concatenate(
        [
            step_bias_grad, decay_grad, skip_grad, bias_shared_grad, taps_shared_grad.reshape(-1),
        ]
    )
    head_row = jnp.pad(head_row, (0, inner - head_row.shape[0]))
    vector_rows = jnp.concatenate(
        [
            gain_grad[0:1],
            channel_grad[: CONV + 1],
            head_row[None],
            norm_gain_grad.reshape(-1, inner),
        ]
    )
    vector_rows = spread_small(summed_in_steps(vector_rows, "dp"), "fsdp")

    def joined_channels(v):
        return v.reshape(fsdp, pairs, PAIR).transpose(1, 0, 2).reshape(INNER)

    def joined_heads(v):
        return v.reshape(fsdp, pairs, 2).transpose(1, 0, 2).reshape(HEADS)

    head_all = vector_rows[:, CONV + 2]
    taps_shared_all = (
        head_all[:, 3 * heads + shared : 3 * heads + 5 * shared]
        .reshape(fsdp, CONV, shared)
        .transpose(1, 0, 2)
        .reshape(CONV, 2 * STATE)
    )
    taps_all = [
        jnp.concatenate([joined_channels(vector_rows[:, 1 + k]), taps_shared_all[k]])
        for k in range(CONV)
    ]
    bias_all = jnp.concatenate(
        [
            joined_channels(vector_rows[:, CONV + 1]),
            head_all[:, 3 * heads : 3 * heads + shared].reshape(-1),
        ]
    )
    norm_rows = vector_rows[:, CONV + 3 :].reshape(fsdp, D)
    norm_all = norm_rows[0]
    for member in range(1, fsdp):
        norm_all = norm_all + norm_rows[member]
    vector_raw = jnp.concatenate(
        [norm_all, joined_channels(vector_rows[:, 0])]
        + taps_all
        + [bias_all]
        + [joined_heads(head_all[:, i * heads : (i + 1) * heads]) for i in range(3)]
    )

    squares = (
        jnp.sum(gate_raw * gate_raw)
        + jnp.sum(x_raw * x_raw)
        + jnp.sum(small_raw * small_raw)
        + jnp.sum(out_raw * out_raw)
    )
    squares = summed(summed(jnp.broadcast_to(squares, (8, 128)), "fsdp"), "dp")[0, 0]
    grad_norm = jnp.sqrt(squares + jnp.sum(vector_raw * vector_raw))
    factor = jnp.minimum(1.0, clip_norm / (grad_norm + 1e-06))

    def returned(raw):
        return exchanged(raw.astype(bf16).reshape(fsdp, rows_in, raw.shape[1]), "fsdp")

    def joined_columns(part):
        return (
            part.reshape(fsdp, rows_in, pairs, PAIR).transpose(1, 2, 0, 3).reshape(rows_in, INNER)
        )

    small_back = returned(small_raw)
    in_raw = jnp.concatenate(
        [
            joined_columns(returned(gate_raw)),
            joined_columns(returned(x_raw)),
            small_back[:, :, :shared].transpose(1, 0, 2).reshape(rows_in, 2 * STATE),
            small_back[:, :, shared:]
            .reshape(fsdp, rows_in, pairs, 2)
            .transpose(1, 2, 0, 3)
            .reshape(rows_in, HEADS),
        ],
        axis=1,
    ).astype(f32)
    in_grad = in_raw * factor
    out_grad = out_raw * factor
    vector_grad = vector_raw * factor
    in_moment, in_square, in_master = adamw(in_weight, in_first, in_second, in_grad, rate_in_proj)
    out_moment, out_square, out_master = adamw(
        out_weight, out_first, out_second, out_grad, rate_out_proj
    )
    vector_moment, vector_square, vector_master = adamw(
        vectors, vector_first, vector_second, vector_grad, rate_vectors
    )
    return (
        layer_out,
        token_grad,
        in_grad,
        out_grad,
        vector_grad,
        grad_norm,
        in_moment,
        in_square,
        in_master,
        in_master.astype(bf16),
        out_moment,
        out_square,
        out_master,
        out_master.astype(bf16),
        vector_moment,
        vector_square,
        vector_master,
    )


def solution(mesh):
    rows = P(("dp", "fsdp"), None)
    return jax.shard_map(
        on_device,
        mesh=mesh,
        in_specs=(rows, P("dp")) + (rows,) * 7 + (P(),) * 3,
        out_specs=(rows,) * 4 + (P(),) * 2 + (rows,) * 8 + (P(),) * 3,
        check_vma=False,
    )
```

time: 1800 us -> 780 us (0.43)
  waiting for transfers between devices: 1330 us -> 209 us
  matrix products: 226 us -> 68 us
  local copies, waits for them, and re-layouts: 42.3 us -> 192 us
  starting transfers between devices: 3.75 us -> 121 us
  Pallas kernels: 0 us -> 78.9 us
  blocking collectives: 55.7 us -> 0 us
  other arithmetic: 113 us -> 74.5 us
    reduce_scatter x2 -> x0, waiting for transfers between devices: 906 us -> none  [the longest x1 742 us: on_device(): lax.psum_scatter(row_term(normed_low, projected_grad, rows_in * lax.axis_...]
    all_gather x4 -> x0, waiting for transfers between devices: 296 us -> none  [the longest x1 202 us: on_device(): lax.all_gather(lowered[0], ('dp', 'fsdp'), axis=0, tiled=True)]
    ppermute x2 -> x119, waiting for transfers between devices: 0.01 us -> 209 us  [the longest x55 58.5 us: swapped(): return lax.ppermute(value, axis, [(i, i ^ flip) for i in range(count)])]
    dot_general x20 -> x13, matrix products: 226 us -> 68 us  [the longest x3 20 us: in_back(): lax.dot_general(grad, weight, (((grad_dim,), (1,)), ((), ())), preferred_...]
    psum x1 -> x0, waiting for transfers between devices: 132 us -> none  [on_device(): vector_raw = lax.psum(vector_term, ('dp', 'fsdp'))]
    ppermute x2 -> x119, starting transfers between devices: 3.46 us -> 121 us  [the longest x55 43.6 us: swapped(): return lax.ppermute(value, axis, [(i, i ^ flip) for i in range(count)])]
    dynamic_update_slice x0 -> x73, local copies, waits for them, and re-layouts: none -> 89.3 us  [the longest x38 79.9 us: placed(): lax.dynamic_update_index_in_dim(whole, part, lax.bitwise_xor(me, flip), 0)]
    pallas_call x0 -> x4, Pallas kernels: none -> 78.9 us  [the longest x1 36.1 us: scan_backward(): pl.pallas_call(scan_backward_kernel, grid=(groups,), in_specs=head_specs(...]
  transfers between devices with their start and end apart: 9 -> 119, of which waited for: 6 -> 48; matrix products, arithmetic and copies ran while one was open for 17% -> 33% of each run, Pallas kernels for 0% -> 0%
where the time goes in v1:
time: 780 us; the launch traced here: 767 us
  waiting for transfers between devices  209 us (27%)
  local copies, waits for them, and re-layouts  192 us (25%)
  starting transfers between devices  121 us (16%)
  Pallas kernels  78.9 us (10%)
  other arithmetic  74.5 us (10%)
  matrix products  68 us (9%)
  between operations  24.2 us (3%)
    dynamic_update_slice x38, local copies, waits for them, and re-layouts, placed(): lax.dynamic_update_index_in_dim(whole, part, lax.bitwise_xor(me, flip), 0)  79.9 us
    ppermute x55, waiting for transfers between devices, swapped(): return lax.ppermute(value, axis, [(i, i ^ flip) for i in range(count)])  58.5 us
    ppermute x55, starting transfers between devices, swapped(): return lax.ppermute(value, axis, [(i, i ^ flip) for i in range(count)])  43.6 us
    ppermute x12, waiting for transfers between devices, gather_rows(): going_right = lax.ppermute(going_right, axis, right)  36.2 us
    pallas_call x1, Pallas kernels, scan_backward(): pl.pallas_call(scan_backward_kernel, grid=(groups,), in_specs=head_specs(...  36.1 us
    ppermute x12, waiting for transfers between devices, scatter_rows(): going_left = lax.ppermute(to_left.astype(bf16), axis, left)  35.4 us
    ppermute x12, waiting for transfers between devices, scatter_rows(): going_right = lax.ppermute(to_right.astype(bf16), axis, right)  34.2 us
    ppermute x12, waiting for transfers between devices, gather_rows(): going_left = lax.ppermute(going_left, axis, left)  20.5 us
  transfers between devices with their start and end apart: 119, of which 48 were waited for; matrix products, arithmetic and copies ran while one was open for 33% of the time, Pallas kernels for 0%

profile of v1, /device:TPU:0, one launch (start us, length us, event | category | flops | bytes accessed | tf_op | source)
XLA Modules:
  0.0 767.3 jit_solution(2023957288051047365)
XLA Ops:
  99.7 10.6 %collective-permute-done.23 = bf16[128,80]{1,0:T(8,128)(2,1)S(1)} collective-permute-done((bf16[128,80]{1,0:T(8,128)(2,1)S(1)}, bf16[128,80]{1,0:T(8,128)(2,1)S(1)}, u32[]{:S(2)}, u32[]{:S(2)}) %collective-permute-start.23) | collective-permute-done | bytes 20512 | tf_op jit(solution)/shard_map/ppermute | solution.py:91
  131.1 6.2 collective-permute-done.7
  148.5 14.7 %collective-permute-done.40 = bf16[256,2048]{1,0:T(8,128)(2,1)S(1)} collective-permute-done((bf16[256,2048]{1,0:T(8,128)(2,1)S(1)}, bf16[256,2048]{1,0:T(8,128)(2,1)S(1)}, u32[]{:S(2)}, u32[]{:S(2)}) %collective-permute-start.40) | collective-permute-done | bytes 1048608 | tf_op jit(solution)/shard_map/ppermute | solution.py:126
  170.2 7.8 %collective-permute-done.8 = bf16[256,1024]{1,0:T(8,128)(2,1)S(1)} collective-permute-done((bf16[256,1024]{1,0:T(8,128)(2,1)S(1)}, bf16[256,1024]{1,0:T(8,128)(2,1)S(1)}, u32[]{:S(2)}, u32[]{:S(2)}) %collective-permute-start.8) | collective-permute-done | bytes 524320 | tf_op jit(solution)/shard_map/ppermute | solution.py:87
  181.2 8.1 %collective-permute-done.46 = bf16[128,2048]{1,0:T(8,128)(2,1)S(1)} collective-permute-done((bf16[128,2048]{1,0:T(8,128)(2,1)S(1)}, bf16[128,2048]{1,0:T(8,128)(2,1)S(1)}, u32[]{:S(2)}, u32[]{:S(2)}) %collective-permute-start.46) | collective-permute-done | bytes 524320 | tf_op jit(solution)/shard_map/ppermute | solution.py:87
  193.3 7.3 collective-permute-done.35
  202.8 7.7 %collective-permute-done.10 = bf16[256,1024]{1,0:T(8,128)(2,1)S(1)} collective-permute-done((bf16[256,1024]{1,0:T(8,128)(2,1)S(1)}, bf16[256,1024]{1,0:T(8,128)(2,1)S(1)}, u32[]{:S(2)}, u32[]{:S(2)}) %collective-permute-start.10) | collective-permute-done | bytes 524320 | tf_op jit(solution)/shard_map/ppermute | solution.py:87
  237.0 8.2 %fusion.93.x_ref = f32[1024,1024]{1,0:T(8,128)} fusion(bf16[1024,2048]{1,0:T(8,128)(2,1)} %bitcast.4.normed_ref, bf16[2048,1024]{1,0:T(8,128)(2,1)S(1)} %constant_dynamic-update-slice_fusion.35), kind=kOutput, calls=%fused_computation.359 | convolution fusion | flops 4294967296 | bytes 12582912 | tf_op jit(solution)/shard_map/dot_general | solution.py:761
  256.8 18.1 %scan_forward.1 = (f32[1024,1024]{1,0:T(8,128)}, bf16[8,128,1024]{2,1,0:T(8,128)(2,1)}) custom-call(f32[1024,1024]{1,0:T(8,128)} %fusion.93.x_ref, f32[4,1024]{1,0:T(4,128)} %bitcast.426, f32[1,1024]{1,0:T(1,128)} %fusion.60.bias_ref, f32[1,1024]{1,0:T(1,128)} %broadcast_in_dim_reshape.14.mask_ref, f32[1,1024]{1,0:T(1,128)} %broadcast_in_dim_reshape.15.skip_ref, ...), custom_call_target="tpu_custom_call" | custom-call | flops 10000000000 | bytes 12000000 | tf_op jit(solution)/shard_map/scan_forward/pallas_call | solution.py:449
  274.9 15.8 %gate_forward.1 = (f32[1024,1024]{1,0:T(8,128)}, f32[1024,1024]{1,0:T(8,128)}, f32[1024,128]{1,0:T(8,128)}) custom-call(bf16[1024,2048]{1,0:T(8,128)(2,1)} %bitcast.4.normed_ref, bf16[2048,1024]{1,0:T(8,128)(2,1)} %copy-done.14, bf16[1024,2048]{1,0:T(8,128)(2,1)} %bitcast.76.cotangent_ref, bf16[1024,2048]{1,0:T(8,128)(2,1)} %constant_dynamic-update-slice_fusion.out_ref, ...), custom_call_target="tpu_custom_call" | custom-call | flops 8999999488 | bytes 28000000 | tf_op jit(solution)/shard_map/gate_forward/pallas_call | solution.py:537
  294.6 12.2 %collective-permute-done.51 = f32[2,1024]{0,1:T(8,128)S(1)} collective-permute-done((f32[2,1024]{0,1:T(8,128)S(1)}, f32[2,1024]{0,1:T(8,128)S(1)}, u32[]{:S(2)}, u32[]{:S(2)}) %collective-permute-start.51) | collective-permute-done | bytes 8224 | tf_op jit(solution)/shard_map/ppermute | solution.py:126
  306.8 9.9 %collective-permute-done.52 = f32[2,1024]{0,1:T(8,128)S(1)} collective-permute-done((f32[2,1024]{0,1:T(8,128)S(1)}, f32[2,1024]{0,1:T(8,128)S(1)}, u32[]{:S(2)}, u32[]{:S(2)}) %collective-permute-start.52) | collective-permute-done | bytes 8224 | tf_op jit(solution)/shard_map/ppermute | solution.py:126
  319.4 9.0 %norm_back.1 = (bf16[1024,1024]{1,0:T(8,128)(2,1)}, bf16[1024,1024]{1,0:T(8,128)(2,1)}, bf16[1024,1024]{1,0:T(8,128)(2,1)}, f32[8,1024]{1,0:T(8,128)}) custom-call(f32[1024,1024]{1,0:T(8,128)} %get-tuple-element.32.y_ref, f32[1024,1024]{1,0:T(8,128)} %get-tuple-element.33.gate_part_ref, f32[1024,1024]{1,0:T(8,128)} %get-tuple-element.34.gated_grad_ref, ...), custom_call_target="tpu_custom_call" | custom-call | flops 30000000 | bytes 18000000 | tf_op jit(solution)/shard_map/norm_back/pallas_call | solution.py:584
  328.4 36.1 %scan_backward.1 = (bf16[1024,1024]{1,0:T(8,128)(2,1)}, f32[1024,128]{1,0:T(8,128)}, f32[1024,128]{1,0:T(8,128)}, f32[1024,512]{1,0:T(8,128)}, f32[8,1,1024]{2,1,0:T(1,128)}, /*index=5*/f32[8,1024]{1,0:T(8,128)}) custom-call(f32[1024,1024]{1,0:T(8,128)} %fusion.93.x_ref, f32[4,1024]{1,0:T(4,128)} %bitcast.427, f32[1,1024]{1,0:T(1,128)} %fusion.60.bias_ref, ...), custom_call_target="tpu_custom_call" | custom-call | flops 30000001024 | bytes 16000000 | tf_op jit(solution)/shard_map/scan_backward/pallas_call | solution.py:477
  364.6 8.5 %fusion.96 = f32[1024,2048]{1,0:T(8,128)} fusion(bf16[1024,1024]{1,0:T(8,128)(2,1)} %get-tuple-element.40, bf16[2048,1024]{1,0:T(8,128)(2,1)S(1)} %copy-done.17), kind=kOutput, calls=%fused_computation.362 | convolution fusion | flops 4294967296 | bytes 14680064 | tf_op jit(solution)/shard_map/dot_general | solution.py:852
  373.1 8.8 %convolution_convert_fusion.1 = bf16[2048,1024]{1,0:T(8,128)(2,1)} fusion(bf16[1024,2048]{1,0:T(8,128)(2,1)} %bitcast.4.normed_ref, bf16[1024,1024]{1,0:T(8,128)(2,1)S(1)} %copy-done.73), kind=kOutput, calls=%fused_computation.8 | convolution fusion | flops 4297064448 | bytes 10485760 | tf_op jit(solution)/shard_map/dot_general | solution.py:797
  381.9 6.8 fusion.95
  388.7 8.6 %convolution_convert_fusion.2 = bf16[2048,1024]{1,0:T(8,128)(2,1)} fusion(bf16[1024,2048]{1,0:T(8,128)(2,1)} %bitcast.4.normed_ref, bf16[1024,1024]{1,0:T(8,128)(2,1)S(1)} %copy-done.72), kind=kOutput, calls=%fused_computation.9 | convolution fusion | flops 4297064448 | bytes 10485760 | tf_op jit(solution)/shard_map/dot_general | solution.py:797
  397.2 8.6 %convolution_convert_fusion = bf16[1024,2048]{1,0:T(8,128)(2,1)} fusion(bf16[1024,1024]{1,0:T(8,128)(2,1)S(1)} %copy-done.71, bf16[1024,2048]{1,0:T(8,128)(2,1)} %bitcast.76.cotangent_ref), kind=kOutput, calls=%fused_computation.7 | convolution fusion | flops 4297064448 | bytes 10485760 | tf_op jit(solution)/shard_map/dot_general | solution.py:775
  405.8 6.1 convolution_convert_fusion.3
  499.9 6.1 collective-permute-done.96
  527.4 7.7 %collective-permute-done.97 = bf16[128,2048]{1,0:T(8,128)(2,1)S(1)} collective-permute-done((bf16[128,2048]{1,0:T(8,128)(2,1)S(1)}, bf16[128,2048]{1,0:T(8,128)(2,1)S(1)}, u32[]{:S(2)}, u32[]{:S(2)}) %collective-permute-start.97) | collective-permute-done | bytes 524320 | tf_op jit(solution)/shard_map/ppermute | solution.py:119
  550.4 13.6 %collective-permute-done.79 = bf16[256,1024]{1,0:T(8,128)(2,1)} collective-permute-done((bf16[256,1024]{1,0:T(8,128)(2,1)}, bf16[256,1024]{1,0:T(8,128)(2,1)}, u32[]{:S(2)}, u32[]{:S(2)}) %collective-permute-start.79) | collective-permute-done | bytes 524320 | tf_op jit(solution)/shard_map/ppermute | solution.py:120
  566.7 8.3 %collective-permute-done.113 = f32[9,1024]{1,0:T(8,128)S(1)} collective-permute-done((f32[9,1024]{1,0:T(8,128)S(1)}, f32[9,1024]{1,0:T(8,128)S(1)}, u32[]{:S(2)}, u32[]{:S(2)}) %collective-permute-start.113) | collective-permute-done | bytes 36896 | tf_op jit(solution)/shard_map/ppermute | solution.py:126
  585.7 6.4 collective-permute-done.65
  598.1 7.8 %collective-permute-done.69 = bf16[256,1024]{1,0:T(8,128)(2,1)S(1)} collective-permute-done((bf16[256,1024]{1,0:T(8,128)(2,1)S(1)}, bf16[256,1024]{1,0:T(8,128)(2,1)S(1)}, u32[]{:S(2)}, u32[]{:S(2)}) %collective-permute-start.69) | collective-permute-done | bytes 524320 | tf_op jit(solution)/shard_map/ppermute | solution.py:120
  620.7 5.8 fusion.8
  631.9 12.5 %dynamic_update_slice.320 = f32[4,9,1024]{0,2,1:T(8,128)} dynamic-update-slice(f32[4,9,1024]{0,2,1:T(8,128)} %broadcast_in_dim.201, f32[1,9,1024]{0,2,1:T(8,128)} %copy.256, s32[]{:T(128)S(6)} %select_n.573, s32[]{:T(128)} %constant.649.clone.1, s32[]{:T(128)} %constant.649.clone.1) | dynamic-update-slice | bytes 73732 | tf_op jit(solution)/shard_map/jit(dynamic_update_index_in_dim)/dynamic_update_slice | solution.py:152
  677.0 14.2 %dynamic_update_slice.321 = f32[4,9,1024]{0,2,1:T(8,128)} dynamic-update-slice(f32[4,9,1024]{0,2,1:T(8,128)} %dynamic_update_slice.320, f32[1,9,1024]{0,2,1:T(8,128)} %copy.257, s32[]{:T(128)S(6)} %select_n.574, s32[]{:T(128)} %constant.649.clone.1, s32[]{:T(128)} %constant.649.clone.1) | dynamic-update-slice | bytes 73732 | tf_op jit(solution)/shard_map/jit(dynamic_update_index_in_dim)/dynamic_update_slice | solution.py:152
  691.1 14.2 %dynamic_update_slice.322 = f32[4,9,1024]{0,2,1:T(8,128)} dynamic-update-slice(f32[4,9,1024]{0,2,1:T(8,128)} %dynamic_update_slice.321, f32[1,9,1024]{0,2,1:T(8,128)} %copy.258, s32[]{:T(128)S(6)} %select_n.575, s32[]{:T(128)} %constant.649.clone.1, s32[]{:T(128)} %constant.649.clone.1) | dynamic-update-slice | bytes 73732 | tf_op jit(solution)/shard_map/jit(dynamic_update_index_in_dim)/dynamic_update_slice | solution.py:152
  705.3 14.2 %dynamic_update_slice.323 = f32[4,9,1024]{0,2,1:T(8,128)} dynamic-update-slice(f32[4,9,1024]{0,2,1:T(8,128)} %dynamic_update_slice.322, f32[1,9,1024]{0,2,1:T(8,128)} %copy.259, s32[]{:T(128)S(6)} %select_n.576, s32[]{:T(128)} %constant.649.clone.1, s32[]{:T(128)} %constant.649.clone.1) | dynamic-update-slice | bytes 73732 | tf_op jit(solution)/shard_map/jit(dynamic_update_index_in_dim)/dynamic_update_slice | solution.py:152
  759.6 6.4 fusion.79
  (689 shorter events, 406.9 us)
Async XLA Ops:
  13.2 102.7 %collective-permute-start.42 = (bf16[128,2048]{1,0:T(8,128)(2,1)}, bf16[128,2048]{1,0:T(8,128)(2,1)}, u32[]{:S(2)}, u32[]{:S(2)}) collective-permute-start(bf16[128,2048]{1,0:T(8,128)(2,1)} %get-tuple-element.74), channel_id=1, source_target_pairs={{0,8},{8,16},{16,24},{24,28},{28,20},{20,12},{12,4},{4,0},{1,9},{9... | collective-permute-start | bytes 1572872 | tf_op jit(solution)/shard_map/ppermute | solution.py:87
  16.2 102.1 %collective-permute-start.43 = (bf16[128,2048]{1,0:T(8,128)(2,1)}, bf16[128,2048]{1,0:T(8,128)(2,1)}, u32[]{:S(2)}, u32[]{:S(2)}) collective-permute-start(bf16[128,2048]{1,0:T(8,128)(2,1)} %get-tuple-element.74), channel_id=1, source_target_pairs={{8,0},{16,8},{24,16},{28,24},{20,28},{12,20},{4,12},{0,4},{9,1},{1... | collective-permute-start | bytes 1572872 | tf_op jit(solution)/shard_map/ppermute | solution.py:88
  21.3 37.8 %collective-permute-start.14 = (bf16[64,80]{1,0:T(8,128)(2,1)}, bf16[64,80]{1,0:T(8,128)(2,1)}, u32[]{:S(2)}, u32[]{:S(2)}) collective-permute-start(bf16[64,80]{1,0:T(8,128)(2,1)} %get-tuple-element.167), channel_id=1, source_target_pairs={{0,1},{1,0},{2,3},{3,2},{4,5},{5,4},{6,7},{7,6},{8,9},{9,8},{10,11... | collective-permute-start | bytes 30728 | tf_op jit(solution)/shard_map/ppermute | solution.py:126
  21.3 38.7 %collective-permute-start.15 = (bf16[64,80]{1,0:T(8,128)(2,1)}, bf16[64,80]{1,0:T(8,128)(2,1)}, u32[]{:S(2)}, u32[]{:S(2)}) collective-permute-start(bf16[64,80]{1,0:T(8,128)(2,1)} %get-tuple-element.168), channel_id=1, source_target_pairs={{0,2},{1,3},{2,0},{3,1},{4,6},{5,7},{6,4},{7,5},{8,10},{9,11},{10,... | collective-permute-start | bytes 30728 | tf_op jit(solution)/shard_map/ppermute | solution.py:126
  23.2 39.5 %collective-permute-start.16 = (bf16[64,80]{1,0:T(8,128)(2,1)}, bf16[64,80]{1,0:T(8,128)(2,1)}, u32[]{:S(2)}, u32[]{:S(2)}) collective-permute-start(bf16[64,80]{1,0:T(8,128)(2,1)} %get-tuple-element.165), channel_id=1, source_target_pairs={{0,3},{1,2},{2,1},{3,0},{4,7},{5,6},{6,5},{7,4},{8,11},{9,10},{10,... | collective-permute-start | bytes 30728 | tf_op jit(solution)/shard_map/ppermute | solution.py:126
  80.9 56.4 %collective-permute-start = (bf16[256,2048]{1,0:T(8,128)(2,1)}, bf16[256,2048]{1,0:T(8,128)(2,1)S(1)}, u32[]{:S(2)}, u32[]{:S(2)}) collective-permute-start(bf16[256,2048]{1,0:T(8,128)(2,1)} %get-tuple-element.81), channel_id=1, source_target_pairs={{0,1},{1,0},{2,3},{3,2},{4,5},{5,4},{6,7},{7,6},{8,9},{9,8},{10,11... | collective-permute-start | bytes 3145736 | tf_op jit(solution)/shard_map/ppermute | solution.py:126
  118.3 26.1 %collective-permute-start.1 = (bf16[256,2048]{1,0:T(8,128)(2,1)S(1)}, bf16[256,2048]{1,0:T(8,128)(2,1)S(1)}, u32[]{:S(2)}, u32[]{:S(2)}) collective-permute-start(bf16[256,2048]{1,0:T(8,128)(2,1)S(1)} %copy-done.25), channel_id=1, source_target_pairs={{0,2},{1,3},{2,0},{3,1},{4,6},{5,7},{6,4},{7,5},{8,10},{9,11},{10,... | collective-permute-start | bytes 3145736 | tf_op jit(solution)/shard_map/ppermute | solution.py:126
  129.2 34.0 %collective-permute-start.40 = (bf16[256,2048]{1,0:T(8,128)(2,1)S(1)}, bf16[256,2048]{1,0:T(8,128)(2,1)S(1)}, u32[]{:S(2)}, u32[]{:S(2)}) collective-permute-start(bf16[256,2048]{1,0:T(8,128)(2,1)S(1)} %copy-done.7), channel_id=1, source_target_pairs={{0,2},{1,3},{2,0},{3,1},{4,6},{5,7},{6,4},{7,5},{8,10},{9,11},{10,... | collective-permute-start | bytes 3145736 | tf_op jit(solution)/shard_map/ppermute | solution.py:126
  137.3 27.3 %collective-permute-start.44 = (bf16[128,2048]{1,0:T(8,128)(2,1)}, bf16[128,2048]{1,0:T(8,128)(2,1)S(1)}, u32[]{:S(2)}, u32[]{:S(2)}) collective-permute-start(bf16[128,2048]{1,0:T(8,128)(2,1)} %collective-permute-done.42), channel_id=1, source_target_pairs={{0,8},{8,16},{16,24},{24,28},{28,20},{20,12},{12,4},{4,0},{1,9},{9... | collective-permute-start | bytes 1572872 | tf_op jit(solution)/shard_map/ppermute | solution.py:87
  137.3 29.8 %collective-permute-start.45 = (bf16[128,2048]{1,0:T(8,128)(2,1)}, bf16[128,2048]{1,0:T(8,128)(2,1)S(1)}, u32[]{:S(2)}, u32[]{:S(2)}) collective-permute-start(bf16[128,2048]{1,0:T(8,128)(2,1)} %collective-permute-done.43), channel_id=1, source_target_pairs={{8,0},{16,8},{24,16},{28,24},{20,28},{12,20},{4,12},{0,4},{9,1},{1... | collective-permute-start | bytes 1572872 | tf_op jit(solution)/shard_map/ppermute | solution.py:88
  170.1 57.6 %collective-permute-start.2 = (bf16[256,2048]{1,0:T(8,128)(2,1)S(1)}, bf16[256,2048]{1,0:T(8,128)(2,1)S(1)}, u32[]{:S(2)}, u32[]{:S(2)}) collective-permute-start(bf16[256,2048]{1,0:T(8,128)(2,1)S(1)} %collective-permute-done.1), channel_id=1, source_target_pairs={{0,1},{1,0},{2,3},{3,2},{4,5},{5,4},{6,7},{7,6},{8,9},{9,8},{10,11... | collective-permute-start | bytes 3145736 | tf_op jit(solution)/shard_map/ppermute | solution.py:126
  200.5 44.7 %collective-permute-start.41 = (bf16[256,2048]{1,0:T(8,128)(2,1)S(1)}, bf16[256,2048]{1,0:T(8,128)(2,1)S(1)}, u32[]{:S(2)}, u32[]{:S(2)}) collective-permute-start(bf16[256,2048]{1,0:T(8,128)(2,1)S(1)} %collective-permute-done.40), channel_id=1, source_target_pairs={{0,1},{1,0},{2,3},{3,2},{4,5},{5,4},{6,7},{7,6},{8,9},{9,8},{10,11... | collective-permute-start | bytes 3145736 | tf_op jit(solution)/shard_map/ppermute | solution.py:126
  427.0 45.0 %collective-permute-start.95 = (bf16[64,2048]{1,0:T(8,128)(2,1)}, bf16[64,2048]{1,0:T(8,128)(2,1)}, u32[]{:S(2)}, u32[]{:S(2)}) collective-permute-start(bf16[64,2048]{1,0:T(8,128)(2,1)} %get-tuple-element.97), channel_id=1, source_target_pairs={{0,8},{8,16},{16,24},{24,28},{28,20},{20,12},{12,4},{4,0},{1,9},{9... | collective-permute-start | bytes 786440 | tf_op jit(solution)/shard_map/ppermute | solution.py:110
  429.6 32.7 %collective-permute-start.73 = (bf16[128,1024]{1,0:T(8,128)(2,1)}, bf16[128,1024]{1,0:T(8,128)(2,1)}, u32[]{:S(2)}, u32[]{:S(2)}) collective-permute-start(bf16[128,1024]{1,0:T(8,128)(2,1)} %get-tuple-element.105), channel_id=1, source_target_pairs={{0,8},{8,16},{16,24},{24,28},{28,20},{20,12},{12,4},{4,0},{1,9},{9... | collective-permute-start | bytes 786440 | tf_op jit(solution)/shard_map/ppermute | solution.py:110
  433.6 30.1 %collective-permute-start.77 = (bf16[128,1024]{1,0:T(8,128)(2,1)}, bf16[128,1024]{1,0:T(8,128)(2,1)}, u32[]{:S(2)}, u32[]{:S(2)}) collective-permute-start(bf16[128,1024]{1,0:T(8,128)(2,1)} %get-tuple-element.107), channel_id=1, source_target_pairs={{8,0},{16,8},{24,16},{28,24},{20,28},{12,20},{4,12},{0,4},{9,1},{1... | collective-permute-start | bytes 786440 | tf_op jit(solution)/shard_map/ppermute | solution.py:111
  463.7 45.3 %collective-permute-start.54 = (bf16[256,2048]{1,0:T(8,128)(2,1)S(1)}, bf16[256,2048]{1,0:T(8,128)(2,1)}, u32[]{:S(2)}, u32[]{:S(2)}) collective-permute-start(bf16[256,2048]{1,0:T(8,128)(2,1)S(1)} %get-tuple-element.120), channel_id=1, source_target_pairs={{0,1},{1,0},{2,3},{3,2},{4,5},{5,4},{6,7},{7,6},{8,9},{9,8},{10,11... | collective-permute-start | bytes 3145736 | tf_op jit(solution)/shard_map/ppermute | solution.py:126
  487.8 24.5 %collective-permute-start.60 = (bf16[256,2048]{1,0:T(8,128)(2,1)}, bf16[256,2048]{1,0:T(8,128)(2,1)}, u32[]{:S(2)}, u32[]{:S(2)}) collective-permute-start(bf16[256,2048]{1,0:T(8,128)(2,1)} %get-tuple-element.118), channel_id=1, source_target_pairs={{0,1},{1,0},{2,3},{3,2},{4,5},{5,4},{6,7},{7,6},{8,9},{9,8},{10,11... | collective-permute-start | bytes 3145736 | tf_op jit(solution)/shard_map/ppermute | solution.py:126
  491.8 54.8 %collective-permute-start.59 = (bf16[256,2048]{1,0:T(8,128)(2,1)}, bf16[256,2048]{1,0:T(8,128)(2,1)S(1)}, u32[]{:S(2)}, u32[]{:S(2)}) collective-permute-start(bf16[256,2048]{1,0:T(8,128)(2,1)} %get-tuple-element.117), channel_id=1, source_target_pairs={{0,1},{1,0},{2,3},{3,2},{4,5},{5,4},{6,7},{7,6},{8,9},{9,8},{10,11... | collective-permute-start | bytes 3145736 | tf_op jit(solution)/shard_map/ppermute | solution.py:126
  535.1 84.5 %collective-permute-start.53 = (bf16[256,2048]{1,0:T(8,128)(2,1)}, bf16[256,2048]{1,0:T(8,128)(2,1)}, u32[]{:S(2)}, u32[]{:S(2)}) collective-permute-start(bf16[256,2048]{1,0:T(8,128)(2,1)} %get-tuple-element.119), channel_id=1, source_target_pairs={{0,1},{1,0},{2,3},{3,2},{4,5},{5,4},{6,7},{7,6},{8,9},{9,8},{10,11... | collective-permute-start | bytes 3145736 | tf_op jit(solution)/shard_map/ppermute | solution.py:126
  537.7 40.1 %collective-permute-start.101 = (bf16[128,2048]{1,0:T(8,128)(2,1)}, bf16[128,2048]{1,0:T(8,128)(2,1)}, u32[]{:S(2)}, u32[]{:S(2)}) collective-permute-start(bf16[128,2048]{1,0:T(8,128)(2,1)} %get-tuple-element.94), channel_id=1, source_target_pairs={{8,0},{16,8},{24,16},{28,24},{20,28},{12,20},{4,12},{0,4},{9,1},{1... | collective-permute-start | bytes 1572872 | tf_op jit(solution)/shard_map/ppermute | solution.py:120
  546.6 33.2 %collective-permute-start.76 = (bf16[256,1024]{1,0:T(8,128)(2,1)}, bf16[256,1024]{1,0:T(8,128)(2,1)}, u32[]{:S(2)}, u32[]{:S(2)}) collective-permute-start(bf16[256,1024]{1,0:T(8,128)(2,1)} %get-tuple-element.101), channel_id=1, source_target_pairs={{0,8},{8,16},{16,24},{24,28},{28,20},{20,12},{12,4},{4,0},{1,9},{9... | collective-permute-start | bytes 1572872 | tf_op jit(solution)/shard_map/ppermute | solution.py:119
  547.7 28.6 %collective-permute-start.68 = (bf16[256,1024]{1,0:T(8,128)(2,1)}, bf16[256,1024]{1,0:T(8,128)(2,1)}, u32[]{:S(2)}, u32[]{:S(2)}) collective-permute-start(bf16[256,1024]{1,0:T(8,128)(2,1)} %get-tuple-element.110), channel_id=1, source_target_pairs={{8,0},{16,8},{24,16},{28,24},{20,28},{12,20},{4,12},{0,4},{9,1},{1... | collective-permute-start | bytes 1572872 | tf_op jit(solution)/shard_map/ppermute | solution.py:120
  575.0 45.7 %collective-permute-start.55 = (bf16[256,2048]{1,0:T(8,128)(2,1)}, bf16[256,2048]{1,0:T(8,128)(2,1)}, u32[]{:S(2)}, u32[]{:S(2)}) collective-permute-start(bf16[256,2048]{1,0:T(8,128)(2,1)} %fusion.13), channel_id=1, source_target_pairs={{0,2},{1,3},{2,0},{3,1},{4,6},{5,7},{6,4},{7,5},{8,10},{9,11},{10,... | collective-permute-start | bytes 3145736 | tf_op jit(solution)/shard_map/ppermute | solution.py:126
  580.6 25.3 %collective-permute-start.69 = (bf16[256,1024]{1,0:T(8,128)(2,1)S(1)}, bf16[256,1024]{1,0:T(8,128)(2,1)S(1)}, u32[]{:S(2)}, u32[]{:S(2)}) collective-permute-start(bf16[256,1024]{1,0:T(8,128)(2,1)S(1)} %add_convert_fusion.9), channel_id=1, source_target_pairs={{8,0},{16,8},{24,16},{28,24},{20,28},{12,20},{4,12},{0,4},{9,1},{1... | collective-permute-start | bytes 1572872 | tf_op jit(solution)/shard_map/ppermute | solution.py:120
  618.7 25.7 %collective-permute-start.103 = (f32[8,128]{1,0:T(8,128)S(1)}, f32[8,128]{1,0:T(8,128)S(1)}, u32[]{:S(2)}, u32[]{:S(2)}) collective-permute-start(f32[8,128]{1,0:T(8,128)S(1)} %broadcast_in_dim.200), channel_id=1, source_target_pairs={{0,1},{1,0},{2,3},{3,2},{4,5},{5,4},{6,7},{7,6},{8,9},{9,8},{10,11... | collective-permute-start | bytes 12296 | tf_op jit(solution)/shard_map/ppermute | solution.py:126
  618.8 25.7 %collective-permute-start.104 = (f32[8,128]{1,0:T(8,128)S(1)}, f32[8,128]{1,0:T(8,128)S(1)}, u32[]{:S(2)}, u32[]{:S(2)}) collective-permute-start(f32[8,128]{1,0:T(8,128)S(1)} %broadcast_in_dim.200), channel_id=1, source_target_pairs={{0,2},{1,3},{2,0},{3,1},{4,6},{5,7},{6,4},{7,5},{8,10},{9,11},{10,... | collective-permute-start | bytes 12296 | tf_op jit(solution)/shard_map/ppermute | solution.py:126
  619.7 24.8 %collective-permute-start.105 = (f32[8,128]{1,0:T(8,128)S(1)}, f32[8,128]{1,0:T(8,128)S(1)}, u32[]{:S(2)}, u32[]{:S(2)}) collective-permute-start(f32[8,128]{1,0:T(8,128)S(1)} %broadcast_in_dim.200), channel_id=1, source_target_pairs={{0,3},{1,2},{2,1},{3,0},{4,7},{5,6},{6,5},{7,4},{8,11},{9,10},{10,... | collective-permute-start | bytes 12296 | tf_op jit(solution)/shard_map/ppermute | solution.py:126
  662.7 82.9 %collective-permute-start.70 = (bf16[64,1024]{1,0:T(8,128)(2,1)}, bf16[64,1024]{1,0:T(8,128)(2,1)S(1)}, u32[]{:S(2)}, u32[]{:S(2)}) collective-permute-start(bf16[64,1024]{1,0:T(8,128)(2,1)} %get-tuple-element.127), channel_id=1, source_target_pairs={{0,1},{1,0},{2,3},{3,2},{4,5},{5,4},{6,7},{7,6},{8,9},{9,8},{10,11... | collective-permute-start | bytes 393224 | tf_op jit(solution)/shard_map/ppermute | solution.py:126
  663.1 83.1 %collective-permute-start.71 = (bf16[64,1024]{1,0:T(8,128)(2,1)}, bf16[64,1024]{1,0:T(8,128)(2,1)}, u32[]{:S(2)}, u32[]{:S(2)}) collective-permute-start(bf16[64,1024]{1,0:T(8,128)(2,1)} %get-tuple-element.126), channel_id=1, source_target_pairs={{0,2},{1,3},{2,0},{3,1},{4,6},{5,7},{6,4},{7,5},{8,10},{9,11},{10,... | collective-permute-start | bytes 393224 | tf_op jit(solution)/shard_map/ppermute | solution.py:126
  666.2 81.6 %collective-permute-start.72 = (bf16[64,1024]{1,0:T(8,128)(2,1)}, bf16[64,1024]{1,0:T(8,128)(2,1)}, u32[]{:S(2)}, u32[]{:S(2)}) collective-permute-start(bf16[64,1024]{1,0:T(8,128)(2,1)} %get-tuple-element.125), channel_id=1, source_target_pairs={{0,3},{1,2},{2,1},{3,0},{4,7},{5,6},{6,5},{7,4},{8,11},{9,10},{10,... | collective-permute-start | bytes 393224 | tf_op jit(solution)/shard_map/ppermute | solution.py:126
  669.1 82.6 %collective-permute-start.81 = (bf16[64,1024]{1,0:T(8,128)(2,1)}, bf16[64,1024]{1,0:T(8,128)(2,1)}, u32[]{:S(2)}, u32[]{:S(2)}) collective-permute-start(bf16[64,1024]{1,0:T(8,128)(2,1)} %get-tuple-element.131), channel_id=1, source_target_pairs={{0,1},{1,0},{2,3},{3,2},{4,5},{5,4},{6,7},{7,6},{8,9},{9,8},{10,11... | collective-permute-start | bytes 393224 | tf_op jit(solution)/shard_map/ppermute | solution.py:126
  672.1 81.2 %collective-permute-start.82 = (bf16[64,1024]{1,0:T(8,128)(2,1)}, bf16[64,1024]{1,0:T(8,128)(2,1)}, u32[]{:S(2)}, u32[]{:S(2)}) collective-permute-start(bf16[64,1024]{1,0:T(8,128)(2,1)} %get-tuple-element.130), channel_id=1, source_target_pairs={{0,2},{1,3},{2,0},{3,1},{4,6},{5,7},{6,4},{7,5},{8,10},{9,11},{10,... | collective-permute-start | bytes 393224 | tf_op jit(solution)/shard_map/ppermute | solution.py:126
  (165 other events, 2732.9 us)

commit v2 on v1

--- a/solution.py
+++ b/solution.py
@@ -34,7 +34,7 @@
 highest = lax.Precision.HIGHEST
 f32 = jnp.float32
 bf16 = jnp.bfloat16
-VMEM_BYTES = 56 * 1024 * 1024
+VMEM_BYTES = 60 * 1024 * 1024
 
 
 def ring_order(count):
@@ -602,6 +602,527 @@
     )(y, gate_part, gated_grad, scales, gain, mask)
 
 
+MESH = pl.DeviceIdType.MESH
+
+
+class Ring:
+    def __init__(self):
+        self.count = lax.axis_size("dp")
+        self.far = self.count // 2
+        me = lax.axis_index("dp")
+        odd = lax.rem(me, 2)
+        self.me = me
+        self.place = (1 - odd) * lax.div(me, 2) + odd * lax.div(2 * self.count - 1 - me, 2)
+
+    def member(self, distance):
+        n = self.count
+        place = lax.rem(self.place + distance + n, n)
+        back = lax.div(place, n // 2)
+        return (1 - back) * 2 * place + back * (2 * n - 1 - 2 * place)
+
+    def target(self, way):
+        return {"dp": self.member(1 if way == 0 else -1)}
+
+
+def partner(flip):
+    f = lax.axis_index("fsdp")
+    return (f, f + 1 - 2 * lax.rem(f, 2), lax.rem(f + 2, 4), 3 - f)[flip]
+
+
+def greet(targets):
+    barrier = pltpu.get_barrier_semaphore()
+    for target in targets:
+        pl.semaphore_signal(barrier, inc=1, device_id=target, device_id_type=MESH)
+    pl.semaphore_wait(barrier, len(targets))
+
+
+def row_slice(ref, start, size):
+    return ref.at[pl.ds(pl.multiple_of(start, 16), size)]
+
+
+class RingGather:
+    def __init__(self, ring, wholes, send, recv):
+        self.ring, self.wholes, self.send, self.recv = ring, wholes, send, recv
+
+    @staticmethod
+    def semaphores(parts, count):
+        return pltpu.SemaphoreType.DMA((parts * 4 * (count // 2),))
+
+    def copy(self, part, way, half, hop):
+        whole = self.wholes[part]
+        rows = whole.shape[0] // self.ring.count
+        size = rows // 2
+        owner = self.ring.member(-hop if way == 0 else hop)
+        place = row_slice(whole, owner * rows + half * size, size)
+        at = ((part * 2 + way) * 2 + half) * self.ring.far + hop
+        return pltpu.make_async_remote_copy(
+            place, place, self.send.at[at], self.recv.at[at],
+            device_id=self.ring.target(way), device_id_type=MESH,
+        )
+
+    def pieces(self, hop):
+        return [
+            (way, half)
+            for half in (0, 1)
+            for way in (0, 1)
+            if hop < self.ring.far - 1 or half == way
+        ]
+
+    def start(self, part, hop):
+        for way, half in self.pieces(hop):
+            if hop:
+                self.copy(part, way, half, hop - 1).wait_recv()
+            self.copy(part, way, half, hop).start()
+
+    def finish(self, part):
+        last = self.ring.far - 1
+        for way, half in self.pieces(last):
+            self.copy(part, way, half, last).wait_recv()
+            if last:
+                self.copy(part, way, 1 - half, last - 1).wait_recv()
+        for hop in range(last + 1):
+            for way, half in self.pieces(hop):
+                self.copy(part, way, half, hop).wait_send()
+
+
+class RingScatter:
+    def __init__(self, ring, held, arrived, send, recv):
+        self.ring, self.held, self.arrived = ring, held, arrived
+        self.send, self.recv = send, recv
+
+    @staticmethod
+    def scratch(count, rows, columns):
+        hops = count // 2
+        return [
+            pltpu.VMEM((2, 2, rows, columns), bf16),
+            pltpu.VMEM((2, hops, rows, columns), bf16),
+            pltpu.SemaphoreType.DMA((2 * hops,)),
+            pltpu.SemaphoreType.DMA((2 * hops,)),
+        ]
+
+    def copy(self, way, hop):
+        rows = self.held.shape[2]
+        size = rows // 2 if hop == 0 else rows
+        at = way * self.ring.far + hop
+        return pltpu.make_async_remote_copy(
+            self.held.at[way, hop % 2, pl.ds(0, size)],
+            self.arrived.at[way, hop, pl.ds(0, size)],
+            self.send.at[at], self.recv.at[at],
+            device_id=self.ring.target(way), device_id_type=MESH,
+        )
+
+    def owner(self, way, hop):
+        distance = self.ring.far - hop
+        return self.ring.member(distance if way == 0 else -distance)
+
+    def start(self, hop, term):
+        rows = self.held.shape[2]
+        half = rows // 2
+        if hop == 0:
+            value = term(self.owner(0, 0)).astype(bf16)
+            self.held[0, 0, 0:half] = value[:half]
+            self.copy(0, 0).start()
+            self.held[1, 0, 0:half] = value[half:]
+            self.copy(1, 0).start()
+            return
+        for way in (0, 1):
+            value = term(self.owner(way, hop))
+            self.copy(way, hop - 1).wait_recv()
+            slot = hop % 2
+            if hop >= 2:
+                self.copy(way, hop - 2).wait_send()
+            if hop == 1:
+                low = slice(way * half, (way + 1) * half)
+                rest = slice((1 - way) * half, (2 - way) * half)
+                self.held[way, slot, low] = (
+                    value[low] + self.arrived[way, 0, 0:half].astype(f32)
+                ).astype(bf16)
+                self.held[way, slot, rest] = value[rest].astype(bf16)
+            else:
+                self.held[way, slot] = (
+                    value + self.arrived[way, hop - 1].astype(f32)
+                ).astype(bf16)
+            self.copy(way, hop).start()
+
+    def finish(self, term):
+        last = self.ring.far - 1
+        value = term(self.ring.me)
+        for way in (0, 1):
+            self.copy(way, last).wait_recv()
+            value = value + self.arrived[way, last].astype(f32)
+        for hop in range(last - 1, last + 1):
+            for way in (0, 1):
+                self.copy(way, hop).wait_send()
+        return value
+
+
+def gather_first_kernel(
+    small_cut, x_cut, normed_own, cotangent_own, small, x, normed, cotangent,
+    local_sem, swap_send, swap_recv, token_send, token_recv, ring_send, ring_recv,
+):
+    ring = Ring()
+    d, f = ring.me, lax.axis_index("fsdp")
+    greet([{"fsdp": partner(k)} for k in (1, 2, 3)] + [ring.target(0), ring.target(1)])
+    cuts, wholes = [small_cut, x_cut], [small, x]
+    sub = small_cut.shape[1]
+    tokens = normed_own.shape[0]
+    local = [
+        pltpu.make_async_copy(
+            cut.at[f], row_slice(whole, (4 * d + f) * sub, sub), local_sem.at[i]
+        )
+        for i, (cut, whole) in enumerate(zip(cuts, wholes))
+    ] + [
+        pltpu.make_async_copy(own, row_slice(whole, f * tokens, tokens), local_sem.at[2 + i])
+        for i, (own, whole) in enumerate([(normed_own, normed), (cotangent_own, cotangent)])
+    ]
+    swaps = [
+        [
+            pltpu.make_async_remote_copy(
+                cut.at[partner(k)], row_slice(whole, (4 * d + f) * sub, sub),
+                swap_send.at[3 * i + k - 1], swap_recv.at[3 * i + k - 1],
+                device_id={"fsdp": partner(k)}, device_id_type=MESH,
+            )
+            for k in (2, 3, 1)
+        ]
+        for i, (cut, whole) in enumerate(zip(cuts, wholes))
+    ]
+
+    def token_copies(i, own, whole):
+        def one(at, source, owner, k):
+            return pltpu.make_async_remote_copy(
+                source, row_slice(whole, owner * tokens, tokens),
+                token_send.at[3 * i + at], token_recv.at[3 * i + at],
+                device_id={"fsdp": partner(k)}, device_id_type=MESH,
+            )
+
+        far = partner(2)
+        return (
+            one(0, own, f, 2), one(1, own, f, 1),
+            one(2, row_slice(whole, far * tokens, tokens), far, 1),
+        )
+
+    normed_copies = token_copies(0, normed_own, normed)
+    cotangent_copies = token_copies(1, cotangent_own, cotangent)
+    for copy in local:
+        copy.start()
+    for row in swaps:
+        for copy in row:
+            copy.start()
+    for copy in normed_copies[:2]:
+        copy.start()
+    rings = RingGather(ring, wholes, ring_send, ring_recv)
+    for part in (0, 1):
+        local[part].wait()
+        for copy in swaps[part]:
+            copy.wait_recv()
+        rings.start(part, 0)
+    for hop in range(1, ring.far):
+        rings.start(0, hop)
+        rings.start(1, hop)
+        if hop == 1:
+            normed_copies[0].wait_recv()
+            normed_copies[2].start()
+            for copy in cotangent_copies[:2]:
+                copy.start()
+        if hop == ring.far - 1:
+            cotangent_copies[0].wait_recv()
+            cotangent_copies[2].start()
+    rings.finish(0)
+    rings.finish(1)
+    for copy in local[2:]:
+        copy.wait()
+    for copies in (normed_copies, cotangent_copies):
+        for copy in copies[1:]:
+            copy.wait_recv()
+        for copy in copies:
+            copy.wait_send()
+    for row in swaps:
+        for copy in row:
+            copy.wait_send()
+
+
+def any_specs(count):
+    return [pl.BlockSpec(memory_space=pl.ANY)] * count
+
+
+def gather_first(small_cut, x_cut, normed_own, cotangent_own):
+    count, members = lax.axis_size("dp"), lax.axis_size("fsdp")
+    rows = count * members * small_cut.shape[1]
+    tokens = members * normed_own.shape[0]
+    return pl.pallas_call(
+        gather_first_kernel,
+        in_specs=any_specs(4),
+        out_specs=any_specs(4),
+        out_shape=[
+            jax.ShapeDtypeStruct((rows, small_cut.shape[2]), bf16),
+            jax.ShapeDtypeStruct((rows, x_cut.shape[2]), bf16),
+            jax.ShapeDtypeStruct((tokens, D), bf16),
+            jax.ShapeDtypeStruct((tokens, D), bf16),
+        ],
+        scratch_shapes=[
+            pltpu.SemaphoreType.DMA((4,)),
+            pltpu.SemaphoreType.DMA((6,)),
+            pltpu.SemaphoreType.DMA((6,)),
+            pltpu.SemaphoreType.DMA((6,)),
+            pltpu.SemaphoreType.DMA((6,)),
+            RingGather.semaphores(2, count),
+            RingGather.semaphores(2, count),
+        ],
+        compiler_params=pltpu.CompilerParams(collective_id=0, has_side_effects=True),
+        name="gather_first",
+    )(small_cut, x_cut, normed_own, cotangent_own)
+
+
+def scan_gather_kernel(
+    normed_ref, weight_ref, taps_ref, bias_ref, mask_ref, skip_ref, column_ref, row_ref, key_ref,
+    query_ref, key_t_ref, block_ref, gate_cut, out_own,
+    x_ref, y_ref, states_ref, gate_all, out_all,
+    padded, state, local_sem, swap_send, swap_recv, ring_send, ring_recv,
+):
+    ring = Ring()
+    d, f = ring.me, lax.axis_index("fsdp")
+    step = pl.program_id(0)
+    rings = RingGather(ring, [gate_all, out_all], ring_send, ring_recv)
+    sub, rows = gate_cut.shape[1], out_own.shape[0]
+    local = [
+        pltpu.make_async_copy(
+            gate_cut.at[f], row_slice(gate_all, (4 * d + f) * sub, sub), local_sem.at[0]
+        ),
+        pltpu.make_async_copy(out_own, row_slice(out_all, d * rows, rows), local_sem.at[1]),
+    ]
+    swaps = [
+        pltpu.make_async_remote_copy(
+            gate_cut.at[partner(k)], row_slice(gate_all, (4 * d + f) * sub, sub),
+            swap_send.at[k - 1], swap_recv.at[k - 1],
+            device_id={"fsdp": partner(k)}, device_id_type=MESH,
+        )
+        for k in (2, 3, 1)
+    ]
+
+    @pl.when(step == 0)
+    def _():
+        greet([{"fsdp": partner(k)} for k in (1, 2, 3)] + [ring.target(0), ring.target(1)])
+        for copy in local + swaps:
+            copy.start()
+        local[1].wait()
+        rings.start(1, 0)
+        local[0].wait()
+        for copy in swaps:
+            copy.wait_recv()
+        rings.start(0, 0)
+
+    for hop in range(1, ring.far):
+        @pl.when(step == hop)
+        def _(hop=hop):
+            rings.start(1, hop)
+            rings.start(0, hop)
+
+    x_ref[...] = dot_rows(normed_ref[...], weight_ref[...])
+    scan_forward_kernel(
+        x_ref, taps_ref, bias_ref, mask_ref, skip_ref, column_ref, row_ref, key_ref, query_ref,
+        key_t_ref, block_ref, y_ref, states_ref, padded, state,
+    )
+
+    @pl.when(step == pl.num_programs(0) - 1)
+    def _():
+        rings.finish(1)
+        rings.finish(0)
+        for copy in swaps:
+            copy.wait_send()
+
+
+def scan_gather(
+    normed, weight, taps, bias, mask, skip, columns, rows, keys, queries, keys_t, gate_cut, out_own
+):
+    length = normed.shape[0]
+    width = weight.shape[1]
+    chunks = length // SPAN
+    count = lax.axis_size("dp")
+    assert width // LANES == count // 2
+    return pl.pallas_call(
+        scan_gather_kernel,
+        grid=(width // LANES,),
+        in_specs=[whole_spec(), lane_spec(D)] + head_specs(length)[1:] + any_specs(2),
+        out_specs=[
+            lane_spec(length),
+            lane_spec(length),
+            pl.BlockSpec((chunks, STATE, LANES), lambda g: (0, 0, g)),
+        ]
+        + any_specs(2),
+        out_shape=[
+            jax.ShapeDtypeStruct((length, width), f32),
+            jax.ShapeDtypeStruct((length, width), f32),
+            jax.ShapeDtypeStruct((chunks, STATE, width), bf16),
+            jax.ShapeDtypeStruct((D, width), bf16),
+            jax.ShapeDtypeStruct((count * out_own.shape[0], D), bf16),
+        ],
+        scratch_shapes=[
+            pltpu.VMEM((length + 8, LANES), f32),
+            pltpu.VMEM((STATE, LANES), f32),
+            pltpu.SemaphoreType.DMA((2,)),
+            pltpu.SemaphoreType.DMA((3,)),
+            pltpu.SemaphoreType.DMA((3,)),
+            RingGather.semaphores(2, count),
+            RingGather.semaphores(2, count),
+        ],
+        compiler_params=pltpu.CompilerParams(
+            collective_id=1, has_side_effects=True, vmem_limit_bytes=VMEM_BYTES
+        ),
+        name="scan_gather",
+    )(
+        normed, weight, taps, bias, mask, skip, columns, rows, keys, queries, keys_t, block_mask(),
+        gate_cut, out_own,
+    )
+
+
+def scan_scatter_kernel(
+    x_ref, taps_ref, bias_ref, mask_ref, skip_ref, column_ref, row_ref, key_ref, query_ref,
+    query_t_ref, block_ref, pick_ref, grad_ref, states_ref,
+    normed_t_ref, gate_grad_ref, gated_ref, gated_t_ref, cotangent_ref, weight_ref, tokens_ref,
+    x_grad_ref, key_grad_ref, query_grad_ref, sums_ref, rest_ref, channel_ref,
+    gate_raw_ref, out_raw_ref, layer_out_ref,
+    padded, following, state_back, inner_grad, added, added_out, added_in, added_send, added_recv,
+    *ring_scratch,
+):
+    ring = Ring()
+    step = pl.program_id(0)
+    steps = pl.num_programs(0)
+    gate_ring = RingScatter(ring, *ring_scratch[:4])
+    out_ring = RingScatter(ring, *ring_scratch[4:])
+    rows_in, rows_out = gate_raw_ref.shape[0], out_raw_ref.shape[0]
+    tokens = tokens_ref.shape[0]
+
+    def gate_term(owner):
+        here = pl.ds(pl.multiple_of(owner * rows_in, rows_in), rows_in)
+        return dot_rows(normed_t_ref[here, :], gate_grad_ref[...])
+
+    def out_term(owner):
+        here = pl.ds(pl.multiple_of(owner * rows_out, rows_out), rows_out)
+        return dot_rows(gated_t_ref[here, :], cotangent_ref[...])
+
+    def added_block(flip):
+        here = pl.ds(pl.multiple_of(partner(flip) * tokens, tokens), tokens)
+        return dot_rows(gated_ref[here, :], weight_ref[...])
+
+    def added_copy(i):
+        return pltpu.make_async_remote_copy(
+            added_out.at[i], added_in.at[i], added_send.at[i], added_recv.at[i],
+            device_id={"fsdp": partner(2 if i == 2 else 1)}, device_id_type=MESH,
+        )
+
+    @pl.when(step == 0)
+    def _():
+        greet([{"fsdp": partner(k)} for k in (1, 2)] + [ring.target(0), ring.target(1)])
+
+    for hop in range(ring.far):
+        @pl.when(step == hop)
+        def _(hop=hop):
+            out_ring.start(hop, out_term)
+            gate_ring.start(hop, gate_term)
+
+    @pl.when(step == 0)
+    def _():
+        for i, flip in ((1, 3), (0, 1)):
+            added_out[i] = added_block(flip).astype(bf16)
+            added_copy(i).start()
+
+    @pl.when(step == 1)
+    def _():
+        value = added_block(2)
+        added_copy(1).wait_recv()
+        added_out[2] = (value + added_in[1].astype(f32)).astype(bf16)
+        added_copy(2).start()
+
+    @pl.when(step == 2)
+    def _():
+        added[...] = added_block(0)
+
+    scan_backward_kernel(
+        x_ref, taps_ref, bias_ref, mask_ref, skip_ref, column_ref, row_ref, key_ref, query_ref,
+        query_t_ref, block_ref, pick_ref, grad_ref, states_ref,
+        x_grad_ref, key_grad_ref, query_grad_ref, sums_ref, rest_ref, channel_ref,
+        padded, following, state_back, inner_grad,
+    )
+
+    @pl.when(step == steps - 1)
+    def _():
+        added_copy(0).wait_recv()
+        added_copy(2).wait_recv()
+        layer_out_ref[...] = (
+            tokens_ref[...].astype(f32)
+            + ((added[...] + added_in[0].astype(f32)) + added_in[2].astype(f32))
+        ).astype(bf16)
+        for i in range(3):
+            added_copy(i).wait_send()
+        out_raw_ref[...] = out_ring.finish(out_term)
+        gate_raw_ref[...] = gate_ring.finish(gate_term)
+
+
+def scan_scatter(
+    x, taps, bias, mask, skip, columns, rows, keys, queries, queries_t, grad, states,
+    normed_t, gate_grad, gated, gated_t, cotangent, weight, tokens,
+):
+    length, width = x.shape
+    chunks = length // SPAN
+    groups = width // LANES
+    count = lax.axis_size("dp")
+    assert groups == count // 2
+    rows_in, rows_out, own = D // count, width // count, tokens.shape[0]
+    same = lambda g: (0, 0)
+    return pl.pallas_call(
+        scan_scatter_kernel,
+        grid=(groups,),
+        in_specs=head_specs(length)
+        + [
+            whole_spec(),
+            lane_spec(length),
+            pl.BlockSpec((chunks, STATE, LANES), lambda g: (0, 0, g)),
+        ]
+        + [whole_spec()] * 7,
+        out_specs=[
+            lane_spec(length),
+            pl.BlockSpec((length, STATE), same),
+            pl.BlockSpec((length, STATE), same),
+            pl.BlockSpec((length, PAIR), lambda g: (0, g)),
+            pl.BlockSpec((chunks, 1, LANES), lambda g: (0, 0, g)),
+            lane_spec(8),
+        ]
+        + [whole_spec()] * 3,
+        out_shape=[
+            jax.ShapeDtypeStruct((length, width), bf16),
+            jax.ShapeDtypeStruct((length, STATE), f32),
+            jax.ShapeDtypeStruct((length, STATE), f32),
+            jax.ShapeDtypeStruct((length, PAIR * groups), f32),
+            jax.ShapeDtypeStruct((chunks, 1, width), f32),
+            jax.ShapeDtypeStruct((8, width), f32),
+            jax.ShapeDtypeStruct((rows_in, width), f32),
+            jax.ShapeDtypeStruct((rows_out, D), f32),
+            jax.ShapeDtypeStruct((own, D), bf16),
+        ],
+        scratch_shapes=[
+            pltpu.VMEM((length + 8, LANES), f32),
+            pltpu.VMEM((8, LANES), f32),
+            pltpu.VMEM((STATE, LANES), f32),
+            pltpu.VMEM((chunks, SPAN, SPAN), f32),
+            pltpu.VMEM((own, D), f32),
+            pltpu.VMEM((3, own, D), bf16),
+            pltpu.VMEM((3, own, D), bf16),
+            pltpu.SemaphoreType.DMA((3,)),
+            pltpu.SemaphoreType.DMA((3,)),
+        ]
+        + RingScatter.scratch(count, rows_in, width)
+        + RingScatter.scratch(count, rows_out, D),
+        compiler_params=pltpu.CompilerParams(
+            collective_id=2, has_side_effects=True, vmem_limit_bytes=VMEM_BYTES
+        ),
+        name="scan_scatter",
+    )(
+        x, taps, bias, mask, skip, columns, rows, keys, queries, queries_t, block_mask(),
+        pick_masks(), grad, states,
+        normed_t, gate_grad, gated, gated_t, cotangent, weight, tokens,
+    )
+
+
 def unpack(vectors):
     offset = D + INNER
     taps_end = offset + CONV * XBC
@@ -650,7 +1171,7 @@
     rows_in, rows_out = in_weight.shape[0], out_weight.shape[0]
     length = tokens.shape[0] * fsdp
     chunks = length // SPAN
-    out_aligned = rows_out == PAIR
+    in_kernels = uses_ring("dp") and rows_out == PAIR and rows_in % 16 == 0
 
     def own_channels(v):
         lead = v.shape[:-1]
@@ -705,13 +1226,23 @@
         block = exchanged(cut, "fsdp")
         return gather_rows(block.reshape(fsdp * rows_in, cut.shape[2]), "dp")
 
-    weight_shared = gathered(shared_cut)
-    weight_x = gathered(channel_cut(in_low[:, INNER : 2 * INNER]))
-    weight_gate = gathered(channel_cut(in_low[:, :INNER]))
+    inputs = tokens.astype(f32)
+    inverse_in = lax.rsqrt(jnp.mean(inputs * inputs, axis=-1, keepdims=True) + norm_eps)
+    normed_own = (inputs * inverse_in * norm_gain[None, :]).astype(bf16)
+    x_cut = channel_cut(in_low[:, INNER : 2 * INNER])
+    gate_cut = channel_cut(in_low[:, :INNER])
     out_low = out_weight.astype(bf16)
-    if out_aligned:
-        weight_out = gather_rows(out_low, "dp")
+
+    if in_kernels:
+        shared_cut = jnp.pad(shared_cut, ((0, 0), (0, 0), (0, PAIR - shared - heads)))
+        weight_shared, weight_x, normed, cotangents = gather_first(
+            shared_cut, x_cut, normed_own, cotangent
+        )
+        weight_shared = weight_shared[:, : shared + heads]
     else:
+        weight_shared = gathered(shared_cut)
+        weight_x = gathered(x_cut)
+        weight_gate = gathered(gate_cut)
         weight_out = lax.dynamic_index_in_dim(
             lax.all_gather(out_low, ("dp", "fsdp"), axis=0, tiled=True).reshape(
                 pairs, fsdp, PAIR, D
@@ -720,12 +1251,8 @@
             1,
             False,
         ).reshape(inner, D)
-
-    inputs = tokens.astype(f32)
-    inverse_in = lax.rsqrt(jnp.mean(inputs * inputs, axis=-1, keepdims=True) + norm_eps)
-    normed_own = (inputs * inverse_in * norm_gain[None, :]).astype(bf16)
-    normed = spread(normed_own, "fsdp").reshape(length, D)
-    cotangents = spread(cotangent, "fsdp").reshape(length, D)
+        normed = spread(normed_own, "fsdp").reshape(length, D)
+        cotangents = spread(cotangent, "fsdp").reshape(length, D)
 
     small = lax.dot_general(
         weight_shared, normed, (((0,), (1,)), ((), ())), preferred_element_type=f32
@@ -758,10 +1285,14 @@
     ).reshape(length, groups * PAIR)
     head_rows = head_rows.reshape(groups * 2 * GROUP, length)
 
-    x_part = jnp.dot(normed, weight_x, preferred_element_type=f32)
-    y, states = scan_forward(
-        x_part, taps_own, bias_own, mask, skip_own, head_columns, head_rows, keys, queries, keys_t
-    )
+    scan_inputs = (taps_own, bias_own, mask, skip_own, head_columns, head_rows, keys, queries)
+    if in_kernels:
+        x_part, y, states, weight_gate, weight_out = scan_gather(
+            normed, weight_x, *scan_inputs, keys_t, gate_cut, out_low
+        )
+    else:
+        x_part = jnp.dot(normed, weight_x, preferred_element_type=f32)
+        y, states = scan_forward(x_part, *scan_inputs, keys_t)
     gate_part, gated_grad, stats = gate_forward(
         normed, weight_gate, cotangents, weight_out, y, gain_own, mask
     )
@@ -772,38 +1303,40 @@
         y, gate_part, gated_grad, jnp.stack([inverse_out, pull], axis=1), gain_own, mask
     )
 
-    out_term = lax.dot_general(
-        gated_low, cotangents, (((0,), (0,)), ((), ())), preferred_element_type=f32
-    ).astype(bf16)
-    if out_aligned:
-        out_raw = scatter_rows(out_term, "dp")
-    else:
-        whole_term = jnp.zeros((pairs, fsdp, PAIR, D), f32)
-        whole_term = lax.dynamic_update_slice(
-            whole_term, out_term.astype(f32).reshape(pairs, 1, PAIR, D), (0, me, 0, 0)
-        )
-        out_raw = lax.psum_scatter(
-            whole_term.reshape(INNER, D), ("dp", "fsdp"), scatter_dimension=0, tiled=True
-        )
-    added = halved(
-        jnp.dot(gated_low, weight_out, preferred_element_type=f32)
-        .astype(bf16)
-        .reshape(fsdp, tokens.shape[0], D),
-        "fsdp",
-    )
-    layer_out = (inputs + added).astype(bf16)
-
     def in_term(grad):
         return lax.dot_general(
             normed, grad, (((0,), (0,)), ((), ())), preferred_element_type=f32
         ).astype(bf16)
 
-    gate_raw = scatter_rows(in_term(gate_grad), "dp")
-
-    x_grad, key_grad, query_grad, sums, rest, channel_grad = scan_backward(
-        x_part, taps_own, bias_own, mask, skip_own, head_columns, head_rows, keys, queries,
-        queries_t, y_grad, states,
-    )
+    if in_kernels:
+        (
+            x_grad, key_grad, query_grad, sums, rest, channel_grad, gate_raw, out_raw, layer_out,
+        ) = scan_scatter(
+            x_part, *scan_inputs, queries_t, y_grad, states,
+            normed.T, gate_grad, gated_low, gated_low.T, cotangents, weight_out, tokens,
+        )
+    else:
+        out_term = lax.dot_general(
+            gated_low, cotangents, (((0,), (0,)), ((), ())), preferred_element_type=f32
+        )
+        whole_term = jnp.zeros((pairs, fsdp, PAIR, D), f32)
+        whole_term = lax.dynamic_update_slice(
+            whole_term, out_term.reshape(pairs, 1, PAIR, D), (0, me, 0, 0)
+        )
+        out_raw = lax.psum_scatter(
+            whole_term.reshape(INNER, D), ("dp", "fsdp"), scatter_dimension=0, tiled=True
+        )
+        added = halved(
+            jnp.dot(gated_low, weight_out, preferred_element_type=f32)
+            .astype(bf16)
+            .reshape(fsdp, tokens.shape[0], D),
+            "fsdp",
+        )
+        layer_out = (inputs + added).astype(bf16)
+        gate_raw = scatter_rows(in_term(gate_grad), "dp")
+        x_grad, key_grad, query_grad, sums, rest, channel_grad = scan_backward(
+            x_part, *scan_inputs, queries_t, y_grad, states
+        )
     x_raw = scatter_rows(in_term(x_grad), "dp")
 
     shared_grads = jnp.concatenate([key_grad, query_grad], axis=1).T.astype(bf16)
@@ -885,6 +1418,7 @@
             norm_gain_grad.reshape(-1, inner),
         ]
     )
+    vector_rows = jnp.pad(vector_rows, ((0, -vector_rows.shape[0] % 8), (0, 0)))
     vector_rows = spread_small(summed_in_steps(vector_rows, "dp"), "fsdp")
 
     def joined_channels(v):
@@ -910,7 +1444,7 @@
             head_all[:, 3 * heads : 3 * heads + shared].reshape(-1),
         ]
     )
-    norm_rows = vector_rows[:, CONV + 3 :].reshape(fsdp, D)
+    norm_rows = vector_rows[:, CONV + 3 : CONV + 3 + D // inner].reshape(fsdp, D)
     norm_all = norm_rows[0]
     for member in range(1, fsdp):
         norm_all = norm_all + norm_rows[member]

time: 780 us -> 743 us (0.953)
  Pallas kernels: 78.9 us -> 304 us
  waiting for transfers between devices: 209 us -> 41 us
  starting transfers between devices: 121 us -> 53.7 us
  matrix products: 68 us -> 40.7 us
  local copies, waits for them, and re-layouts: 192 us -> 212 us
  other arithmetic: 74.5 us -> 60.6 us
    pallas_call x2 -> x3, Pallas kernels: 54.2 us -> 279 us  [the longest x1 109 us: scan_gather(): pl.pallas_call(scan_gather_kernel, grid=(width // LANES,), in_specs=[whol...]
    ppermute x32 -> x0, waiting for transfers between devices: 79.2 us -> none  [the longest x12 36.2 us: gather_rows(): going_right = lax.ppermute(going_right, axis, right)]
    ppermute x32 -> x0, starting transfers between devices: 39.9 us -> none  [the longest x12 18.2 us: gather_rows(): going_left = lax.ppermute(going_left, axis, left)]
    ppermute x55 -> x37, waiting for transfers between devices: 58.5 us -> 24.7 us  [swapped(): return lax.ppermute(value, axis, [(i, i ^ flip) for i in range(count)])]
    ppermute x12 -> x6, waiting for transfers between devices: 35.4 us -> 2.12 us  [scatter_rows(): going_left = lax.ppermute(to_left.astype(bf16), axis, left)]
    dynamic_update_slice x38 -> x20, local copies, waits for them, and re-layouts: 79.9 us -> 104 us  [placed(): lax.dynamic_update_index_in_dim(whole, part, lax.bitwise_xor(me, flip), 0)]
    dot_general x3 -> x0, matrix products: 22.9 us -> none  [the longest x1 8.58 us: on_device(): lax.dot_general(gated_low, cotangents, (((0,), (0,)), ((), ())), preferre...]
    ppermute x12 -> x6, waiting for transfers between devices: 34.2 us -> 12.8 us  [scatter_rows(): going_right = lax.ppermute(to_right.astype(bf16), axis, right)]
  transfers between devices with their start and end apart: 119 -> 53, of which waited for: 48 -> 12; matrix products, arithmetic and copies ran while one was open for 33% -> 33% of each run, Pallas kernels for 0% -> 0%
where the time goes in v2:
time: 743 us; the launch traced here: 730 us
  Pallas kernels  304 us (41%)
  local copies, waits for them, and re-layouts  212 us (29%)
  other arithmetic  60.6 us (8%)
  starting transfers between devices  53.7 us (7%)
  waiting for transfers between devices  41 us (6%)
  matrix products  40.7 us (5%)
  between operations  18.7 us (3%)
    pallas_call x1, Pallas kernels, scan_gather(): pl.pallas_call(scan_gather_kernel, grid=(width // LANES,), in_specs=[whol...  109 us
    dynamic_update_slice x20, local copies, waits for them, and re-layouts, placed(): lax.dynamic_update_index_in_dim(whole, part, lax.bitwise_xor(me, flip), 0)  104 us
    pallas_call x1, Pallas kernels, scan_scatter(): pl.pallas_call(scan_scatter_kernel, grid=(groups,), in_specs=head_specs(l...  96.3 us
    pallas_call x1, Pallas kernels, gather_first(): pl.pallas_call(gather_first_kernel, in_specs=any_specs(4), out_specs=any_...  73 us
    ppermute x37, starting transfers between devices, swapped(): return lax.ppermute(value, axis, [(i, i ^ flip) for i in range(count)])  35.9 us
    dot_general x3, matrix products, in_back(): lax.dot_general(grad, weight, (((grad_dim,), (1,)), ((), ())), preferred_...  26.8 us
    ppermute x37, waiting for transfers between devices, swapped(): return lax.ppermute(value, axis, [(i, i ^ flip) for i in range(count)])  24.7 us
    broadcast_in_dim x7, local copies, waits for them, and re-layouts, placed(): lax.dynamic_update_index_in_dim(whole, part, lax.bitwise_xor(me, flip), 0)  19.4 us
  transfers between devices with their start and end apart: 53, of which 12 were waited for; matrix products, arithmetic and copies ran while one was open for 33% of the time, Pallas kernels for 0%

profile of v2, /device:TPU:0, one launch (start us, length us, event | category | flops | bytes accessed | tf_op | source)
XLA Modules:
  0.0 730.2 jit_solution(669278860951097960)
XLA Ops:
  10.9 73.0 %gather_first.1 = (bf16[2048,128]{1,0:T(8,128)(2,1)}, bf16[2048,1024]{1,0:T(8,128)(2,1)}, bf16[1024,2048]{1,0:T(8,128)(2,1)}, bf16[1024,2048]{1,0:T(8,128)(2,1)}) custom-call(bf16[4,64,128]{2,1,0:T(8,128)(2,1)} %fusion.34.small_cut, bf16[4,64,1024]{2,1,0:T(8,128)(2,1)} %reshape.629.x_cut, bf16[256,2048]{1,0:T(8,128)(2,1)} %fusion.3.normed_own, ...), custom_call_target="tpu_custom_call" | custom-call | tf_op jit(solution)/shard_map/gather_first/pallas_call | solution.py:852
  84.0 3.8 fusion.20
  97.9 6.4 copy.175
  118.9 109.4 %scan_gather.1 = (f32[1024,1024]{1,0:T(8,128)}, f32[1024,1024]{1,0:T(8,128)}, bf16[8,128,1024]{2,1,0:T(8,128)(2,1)}, bf16[2048,1024]{1,0:T(8,128)(2,1)}, bf16[1024,2048]{1,0:T(8,128)(2,1)}) custom-call(bf16[1024,2048]{1,0:T(8,128)(2,1)} %get-tuple-element.42.normed_ref, bf16[2048,1024]{1,0:T(8,128)(2,1)} %get-tuple-element.43.weight_ref, ...), custom_call_target="tpu_custom_call" | custom-call | tf_op jit(solution)/shard_map/scan_gather/pallas_call | solution.py:942
  228.3 16.1 %gate_forward.1 = (f32[1024,1024]{1,0:T(8,128)}, f32[1024,1024]{1,0:T(8,128)}, f32[1024,128]{1,0:T(8,128)}) custom-call(bf16[1024,2048]{1,0:T(8,128)(2,1)} %get-tuple-element.42.normed_ref, bf16[2048,1024]{1,0:T(8,128)(2,1)} %get-tuple-element.47.weight_ref, bf16[1024,2048]{1,0:T(8,128)(2,1)} %get-tuple-element.48.cotangent_ref, ...), custom_call_target="tpu_custom_call" | custom-call | flops 8999999488 | bytes 28000000 | tf_op jit(solution)/shard_map/gate_forward/pallas_call | solution.py:537
  260.3 10.3 %collective-permute-done.5 = f32[2,1024]{0,1:T(8,128)S(1)} collective-permute-done((f32[2,1024]{0,1:T(8,128)S(1)}, f32[2,1024]{0,1:T(8,128)S(1)}, u32[]{:S(2)}, u32[]{:S(2)}) %collective-permute-start.5) | collective-permute-done | bytes 8224 | tf_op jit(solution)/shard_map/ppermute | solution.py:126
  273.4 8.9 %norm_back.1 = (bf16[1024,1024]{1,0:T(8,128)(2,1)}, bf16[1024,1024]{1,0:T(8,128)(2,1)}, bf16[1024,1024]{1,0:T(8,128)(2,1)}, f32[8,1024]{1,0:T(8,128)}) custom-call(f32[1024,1024]{1,0:T(8,128)} %get-tuple-element.46.y_ref, f32[1024,1024]{1,0:T(8,128)} %get-tuple-element.50.gate_part_ref, f32[1024,1024]{1,0:T(8,128)} %get-tuple-element.51.gated_grad_ref, ...), custom_call_target="tpu_custom_call" | custom-call | flops 30000000 | bytes 18000000 | tf_op jit(solution)/shard_map/norm_back/pallas_call | solution.py:584
  282.3 4.1 copy.176
  286.4 9.0 %fusion.85 = f32[1024,2048]{1,0:T(8,128)} fusion(bf16[1024,1024]{1,0:T(8,128)(2,1)S(1)} %copy-done.14, bf16[2048,1024]{1,0:T(8,128)(2,1)} %get-tuple-element.47.weight_ref), kind=kOutput, calls=%fused_computation.247 | convolution fusion | flops 4294967296 | bytes 14680064 | tf_op jit(solution)/shard_map/dot_general | solution.py:1385
  295.4 96.3 %scan_scatter.1 = (bf16[1024,1024]{1,0:T(8,128)(2,1)}, f32[1024,128]{1,0:T(8,128)}, f32[1024,128]{1,0:T(8,128)}, f32[1024,512]{1,0:T(8,128)}, f32[8,1,1024]{2,1,...) custom-call(f32[1024,1024]{1,0:T(8,128)} %get-tuple-element.45.x_ref, ...), custom_call_target="tpu_custom_call" | custom-call | tf_op jit(solution)/shard_map/scan_scatter/pallas_call | solution.py:1072
  391.7 10.8 %fusion.86 = f32[1024,2048]{1,0:T(8,128)} fusion(bf16[1024,1024]{1,0:T(8,128)(2,1)} %get-tuple-element.58, bf16[2048,1024]{1,0:T(8,128)(2,1)} %get-tuple-element.43.weight_ref), kind=kOutput, calls=%fused_computation.248 | convolution fusion | flops 4294967296 | bytes 14680064 | tf_op jit(solution)/shard_map/dot_general | solution.py:1385
  402.5 6.3 convolution_convert_fusion
  453.4 7.1 add_convert_fusion
  482.4 5.3 collective-permute-done.16
  497.1 4.0 collective-permute-done.17
  512.8 5.5 collective-permute-done.35
  522.8 3.8 fusion.9
  527.9 7.6 %collective-permute-done.47 = f32[16,1024]{1,0:T(8,128)S(1)} collective-permute-done((f32[16,1024]{1,0:T(8,128)S(1)}, f32[16,1024]{1,0:T(8,128)S(1)}, u32[]{:S(2)}, u32[]{:S(2)}) %collective-permute-start.47) | collective-permute-done | bytes 65568 | tf_op jit(solution)/shard_map/ppermute | solution.py:126
  543.2 4.0 collective-permute-start.49
  549.5 4.3 fusion.7
  567.4 5.0 copy.194
  572.3 4.1 broadcast_in_dim.125
  576.5 21.1 %dynamic_update_slice.95 = f32[4,16,1024]{0,2,1:T(8,128)} dynamic-update-slice(f32[4,16,1024]{0,2,1:T(8,128)} %broadcast_in_dim.125, f32[1,16,1024]{0,2,1:T(8,128)} %copy.194, s32[]{:T(128)S(6)} %select_n.226, s32[]{:T(128)} %constant.320.clone.1, s32[]{:T(128)} %constant.320.clone.1) | dynamic-update-slice | bytes 131076 | tf_op jit(solution)/shard_map/jit(dynamic_update_index_in_dim)/dynamic_update_slice | solution.py:152
  597.6 4.9 collective-permute-start.25
  602.5 4.7 copy.195
  607.2 4.7 copy.196
  611.9 4.7 copy.197
  616.6 24.3 %dynamic_update_slice.96 = f32[4,16,1024]{0,2,1:T(8,128)} dynamic-update-slice(f32[4,16,1024]{0,2,1:T(8,128)} %dynamic_update_slice.95, f32[1,16,1024]{0,2,1:T(8,128)} %copy.195, s32[]{:T(128)S(6)} %select_n.230, s32[]{:T(128)} %constant.320.clone.1, s32[]{:T(128)} %constant.320.clone.1) | dynamic-update-slice | bytes 131076 | tf_op jit(solution)/shard_map/jit(dynamic_update_index_in_dim)/dynamic_update_slice | solution.py:152
  640.9 24.3 %dynamic_update_slice.97 = f32[4,16,1024]{0,2,1:T(8,128)} dynamic-update-slice(f32[4,16,1024]{0,2,1:T(8,128)} %dynamic_update_slice.96, f32[1,16,1024]{0,2,1:T(8,128)} %copy.196, s32[]{:T(128)S(6)} %select_n.231, s32[]{:T(128)} %constant.320.clone.1, s32[]{:T(128)} %constant.320.clone.1) | dynamic-update-slice | bytes 131076 | tf_op jit(solution)/shard_map/jit(dynamic_update_index_in_dim)/dynamic_update_slice | solution.py:152
  665.3 24.3 %dynamic_update_slice.98 = f32[4,16,1024]{0,2,1:T(8,128)} dynamic-update-slice(f32[4,16,1024]{0,2,1:T(8,128)} %dynamic_update_slice.97, f32[1,16,1024]{0,2,1:T(8,128)} %copy.197, s32[]{:T(128)S(6)} %select_n.232, s32[]{:T(128)} %constant.320.clone.1, s32[]{:T(128)} %constant.320.clone.1) | dynamic-update-slice | bytes 131076 | tf_op jit(solution)/shard_map/jit(dynamic_update_index_in_dim)/dynamic_update_slice | solution.py:152
  717.7 4.4 fusion.69
  722.8 4.8 fusion.71
  (439 shorter events, 184.2 us)
Async XLA Ops:
  89.2 25.1 %collective-permute-start = (bf16[64,1024]{1,0:T(8,128)(2,1)}, bf16[64,1024]{1,0:T(8,128)(2,1)}, u32[]{:S(2)}, u32[]{:S(2)}) collective-permute-start(bf16[64,1024]{1,0:T(8,128)(2,1)} %get-tuple-element.94), channel_id=1, source_target_pairs={{0,1},{1,0},{2,3},{3,2},{4,5},{5,4},{6,7},{7,6},{8,9},{9,8},{10,11... | collective-permute-start | bytes 393224 | tf_op jit(solution)/shard_map/ppermute | solution.py:126
  89.3 26.0 %collective-permute-start.1 = (bf16[64,1024]{1,0:T(8,128)(2,1)}, bf16[64,1024]{1,0:T(8,128)(2,1)}, u32[]{:S(2)}, u32[]{:S(2)}) collective-permute-start(bf16[64,1024]{1,0:T(8,128)(2,1)} %get-tuple-element.94), channel_id=1, source_target_pairs={{0,2},{1,3},{2,0},{3,1},{4,6},{5,7},{6,4},{7,5},{8,10},{9,11},{10,... | collective-permute-start | bytes 393224 | tf_op jit(solution)/shard_map/ppermute | solution.py:126
  90.7 25.5 %collective-permute-start.2 = (bf16[64,1024]{1,0:T(8,128)(2,1)}, bf16[64,1024]{1,0:T(8,128)(2,1)}, u32[]{:S(2)}, u32[]{:S(2)}) collective-permute-start(bf16[64,1024]{1,0:T(8,128)(2,1)} %get-tuple-element.94), channel_id=1, source_target_pairs={{0,3},{1,2},{2,1},{3,0},{4,7},{5,6},{6,5},{7,4},{8,11},{9,10},{10,... | collective-permute-start | bytes 393224 | tf_op jit(solution)/shard_map/ppermute | solution.py:126
  245.5 13.7 %collective-permute-start.3 = (f32[2,1024]{0,1:T(8,128)S(1)}, f32[2,1024]{0,1:T(8,128)S(1)}, u32[]{:S(2)}, u32[]{:S(2)}) collective-permute-start(f32[2,1024]{0,1:T(8,128)S(1)} %slice_bitcast_fusion.1), channel_id=1, source_target_pairs={{0,1},{1,0},{2,3},{3,2},{4,5},{5,4},{6,7},{7,6},{8,9},{9,8},{10,11... | collective-permute-start | bytes 24584 | tf_op jit(solution)/shard_map/ppermute | solution.py:126
  245.6 14.8 %collective-permute-start.4 = (f32[2,1024]{0,1:T(8,128)S(1)}, f32[2,1024]{0,1:T(8,128)S(1)}, u32[]{:S(2)}, u32[]{:S(2)}) collective-permute-start(f32[2,1024]{0,1:T(8,128)S(1)} %slice_bitcast_fusion.1), channel_id=1, source_target_pairs={{0,2},{1,3},{2,0},{3,1},{4,6},{5,7},{6,4},{7,5},{8,10},{9,11},{10,... | collective-permute-start | bytes 24584 | tf_op jit(solution)/shard_map/ppermute | solution.py:126
  247.1 23.6 %collective-permute-start.5 = (f32[2,1024]{0,1:T(8,128)S(1)}, f32[2,1024]{0,1:T(8,128)S(1)}, u32[]{:S(2)}, u32[]{:S(2)}) collective-permute-start(f32[2,1024]{0,1:T(8,128)S(1)} %slice_bitcast_fusion.1), channel_id=1, source_target_pairs={{0,3},{1,2},{2,1},{3,0},{4,7},{5,6},{6,5},{7,4},{8,11},{9,10},{10,... | collective-permute-start | bytes 24584 | tf_op jit(solution)/shard_map/ppermute | solution.py:126
  410.0 35.1 %collective-permute-start.6 = (bf16[64,1024]{1,0:T(8,128)(2,1)}, bf16[64,1024]{1,0:T(8,128)(2,1)}, u32[]{:S(2)}, u32[]{:S(2)}) collective-permute-start(bf16[64,1024]{1,0:T(8,128)(2,1)} %get-tuple-element.134), channel_id=1, source_target_pairs={{0,1},{1,0},{2,3},{3,2},{4,5},{5,4},{6,7},{7,6},{8,9},{9,8},{10,11... | collective-permute-start | bytes 393224 | tf_op jit(solution)/shard_map/ppermute | solution.py:126
  410.0 36.2 %collective-permute-start.7 = (bf16[64,1024]{1,0:T(8,128)(2,1)}, bf16[64,1024]{1,0:T(8,128)(2,1)}, u32[]{:S(2)}, u32[]{:S(2)}) collective-permute-start(bf16[64,1024]{1,0:T(8,128)(2,1)} %get-tuple-element.133), channel_id=1, source_target_pairs={{0,2},{1,3},{2,0},{3,1},{4,6},{5,7},{6,4},{7,5},{8,10},{9,11},{10,... | collective-permute-start | bytes 393224 | tf_op jit(solution)/shard_map/ppermute | solution.py:126
  410.5 37.2 %collective-permute-start.8 = (bf16[64,1024]{1,0:T(8,128)(2,1)}, bf16[64,1024]{1,0:T(8,128)(2,1)}, u32[]{:S(2)}, u32[]{:S(2)}) collective-permute-start(bf16[64,1024]{1,0:T(8,128)(2,1)} %get-tuple-element.132), channel_id=1, source_target_pairs={{0,3},{1,2},{2,1},{3,0},{4,7},{5,6},{6,5},{7,4},{8,11},{9,10},{10,... | collective-permute-start | bytes 393224 | tf_op jit(solution)/shard_map/ppermute | solution.py:126
  441.5 31.3 %collective-permute-start.15 = (bf16[128,1024]{1,0:T(8,128)(2,1)}, bf16[128,1024]{1,0:T(8,128)(2,1)S(1)}, u32[]{:S(2)}, u32[]{:S(2)}) collective-permute-start(bf16[128,1024]{1,0:T(8,128)(2,1)} %get-tuple-element.111), channel_id=1, source_target_pairs={{0,8},{8,16},{16,24},{24,28},{28,20},{20,12},{12,4},{4,0},{1,9},{9... | collective-permute-start | bytes 786440 | tf_op jit(solution)/shard_map/ppermute | solution.py:110
  442.1 31.4 %collective-permute-start.19 = (bf16[128,1024]{1,0:T(8,128)(2,1)}, bf16[128,1024]{1,0:T(8,128)(2,1)S(1)}, u32[]{:S(2)}, u32[]{:S(2)}) collective-permute-start(bf16[128,1024]{1,0:T(8,128)(2,1)} %get-tuple-element.113), channel_id=1, source_target_pairs={{8,0},{16,8},{24,16},{28,24},{20,28},{12,20},{4,12},{0,4},{9,1},{1... | collective-permute-start | bytes 786440 | tf_op jit(solution)/shard_map/ppermute | solution.py:111
  445.1 16.7 %collective-permute-start.12 = (bf16[64,1024]{1,0:T(8,128)(2,1)S(1)}, bf16[64,1024]{1,0:T(8,128)(2,1)S(1)}, u32[]{:S(2)}, u32[]{:S(2)}) collective-permute-start(bf16[64,1024]{1,0:T(8,128)(2,1)S(1)} %get-tuple-element.123), channel_id=1, source_target_pairs={{0,1},{1,0},{2,3},{3,2},{4,5},{5,4},{6,7},{7,6},{8,9},{9,8},{10,11... | collective-permute-start | bytes 393224 | tf_op jit(solution)/shard_map/ppermute | solution.py:126
  446.3 16.5 %collective-permute-start.13 = (bf16[64,1024]{1,0:T(8,128)(2,1)S(1)}, bf16[64,1024]{1,0:T(8,128)(2,1)S(1)}, u32[]{:S(2)}, u32[]{:S(2)}) collective-permute-start(bf16[64,1024]{1,0:T(8,128)(2,1)S(1)} %get-tuple-element.122), channel_id=1, source_target_pairs={{0,2},{1,3},{2,0},{3,1},{4,6},{5,7},{6,4},{7,5},{8,10},{9,11},{10,... | collective-permute-start | bytes 393224 | tf_op jit(solution)/shard_map/ppermute | solution.py:126
  447.8 15.6 %collective-permute-start.14 = (bf16[64,1024]{1,0:T(8,128)(2,1)S(1)}, bf16[64,1024]{1,0:T(8,128)(2,1)S(1)}, u32[]{:S(2)}, u32[]{:S(2)}) collective-permute-start(bf16[64,1024]{1,0:T(8,128)(2,1)S(1)} %get-tuple-element.121), channel_id=1, source_target_pairs={{0,3},{1,2},{2,1},{3,0},{4,7},{5,6},{6,5},{7,4},{8,11},{9,10},{10,... | collective-permute-start | bytes 393224 | tf_op jit(solution)/shard_map/ppermute | solution.py:126
  461.8 31.1 %collective-permute-start.10 = (bf16[256,2048]{1,0:T(8,128)(2,1)S(1)}, bf16[256,2048]{1,0:T(8,128)(2,1)}, u32[]{:S(2)}, u32[]{:S(2)}) collective-permute-start(bf16[256,2048]{1,0:T(8,128)(2,1)S(1)} %get-tuple-element.116), channel_id=1, source_target_pairs={{0,1},{1,0},{2,3},{3,2},{4,5},{5,4},{6,7},{7,6},{8,9},{9,8},{10,11... | collective-permute-start | bytes 3145736 | tf_op jit(solution)/shard_map/ppermute | solution.py:126
  466.6 56.2 %collective-permute-start.9 = (bf16[256,2048]{1,0:T(8,128)(2,1)}, bf16[256,2048]{1,0:T(8,128)(2,1)}, u32[]{:S(2)}, u32[]{:S(2)}) collective-permute-start(bf16[256,2048]{1,0:T(8,128)(2,1)} %get-tuple-element.115), channel_id=1, source_target_pairs={{0,1},{1,0},{2,3},{3,2},{4,5},{5,4},{6,7},{7,6},{8,9},{9,8},{10,11... | collective-permute-start | bytes 3145736 | tf_op jit(solution)/shard_map/ppermute | solution.py:126
  474.7 12.9 %collective-permute-start.16 = (bf16[256,1024]{1,0:T(8,128)(2,1)S(1)}, bf16[256,1024]{1,0:T(8,128)(2,1)S(1)}, u32[]{:S(2)}, u32[]{:S(2)}) collective-permute-start(bf16[256,1024]{1,0:T(8,128)(2,1)S(1)} %pad_maximum_fusion), channel_id=1, source_target_pairs={{0,8},{8,16},{16,24},{24,28},{28,20},{20,12},{12,4},{4,0},{1,9},{9... | collective-permute-start | bytes 1572872 | tf_op jit(solution)/shard_map/ppermute | solution.py:119
  477.9 12.4 %collective-permute-start.29 = (bf16[256,80]{0,1:T(8,128)(2,1)S(1)}, bf16[256,80]{0,1:T(8,128)(2,1)S(1)}, u32[]{:S(2)}, u32[]{:S(2)}) collective-permute-start(bf16[256,80]{0,1:T(8,128)(2,1)S(1)} %get-tuple-element.140), channel_id=1, source_target_pairs={{0,8},{8,16},{16,24},{24,28},{28,20},{20,12},{12,4},{4,0},{1,9},{9... | collective-permute-start | bytes 122888 | tf_op jit(solution)/shard_map/ppermute | solution.py:119
  481.9 15.2 %collective-permute-start.20 = (bf16[256,1024]{1,0:T(8,128)(2,1)}, bf16[256,1024]{1,0:T(8,128)(2,1)}, u32[]{:S(2)}, u32[]{:S(2)}) collective-permute-start(bf16[256,1024]{1,0:T(8,128)(2,1)} %pad_maximum_fusion.1), channel_id=1, source_target_pairs={{8,0},{16,8},{24,16},{28,24},{20,28},{12,20},{4,12},{0,4},{9,1},{1... | collective-permute-start | bytes 1572872 | tf_op jit(solution)/shard_map/ppermute | solution.py:120
  490.3 10.8 %collective-permute-start.17 = (bf16[256,1024]{1,0:T(8,128)(2,1)}, bf16[256,1024]{1,0:T(8,128)(2,1)}, u32[]{:S(2)}, u32[]{:S(2)}) collective-permute-start(bf16[256,1024]{1,0:T(8,128)(2,1)} %add_convert_fusion.4), channel_id=1, source_target_pairs={{0,8},{8,16},{16,24},{24,28},{28,20},{20,12},{12,4},{4,0},{1,9},{9... | collective-permute-start | bytes 1572872 | tf_op jit(solution)/shard_map/ppermute | solution.py:119
  495.9 26.9 %collective-permute-start.11 = (bf16[256,2048]{1,0:T(8,128)(2,1)}, bf16[256,2048]{1,0:T(8,128)(2,1)}, u32[]{:S(2)}, u32[]{:S(2)}) collective-permute-start(bf16[256,2048]{1,0:T(8,128)(2,1)} %fusion.10), channel_id=1, source_target_pairs={{0,2},{1,3},{2,0},{3,1},{4,6},{5,7},{6,4},{7,5},{8,10},{9,11},{10,... | collective-permute-start | bytes 3145736 | tf_op jit(solution)/shard_map/ppermute | solution.py:126
  504.0 14.9 %collective-permute-start.21 = (bf16[256,1024]{1,0:T(8,128)(2,1)}, bf16[256,1024]{1,0:T(8,128)(2,1)}, u32[]{:S(2)}, u32[]{:S(2)}) collective-permute-start(bf16[256,1024]{1,0:T(8,128)(2,1)} %get-tuple-element.108), channel_id=1, source_target_pairs={{8,0},{16,8},{24,16},{28,24},{20,28},{12,20},{4,12},{0,4},{9,1},{1... | collective-permute-start | bytes 1572872 | tf_op jit(solution)/shard_map/ppermute | solution.py:120
  518.5 17.1 %collective-permute-start.18 = (bf16[256,1024]{1,0:T(8,128)(2,1)}, bf16[256,1024]{1,0:T(8,128)(2,1)}, u32[]{:S(2)}, u32[]{:S(2)}) collective-permute-start(bf16[256,1024]{1,0:T(8,128)(2,1)} %get-tuple-element.107), channel_id=1, source_target_pairs={{0,8},{8,16},{16,24},{24,28},{28,20},{20,12},{12,4},{4,0},{1,9},{9... | collective-permute-start | bytes 1572872 | tf_op jit(solution)/shard_map/ppermute | solution.py:119
  521.1 14.5 %collective-permute-start.22 = (bf16[256,1024]{1,0:T(8,128)(2,1)}, bf16[256,1024]{1,0:T(8,128)(2,1)}, u32[]{:S(2)}, u32[]{:S(2)}) collective-permute-start(bf16[256,1024]{1,0:T(8,128)(2,1)} %add_convert_fusion.1), channel_id=1, source_target_pairs={{8,0},{16,8},{24,16},{28,24},{20,28},{12,20},{4,12},{0,4},{9,1},{1... | collective-permute-start | bytes 1572872 | tf_op jit(solution)/shard_map/ppermute | solution.py:120
  543.2 17.2 %collective-permute-start.49 = (f32[16,1024]{1,0:T(8,128)S(1)}, f32[16,1024]{1,0:T(8,128)S(1)}, u32[]{:S(2)}, u32[]{:S(2)}) collective-permute-start(f32[16,1024]{1,0:T(8,128)S(1)} %add.787), channel_id=1, source_target_pairs={{0,16},{4,20},{8,24},{12,28},{16,0},{20,4},{24,8},{28,12},{1,17},{... | collective-permute-start | bytes 196616 | tf_op jit(solution)/shard_map/ppermute | solution.py:126
  553.9 10.6 %collective-permute-start.42 = (f32[8,128]{1,0:T(8,128)S(1)}, f32[8,128]{1,0:T(8,128)S(1)}, u32[]{:S(2)}, u32[]{:S(2)}) collective-permute-start(f32[8,128]{1,0:T(8,128)S(1)} %add_add_fusion.3), channel_id=1, source_target_pairs={{0,12},{4,8},{8,4},{12,0},{16,28},{20,24},{24,20},{28,16},{1,13},{... | collective-permute-start | bytes 12296 | tf_op jit(solution)/shard_map/ppermute | solution.py:126
  564.5 145.3 %collective-permute-start.23 = (bf16[64,1024]{1,0:T(8,128)(2,1)}, bf16[64,1024]{1,0:T(8,128)(2,1)S(1)}, u32[]{:S(2)}, u32[]{:S(2)}) collective-permute-start(bf16[64,1024]{1,0:T(8,128)(2,1)} %get-tuple-element.127), channel_id=1, source_target_pairs={{0,1},{1,0},{2,3},{3,2},{4,5},{5,4},{6,7},{7,6},{8,9},{9,8},{10,11... | collective-permute-start | bytes 393224 | tf_op jit(solution)/shard_map/ppermute | solution.py:126
  564.5 145.9 %collective-permute-start.24 = (bf16[64,1024]{1,0:T(8,128)(2,1)}, bf16[64,1024]{1,0:T(8,128)(2,1)}, u32[]{:S(2)}, u32[]{:S(2)}) collective-permute-start(bf16[64,1024]{1,0:T(8,128)(2,1)} %get-tuple-element.126), channel_id=1, source_target_pairs={{0,2},{1,3},{2,0},{3,1},{4,6},{5,7},{6,4},{7,5},{8,10},{9,11},{10,... | collective-permute-start | bytes 393224 | tf_op jit(solution)/shard_map/ppermute | solution.py:126
  564.9 32.7 %collective-permute-start.50 = (f32[16,1024]{1,0:T(8,128)S(1)}, f32[16,1024]{1,0:T(8,128)S(1)}, u32[]{:S(2)}, u32[]{:S(2)}) collective-permute-start(f32[16,1024]{1,0:T(8,128)S(1)} %add.788), channel_id=1, source_target_pairs={{0,1},{1,0},{2,3},{3,2},{4,5},{5,4},{6,7},{7,6},{8,9},{9,8},{10,11... | collective-permute-start | bytes 196616 | tf_op jit(solution)/shard_map/ppermute | solution.py:126
  565.1 42.1 %collective-permute-start.51 = (f32[16,1024]{1,0:T(8,128)S(1)}, f32[16,1024]{1,0:T(8,128)S(1)}, u32[]{:S(2)}, u32[]{:S(2)}) collective-permute-start(f32[16,1024]{1,0:T(8,128)S(1)} %add.788), channel_id=1, source_target_pairs={{0,2},{1,3},{2,0},{3,1},{4,6},{5,7},{6,4},{7,5},{8,10},{9,11},{10,... | collective-permute-start | bytes 196616 | tf_op jit(solution)/shard_map/ppermute | solution.py:126
  566.8 45.1 %collective-permute-start.52 = (f32[16,1024]{1,0:T(8,128)S(1)}, f32[16,1024]{1,0:T(8,128)S(1)}, u32[]{:S(2)}, u32[]{:S(2)}) collective-permute-start(f32[16,1024]{1,0:T(8,128)S(1)} %add.788), channel_id=1, source_target_pairs={{0,3},{1,2},{2,1},{3,0},{4,7},{5,6},{6,5},{7,4},{8,11},{9,10},{10,... | collective-permute-start | bytes 196616 | tf_op jit(solution)/shard_map/ppermute | solution.py:126
  597.6 114.5 %collective-permute-start.25 = (bf16[64,1024]{1,0:T(8,128)(2,1)}, bf16[64,1024]{1,0:T(8,128)(2,1)}, u32[]{:S(2)}, u32[]{:S(2)}) collective-permute-start(bf16[64,1024]{1,0:T(8,128)(2,1)} %get-tuple-element.125), channel_id=1, source_target_pairs={{0,3},{1,2},{2,1},{3,0},{4,7},{5,6},{6,5},{7,4},{8,11},{9,10},{10,... | collective-permute-start | bytes 393224 | tf_op jit(solution)/shard_map/ppermute | solution.py:126
  (87 other events, 799.4 us)

commit v3 on v2

--- a/solution.py
+++ b/solution.py
@@ -307,6 +307,7 @@
         key_grad_ref[...] = jnp.zeros_like(key_grad_ref)
         query_grad_ref[...] = jnp.zeros_like(query_grad_ref)
         inner_grad[...] = jnp.zeros_like(inner_grad)
+        sums_ref[...] = jnp.zeros_like(sums_ref)
 
     taps, bias, skip = taps_ref[...], bias_ref[...], skip_ref[...]
     row_at = lax.broadcasted_iota(jnp.int32, (rows, rows), 0)
@@ -366,7 +367,7 @@
         first = grad * y - weighted_low.astype(f32) * inside
         first_high = first.astype(bf16)
         first_rest = (first - first_high.astype(f32)).astype(bf16)
-        sums_ref[here, :] = (
+        sums_ref[here, :] = sums_ref[here, :] + (
             dot_rows(first_high, pick_ref[0])
             + dot_rows(first_rest, pick_ref[0])
             + dot_rows((weighted * outside).astype(bf16), pick_ref[1])
@@ -413,10 +414,16 @@
     return (row == lane).astype(bf16)
 
 
-def pick_masks():
+def pick_masks(groups):
     lane = jnp.arange(LANES)[:, None] // HEAD_DIM
     target = jnp.arange(PAIR)[None, :]
-    return jnp.stack([(target == lane + GROUP * kind).astype(bf16) for kind in range(3)])
+    return jnp.stack(
+        [
+            (target == (kind * groups + group) * GROUP + lane).astype(bf16)
+            for group in range(groups)
+            for kind in range(3)
+        ]
+    )
 
 
 def whole_spec():
@@ -479,7 +486,7 @@
         grid=(groups,),
         in_specs=head_specs(length)
         + [
-            whole_spec(),
+            pl.BlockSpec((3, LANES, PAIR), lambda g: (g, 0, 0)),
             lane_spec(length),
             pl.BlockSpec((chunks, STATE, LANES), lambda g: (0, 0, g)),
         ],
@@ -487,7 +494,7 @@
             lane_spec(length),
             pl.BlockSpec((length, STATE), same),
             pl.BlockSpec((length, STATE), same),
-            pl.BlockSpec((length, PAIR), lambda g: (0, g)),
+            pl.BlockSpec((length, PAIR), same),
             pl.BlockSpec((chunks, 1, LANES), lambda g: (0, 0, g)),
             lane_spec(8),
         ],
@@ -495,7 +502,7 @@
             jax.ShapeDtypeStruct((length, width), bf16),
             jax.ShapeDtypeStruct((length, STATE), f32),
             jax.ShapeDtypeStruct((length, STATE), f32),
-            jax.ShapeDtypeStruct((length, PAIR * groups), f32),
+            jax.ShapeDtypeStruct((length, PAIR), f32),
             jax.ShapeDtypeStruct((chunks, 1, width), f32),
             jax.ShapeDtypeStruct((8, width), f32),
         ],
@@ -512,7 +519,7 @@
         name="scan_backward",
     )(
         x, taps, bias, mask, skip, columns, rows, keys, queries, queries_t, block_mask(),
-        pick_masks(), grad, states,
+        pick_masks(groups), grad, states,
     )
 
 
@@ -975,12 +982,16 @@
     )
 
 
+def total_squares(value):
+    return jnp.sum(jnp.sum(value * value, axis=0, keepdims=True), axis=1, keepdims=True)
+
+
 def scan_scatter_kernel(
     x_ref, taps_ref, bias_ref, mask_ref, skip_ref, column_ref, row_ref, key_ref, query_ref,
     query_t_ref, block_ref, pick_ref, grad_ref, states_ref,
     normed_t_ref, gate_grad_ref, gated_ref, gated_t_ref, cotangent_ref, weight_ref, tokens_ref,
     x_grad_ref, key_grad_ref, query_grad_ref, sums_ref, rest_ref, channel_ref,
-    gate_raw_ref, out_raw_ref, layer_out_ref,
+    gate_raw_ref, out_raw_ref, layer_out_ref, squares_ref,
     padded, following, state_back, inner_grad, added, added_out, added_in, added_send, added_recv,
     *ring_scratch,
 ):
@@ -1054,8 +1065,13 @@
         ).astype(bf16)
         for i in range(3):
             added_copy(i).wait_send()
-        out_raw_ref[...] = out_ring.finish(out_term)
-        gate_raw_ref[...] = gate_ring.finish(gate_term)
+        out_raw = out_ring.finish(out_term)
+        out_raw_ref[...] = out_raw
+        gate_raw = gate_ring.finish(gate_term)
+        gate_raw_ref[...] = gate_raw.astype(bf16)
+        squares_ref[...] = jnp.broadcast_to(
+            total_squares(out_raw) + total_squares(gate_raw), squares_ref.shape
+        )
 
 
 def scan_scatter(
@@ -1074,7 +1090,7 @@
         grid=(groups,),
         in_specs=head_specs(length)
         + [
-            whole_spec(),
+            pl.BlockSpec((3, LANES, PAIR), lambda g: (g, 0, 0)),
             lane_spec(length),
             pl.BlockSpec((chunks, STATE, LANES), lambda g: (0, 0, g)),
         ]
@@ -1083,21 +1099,22 @@
             lane_spec(length),
             pl.BlockSpec((length, STATE), same),
             pl.BlockSpec((length, STATE), same),
-            pl.BlockSpec((length, PAIR), lambda g: (0, g)),
+            pl.BlockSpec((length, PAIR), same),
             pl.BlockSpec((chunks, 1, LANES), lambda g: (0, 0, g)),
             lane_spec(8),
         ]
-        + [whole_spec()] * 3,
+        + [whole_spec()] * 4,
         out_shape=[
             jax.ShapeDtypeStruct((length, width), bf16),
             jax.ShapeDtypeStruct((length, STATE), f32),
             jax.ShapeDtypeStruct((length, STATE), f32),
-            jax.ShapeDtypeStruct((length, PAIR * groups), f32),
+            jax.ShapeDtypeStruct((length, PAIR), f32),
             jax.ShapeDtypeStruct((chunks, 1, width), f32),
             jax.ShapeDtypeStruct((8, width), f32),
-            jax.ShapeDtypeStruct((rows_in, width), f32),
+            jax.ShapeDtypeStruct((rows_in, width), bf16),
             jax.ShapeDtypeStruct((rows_out, D), f32),
             jax.ShapeDtypeStruct((own, D), bf16),
+            jax.ShapeDtypeStruct((8, PAIR), f32),
         ],
         scratch_shapes=[
             pltpu.VMEM((length + 8, LANES), f32),
@@ -1118,9 +1135,442 @@
         name="scan_scatter",
     )(
         x, taps, bias, mask, skip, columns, rows, keys, queries, queries_t, block_mask(),
-        pick_masks(), grad, states,
+        pick_masks(groups), grad, states,
         normed_t, gate_grad, gated, gated_t, cotangent, weight, tokens,
     )
+
+
+def flipped(member, flip):
+    return member + flip - 2 * flip * lax.rem(lax.div(member, flip), 2)
+
+
+def shifted(value, by):
+    length = value.shape[1]
+    lane = lax.broadcasted_iota(jnp.int32, value.shape, 1)
+    if by == 0:
+        return value
+    if by > 0:
+        return jnp.where(lane >= by, pltpu.roll(value, by, 1), 0.0)
+    return jnp.where(lane < length + by, pltpu.roll(value, length + by, 1), 0.0)
+
+
+def last_scatter_kernel(
+    x_grad_ref, normed_t_ref, gate_grad_hbm, weight_gate_hbm, weight_x_hbm, weight_small_ref,
+    key_grad_ref, query_grad_ref, sums_ref, rest_ref, head_pick_ref, steps_ref, heads_ref,
+    shared_part_ref, shared_pre_ref, taps_ref, tokens_ref, cotangent_ref, inverse_ref, gain_ref,
+    gate_raw_ref, channel_ref, gate_gain_ref, squares_ref,
+    gate_back_ref, x_back_ref, small_back_ref, token_grad_ref, vectors_ref, total_ref,
+    gate_grad, weight_gate, weight_x, load_sem,
+    shared_own, shared_out, shared_in, swap_send, swap_recv, raw, small_t, small_n,
+    kept, back_out, back_in, back_send, back_recv,
+    vector_sum, vector_in, vector_send, vector_recv,
+    x_out, small_out, return_send, return_recv, local_sem,
+    scalar_out, scalar_in, scalar_send, scalar_recv,
+    *ring_scratch,
+):
+    ring = Ring()
+    d, f = ring.me, lax.axis_index("fsdp")
+    count = ring.count
+    x_ring = RingScatter(ring, *ring_scratch[:4])
+    small_ring = RingScatter(ring, *ring_scratch[4:])
+    loads = [
+        pltpu.make_async_copy(source, target, load_sem.at[i])
+        for i, (source, target) in enumerate(
+            [(gate_grad_hbm, gate_grad), (weight_gate_hbm, weight_gate), (weight_x_hbm, weight_x)]
+        )
+    ]
+    for load in loads:
+        load.start()
+    near = [{"fsdp": partner(k)} for k in (1, 2, 3)]
+    over = [{"dp": lax.rem(d + k, count)} for k in range(1, count)]
+    greet(near + over)
+    length, shared = x_grad_ref.shape[0], shared_own.shape[1]
+    rows, sub = x_out.shape[0], x_back_ref.shape[1]
+    tokens = tokens_ref.shape[0]
+
+    def rows_of(owner):
+        return pl.ds(pl.multiple_of(owner * rows, rows), rows)
+
+    def x_term(owner):
+        return dot_rows(normed_t_ref[rows_of(owner), :], x_grad_ref[...])
+
+    def small_term(owner):
+        return dot_lanes(normed_t_ref[rows_of(owner), :], small_t[...])
+
+    def to_partner(k, source, target, send, recv, at):
+        return pltpu.make_async_remote_copy(
+            source, target, send.at[at], recv.at[at],
+            device_id={"fsdp": partner(k)}, device_id_type=MESH,
+        )
+
+    def return_copy(part, k):
+        source = (gate_raw_ref, x_out, small_out)[part]
+        target = (gate_back_ref, x_back_ref, small_back_ref)[part]
+        return to_partner(
+            k, row_slice(source, partner(k) * sub, sub), target.at[f],
+            return_send, return_recv, part * 3 + k - 1,
+        )
+
+    def own_copy(part):
+        source = (gate_raw_ref, x_out, small_out)[part]
+        target = (gate_back_ref, x_back_ref, small_back_ref)[part]
+        return pltpu.make_async_copy(
+            row_slice(source, f * sub, sub), target.at[f], local_sem.at[part]
+        )
+
+    x_ring.start(0, x_term)
+
+    for i, ref in ((0, key_grad_ref), (2, query_grad_ref)):
+        turned = ref[...].T
+        for j in (0, 1):
+            shared_own[i + j] = turned[j * shared : (j + 1) * shared]
+            shared_out[i + j] = turned[j * shared : (j + 1) * shared].astype(bf16)
+
+    def shared_copy(k):
+        return to_partner(
+            k, shared_out.at[partner(k)], shared_in.at[k - 1], swap_send, swap_recv, k - 1
+        )
+
+    for k in (2, 3, 1):
+        shared_copy(k).start()
+    for k in (2, 3, 1):
+        return_copy(0, k).start()
+    own_copy(0).start()
+
+    at_row = lax.broadcasted_iota(jnp.int32, (SPAN, SPAN), 0)
+    at_lane = lax.broadcasted_iota(jnp.int32, (SPAN, SPAN), 1)
+    later = (at_lane >= at_row).astype(f32)
+    earlier = (at_lane < at_row).astype(f32)
+    precise = partial(jnp.dot, precision=highest, preferred_element_type=f32)
+    heads = HEADS // 4
+    rest = precise(rest_ref[...], head_pick_ref[...])
+    decay, head_mask = heads_ref[0:1, :], heads_ref[1:2, :]
+    step_bias_grad = jnp.zeros((1, PAIR), f32)
+    decay_grad = jnp.zeros((1, PAIR), f32)
+    for c in range(length // SPAN):
+        here = slice(c * SPAN, (c + 1) * SPAN)
+        sums = sums_ref[here, :]
+        log_grad = (
+            precise(later, sums)
+            + pltpu.roll(precise(earlier, sums), PAIR - heads, 1)
+            + rest[c : c + 1]
+        )
+        steps = steps_ref[here, :]
+        logits = pltpu.roll(steps, PAIR - heads, 1)
+        raw_grad = (decay * log_grad + pltpu.roll(sums, PAIR - 2 * heads, 1)) * jax.nn.sigmoid(
+            logits
+        )
+        step_bias_grad = step_bias_grad + jnp.sum(raw_grad, axis=0, keepdims=True)
+        decay_grad = decay_grad + jnp.sum(steps * log_grad, axis=0, keepdims=True)
+        raw[here, :] = raw_grad * head_mask
+    decay_grad = decay_grad * decay
+
+    x_ring.start(1, x_term)
+
+    for k in (2, 3, 1):
+        shared_copy(k).wait_recv()
+    part, pre = shared_part_ref[...], shared_pre_ref[...]
+    gate = jax.nn.sigmoid(pre)
+    pre_grad = shared_own[f]
+    for k in (1, 2, 3):
+        pre_grad = pre_grad + shared_in[k - 1].astype(f32)
+    pre_grad = pre_grad * (gate * (1.0 + pre * (1.0 - gate)))
+    shared_grad = jnp.zeros_like(pre_grad)
+    lane = lax.broadcasted_iota(jnp.int32, (shared, PAIR), 1)
+    shared_sums = jnp.where(lane == CONV, jnp.sum(pre_grad, axis=1, keepdims=True), 0.0)
+    for k in range(CONV):
+        shift = CONV - 1 - k
+        shared_grad = shared_grad + taps_ref[:, k : k + 1] * shifted(pre_grad, -shift)
+        shared_sums = shared_sums + jnp.where(
+            lane == k, jnp.sum(pre_grad * shifted(part, shift), axis=1, keepdims=True), 0.0
+        )
+    small_t[0:shared, :] = shared_grad.astype(bf16)
+    small_t[shared:, :] = raw[...].T[0 : PAIR - shared].astype(bf16)
+    small_n[...] = small_t[...].T
+    small_ring.start(0, small_term)
+
+    for load in loads:
+        load.wait()
+
+    def back_block(flip):
+        here = pl.ds(pl.multiple_of(partner(flip) * tokens, tokens), tokens)
+        return (
+            dot_lanes(gate_grad[here, :], weight_gate[...])
+            + dot_lanes(x_grad_ref[here, :], weight_x[...])
+            + dot_lanes(small_n[here, :], weight_small_ref[...])
+        )
+
+    def back_copy(i):
+        return to_partner(
+            2 if i == 2 else 1, back_out.at[i], back_in.at[i], back_send, back_recv, i
+        )
+
+    for i, flip in ((1, 3), (0, 1)):
+        back_out[i] = back_block(flip).astype(bf16)
+        back_copy(i).start()
+    value = back_block(2)
+    back_copy(1).wait_recv()
+    back_out[2] = (value + back_in[1].astype(f32)).astype(bf16)
+    back_copy(2).start()
+    x_ring.start(2, x_term)
+    small_ring.start(1, small_term)
+    kept[...] = back_block(0)
+    for hop in range(3, ring.far):
+        x_ring.start(hop, x_term)
+        small_ring.start(hop - 1, small_term)
+    back_copy(0).wait_recv()
+    back_copy(2).wait_recv()
+    inputs, inverse = tokens_ref[...].astype(f32), inverse_ref[...]
+    normed_grad = (kept[...] + back_in[0].astype(f32)) + back_in[2].astype(f32)
+    pulled = normed_grad * gain_ref[...]
+    scaled = inputs * inverse
+    input_grad = inverse * (
+        pulled - scaled * (jnp.sum(pulled * scaled, axis=1, keepdims=True) / D)
+    )
+    token_grad_ref[...] = (cotangent_ref[...].astype(f32) + input_grad).astype(bf16)
+    gain_grad = jnp.sum(normed_grad * scaled, axis=0, keepdims=True)
+
+    width = vector_sum.shape[1]
+    vector_sum[...] = jnp.zeros_like(vector_sum)
+    vector_sum[0:1, :] = gate_gain_ref[0:1, :]
+    vector_sum[1 : CONV + 3, :] = channel_ref[0 : CONV + 2, :]
+    for i in range(D // width):
+        vector_sum[CONV + 3 + i : CONV + 4 + i, :] = gain_grad[:, i * width : (i + 1) * width]
+    vector_sum[15:16, 0:PAIR] = step_bias_grad
+    vector_sum[15:16, PAIR : 2 * PAIR] = decay_grad
+    wide = jnp.concatenate([shared_sums, jnp.zeros((PAIR - shared, PAIR), f32)], axis=0)
+    vector_sum[16:24, 0:PAIR] = wide.T[0:8]
+
+    def vector_copy(step, flip):
+        return pltpu.make_async_remote_copy(
+            vector_in.at[step, 0], vector_in.at[step, 1], vector_send.at[step],
+            vector_recv.at[step],
+            device_id={"dp": flipped(d, flip)}, device_id_type=MESH,
+        )
+
+    flips = []
+    while 1 << len(flips) < count:
+        flips.append(1 << len(flips))
+    for step, flip in enumerate(flips):
+        vector_in[step, 0] = vector_sum[...]
+        vector_copy(step, flip).start()
+        if step == 0:
+            small_ring.start(ring.far - 1, small_term)
+        vector_copy(step, flip).wait_recv()
+        vector_sum[...] = vector_sum[...] + vector_in[step, 1]
+
+    def vector_spread(k):
+        return to_partner(
+            k, vector_sum, vectors_ref.at[f], vector_send, vector_recv, len(flips) + k - 1
+        )
+
+    for k in (2, 3, 1):
+        vector_spread(k).start()
+    vectors_ref[f] = vector_sum[...]
+
+    x_raw = x_ring.finish(x_term)
+    x_out[...] = x_raw.astype(bf16)
+    for k in (2, 3, 1):
+        return_copy(1, k).start()
+    own_copy(1).start()
+    small_raw = small_ring.finish(small_term)
+    small_out[...] = small_raw.astype(bf16)
+    for k in (2, 3, 1):
+        return_copy(2, k).start()
+    own_copy(2).start()
+
+    total = squares_ref[...] + jnp.broadcast_to(
+        total_squares(x_raw) + total_squares(small_raw), squares_ref.shape
+    )
+    scalar_out[0] = total
+
+    def near_scalar(k):
+        return to_partner(
+            k, scalar_out.at[0], scalar_in.at[k], scalar_send, scalar_recv, k
+        )
+
+    for k in (2, 3, 1):
+        near_scalar(k).start()
+    for k in (2, 3, 1):
+        near_scalar(k).wait_recv()
+    total = (total + scalar_in[1]) + (scalar_in[2] + scalar_in[3])
+    scalar_out[1] = total
+
+    def far_scalar(k):
+        member = d
+        for bit in flips:
+            if k & bit:
+                member = flipped(member, bit)
+        return pltpu.make_async_remote_copy(
+            scalar_out.at[1], scalar_in.at[3 + k], scalar_send.at[3 + k], scalar_recv.at[3 + k],
+            device_id={"dp": member}, device_id_type=MESH,
+        )
+
+    for k in range(count - 1, 0, -1):
+        far_scalar(k).start()
+    parts = [total]
+    for k in range(1, count):
+        far_scalar(k).wait_recv()
+        parts.append(scalar_in[3 + k])
+    while len(parts) > 1:
+        parts = [parts[i] + parts[i + 1] for i in range(0, len(parts), 2)]
+    total_ref[...] = parts[0]
+
+    for k in (1, 2, 3):
+        vector_spread(k).wait_recv()
+        vector_spread(k).wait_send()
+        shared_copy(k).wait_send()
+        near_scalar(k).wait_send()
+        for i in range(3):
+            return_copy(i, k).wait_recv()
+            return_copy(i, k).wait_send()
+    for k in range(1, count):
+        far_scalar(k).wait_send()
+    for i in range(3):
+        back_copy(i).wait_send()
+        own_copy(i).wait()
+    for step, flip in enumerate(flips):
+        vector_copy(step, flip).wait_send()
+
+
+def last_scatter(
+    x_grad, normed_t, gate_grad, weight_gate, weight_x, weight_small, key_grad, query_grad, sums,
+    rest, steps, head_rows, shared_part, shared_pre, taps, tokens, cotangent, inverse, gain,
+    gate_raw, channel, gate_gain, squares,
+):
+    length, width = x_grad.shape
+    count, members = lax.axis_size("dp"), lax.axis_size("fsdp")
+    rows = D // count
+    sub, own, shared = rows // members, tokens.shape[0], shared_part.shape[0]
+    hops = max(count - 1, 1).bit_length()
+    head_pick = (
+        jnp.arange(width)[:, None] // HEAD_DIM == jnp.arange(PAIR)[None, :]
+    ).astype(f32)
+    dma = pltpu.SemaphoreType.DMA
+    sd = jax.ShapeDtypeStruct
+    return pl.pallas_call(
+        last_scatter_kernel,
+        in_specs=[whole_spec()] * 2 + any_specs(3) + [whole_spec()] * 19,
+        out_specs=[whole_spec()] * 6,
+        out_shape=[
+            sd((members, sub, width), bf16),
+            sd((members, sub, width), bf16),
+            sd((members, sub, PAIR), bf16),
+            sd((own, D), bf16),
+            sd((members, 24, width), f32),
+            sd((8, PAIR), f32),
+        ],
+        scratch_shapes=[
+            pltpu.VMEM((length, width), bf16),
+            pltpu.VMEM((D, width), bf16),
+            pltpu.VMEM((D, width), bf16),
+            dma((3,)),
+            pltpu.VMEM((members, shared, length), f32),
+            pltpu.VMEM((members, shared, length), bf16),
+            pltpu.VMEM((members - 1, shared, length), bf16),
+            dma((3,)),
+            dma((3,)),
+            pltpu.VMEM((length, PAIR), f32),
+            pltpu.VMEM((PAIR, length), bf16),
+            pltpu.VMEM((length, PAIR), bf16),
+            pltpu.VMEM((own, D), f32),
+            pltpu.VMEM((3, own, D), bf16),
+            pltpu.VMEM((3, own, D), bf16),
+            dma((3,)),
+            dma((3,)),
+            pltpu.VMEM((24, width), f32),
+            pltpu.VMEM((hops, 2, 24, width), f32),
+            dma((hops + 3,)),
+            dma((hops + 3,)),
+            pltpu.VMEM((rows, width), bf16),
+            pltpu.VMEM((rows, PAIR), bf16),
+            dma((9,)),
+            dma((9,)),
+            dma((3,)),
+            pltpu.VMEM((2, 8, PAIR), f32),
+            pltpu.VMEM((3 + count, 8, PAIR), f32),
+            dma((3 + count,)),
+            dma((3 + count,)),
+        ]
+        + RingScatter.scratch(count, rows, width)
+        + RingScatter.scratch(count, rows, PAIR),
+        compiler_params=pltpu.CompilerParams(
+            collective_id=3, has_side_effects=True, vmem_limit_bytes=VMEM_BYTES
+        ),
+        name="last_scatter",
+    )(
+        x_grad, normed_t, gate_grad, weight_gate, weight_x, weight_small, key_grad, query_grad,
+        sums, rest, head_pick, steps, head_rows, shared_part, shared_pre, taps, tokens, cotangent,
+        inverse, gain, gate_raw, channel, gate_gain, squares,
+    )
+
+
+COLUMN_TILE = 512
+
+
+def step_in_kernel(
+    factor_ref, gate_ref, x_ref, small_ref, turn_ref, weight_ref, first_ref, second_ref,
+    grad_ref, moment_ref, square_ref, master_ref, rounded_ref, raw,
+):
+    step = pl.program_id(0)
+    tiles = INNER // COLUMN_TILE
+
+    def joined(ref):
+        return jnp.concatenate([ref[i] for i in range(ref.shape[0])], axis=1)
+
+    @pl.when(step < tiles)
+    def _():
+        raw[...] = joined(gate_ref).astype(f32)
+
+    @pl.when((step >= tiles) & (step < 2 * tiles))
+    def _():
+        raw[...] = joined(x_ref).astype(f32)
+
+    @pl.when(step == 2 * tiles)
+    def _():
+        raw[...] = dot_rows(joined(small_ref), turn_ref[...])
+
+    grad = raw[...] * factor_ref[0:1, 0:1]
+    moment, square, master = adamw(
+        weight_ref[...], first_ref[...], second_ref[...], grad, rate_in_proj
+    )
+    grad_ref[...] = grad
+    moment_ref[...] = moment
+    square_ref[...] = square
+    master_ref[...] = master
+    rounded_ref[...] = master.astype(bf16)
+
+
+def step_in(factor, gate, x, small, weight, first, second):
+    members, rows, width = x.shape
+    tiles = INNER // COLUMN_TILE
+    shared, heads = 2 * STATE // members, HEADS // members
+    target = jnp.arange(COLUMN_TILE)
+    head = target - 2 * STATE
+    source = jnp.where(
+        target < 2 * STATE,
+        target // shared * PAIR + target % shared,
+        head // 2 % members * PAIR + shared + head // (2 * members) * 2 + head % 2,
+    )
+    turn = (
+        (jnp.arange(members * PAIR)[:, None] == source[None, :])
+        & (target < 2 * STATE + HEADS)[None, :]
+    ).astype(bf16)
+    piece = lambda low: pl.BlockSpec(
+        (members, rows, PAIR), lambda j: (0, 0, jnp.clip(j - low, 0, tiles - 1))
+    )
+    flat = pl.BlockSpec((rows, COLUMN_TILE), lambda j: (0, j))
+    shape = jax.ShapeDtypeStruct(weight.shape, f32)
+    return pl.pallas_call(
+        step_in_kernel,
+        grid=(2 * tiles + 1,),
+        in_specs=[whole_spec(), piece(0), piece(tiles), whole_spec(), whole_spec()] + [flat] * 3,
+        out_specs=[flat] * 5,
+        out_shape=[shape] * 4 + [jax.ShapeDtypeStruct(weight.shape, bf16)],
+        scratch_shapes=[pltpu.VMEM((rows, COLUMN_TILE), f32)],
+        compiler_params=pltpu.CompilerParams(vmem_limit_bytes=VMEM_BYTES),
+        name="step_in",
+    )(factor, gate, x, small, turn, weight, first, second)
 
 
 def unpack(vectors):
@@ -1238,7 +1688,7 @@
         weight_shared, weight_x, normed, cotangents = gather_first(
             shared_cut, x_cut, normed_own, cotangent
         )
-        weight_shared = weight_shared[:, : shared + heads]
+        normed_t = normed.T
     else:
         weight_shared = gathered(shared_cut)
         weight_x = gathered(x_cut)
@@ -1258,7 +1708,7 @@
         weight_shared, normed, (((0,), (1,)), ((), ())), preferred_element_type=f32
     )
     shared_part = small[:shared]
-    step_raw = small[shared:] * head_mask[:, None]
+    step_raw = small[shared : shared + heads] * head_mask[:, None]
     shared_padded = jnp.pad(shared_part, ((0, 0), (CONV - 1, 0)))
     shared_pre = bias_shared[:, None] + sum(
         taps_shared[k][:, None] * shared_padded[:, k : k + length] for k in range(CONV)
@@ -1311,9 +1761,10 @@
     if in_kernels:
         (
             x_grad, key_grad, query_grad, sums, rest, channel_grad, gate_raw, out_raw, layer_out,
+            squares,
         ) = scan_scatter(
             x_part, *scan_inputs, queries_t, y_grad, states,
-            normed.T, gate_grad, gated_low, gated_low.T, cotangents, weight_out, tokens,
+            normed_t, gate_grad, gated_low, gated_low.T, cotangents, weight_out, tokens,
         )
     else:
         out_term = lax.dot_general(
@@ -1337,89 +1788,102 @@
         x_grad, key_grad, query_grad, sums, rest, channel_grad = scan_backward(
             x_part, *scan_inputs, queries_t, y_grad, states
         )
-    x_raw = scatter_rows(in_term(x_grad), "dp")
-
-    shared_grads = jnp.concatenate([key_grad, query_grad], axis=1).T.astype(bf16)
-    arrived = exchanged(shared_grads.reshape(fsdp, shared, length), "fsdp").astype(f32)
-    activated_grad = jnp.sum(arrived, axis=0)
-    shared_pre_grad = activated_grad * shared_gate * (1.0 + shared_pre * (1.0 - shared_gate))
-    shared_ahead = jnp.pad(shared_pre_grad, ((0, 0), (0, CONV - 1)))
-    shared_grad = sum(
-        taps_shared[k][:, None] * shared_ahead[:, CONV - 1 - k : CONV - 1 - k + length]
-        for k in range(CONV)
-    )
-    taps_shared_grad = jnp.stack(
-        [
-            jnp.sum(shared_pre_grad * shared_padded[:, k : k + length], axis=1)
+    if in_kernels:
+        steps = jnp.concatenate(
+            [step_sizes, step_logits, jnp.zeros((PAIR - 2 * heads, length), f32)]
+        ).T
+        head_consts = jnp.pad(jnp.stack([decay_own, head_mask]), ((0, 6), (0, PAIR - heads)))
+        gate_back, x_back, small_back, token_grad, vector_rows, squares = last_scatter(
+            x_grad, normed_t, gate_grad, weight_gate, weight_x, weight_shared, key_grad,
+            query_grad, sums, rest.reshape(chunks, inner), steps, head_consts, shared_part,
+            shared_pre, jnp.pad(taps_shared.T, ((0, 0), (0, PAIR - CONV))), tokens, cotangent,
+            inverse_in, norm_gain[None], gate_raw, channel_grad, gain_grad, squares,
+        )
+        squares = squares[0, 0]
+    else:
+        x_raw = scatter_rows(in_term(x_grad), "dp")
+
+        shared_grads = jnp.concatenate([key_grad, query_grad], axis=1).T.astype(bf16)
+        arrived = exchanged(shared_grads.reshape(fsdp, shared, length), "fsdp").astype(f32)
+        activated_grad = jnp.sum(arrived, axis=0)
+        shared_pre_grad = activated_grad * shared_gate * (1.0 + shared_pre * (1.0 - shared_gate))
+        shared_ahead = jnp.pad(shared_pre_grad, ((0, 0), (0, CONV - 1)))
+        shared_grad = sum(
+            taps_shared[k][:, None] * shared_ahead[:, CONV - 1 - k : CONV - 1 - k + length]
             for k in range(CONV)
-        ]
-    )
-    bias_shared_grad = jnp.sum(shared_pre_grad, axis=1)
-
-    sums = (
-        sums.reshape(length, groups, PAIR)[:, :, : 3 * GROUP]
-        .reshape(length, groups, 3, GROUP)
-        .transpose(2, 1, 3, 0)
-        .reshape(3, heads, chunks, SPAN)
-    )
-    before = (jnp.arange(SPAN)[:, None] < jnp.arange(SPAN)[None, :]).astype(f32)
-    rest = rest.reshape(chunks, heads, HEAD_DIM).sum(axis=2).T
-    log_grad = (
-        jnp.dot(sums[0], 1.0 - before, precision=highest)
-        + jnp.dot(sums[1], before, precision=highest)
-        + rest[:, :, None]
-    ).reshape(heads, length)
-    step_grad = decay_own[:, None] * log_grad + sums[2].reshape(heads, length)
-    raw_grad = step_grad * jax.nn.sigmoid(step_logits)
-    step_bias_grad = jnp.sum(raw_grad, axis=1)
-    decay_grad = jnp.sum(step_sizes * log_grad, axis=1) * decay_own
-    small_grad = jnp.concatenate([shared_grad, raw_grad * head_mask[:, None]], axis=0).astype(bf16)
-    small_raw = scatter_rows(
-        lax.dot_general(
-            normed, small_grad, (((0,), (1,)), ((), ())), preferred_element_type=f32
-        ).astype(bf16),
-        "dp",
-    )
-
-    def in_back(grad, weight, grad_dim=1):
-        return lax.dot_general(
-            grad, weight, (((grad_dim,), (1,)), ((), ())), preferred_element_type=f32
-        )
-
-    normed_grad = halved(
-        (
-            in_back(gate_grad, weight_gate)
-            + in_back(x_grad, weight_x)
-            + in_back(small_grad, weight_shared, 0)
-        )
-        .astype(bf16)
-        .reshape(fsdp, tokens.shape[0], D),
-        "fsdp",
-    )
-    pulled = normed_grad * norm_gain[None, :]
-    input_grad = inverse_in * pulled - inputs * (
-        inverse_in**3 * jnp.mean(pulled * inputs, axis=-1, keepdims=True)
-    )
-    token_grad = (cotangent.astype(f32) + input_grad).astype(bf16)
-    norm_gain_grad = jnp.sum(normed_grad * inputs * inverse_in, axis=0)
-
-    skip_grad = channel_grad[CONV + 1].reshape(heads, HEAD_DIM).sum(axis=1)
-    head_row = jnp.concatenate(
-        [
-            step_bias_grad, decay_grad, skip_grad, bias_shared_grad, taps_shared_grad.reshape(-1),
-        ]
-    )
-    head_row = jnp.pad(head_row, (0, inner - head_row.shape[0]))
-    vector_rows = jnp.concatenate(
-        [
-            gain_grad[0:1],
-            channel_grad[: CONV + 1],
-            head_row[None],
-            norm_gain_grad.reshape(-1, inner),
-        ]
-    )
-    vector_rows = jnp.pad(vector_rows, ((0, -vector_rows.shape[0] % 8), (0, 0)))
-    vector_rows = spread_small(summed_in_steps(vector_rows, "dp"), "fsdp")
+        )
+        taps_shared_grad = jnp.stack(
+            [
+                jnp.sum(shared_pre_grad * shared_padded[:, k : k + length], axis=1)
+                for k in range(CONV)
+            ]
+        )
+        bias_shared_grad = jnp.sum(shared_pre_grad, axis=1)
+
+        sums = sums.T[: 3 * heads].reshape(3, heads, chunks, SPAN)
+        before = (jnp.arange(SPAN)[:, None] < jnp.arange(SPAN)[None, :]).astype(f32)
+        rest = rest.reshape(chunks, heads, HEAD_DIM).sum(axis=2).T
+        log_grad = (
+            jnp.dot(sums[0], 1.0 - before, precision=highest)
+            + jnp.dot(sums[1], before, precision=highest)
+            + rest[:, :, None]
+        ).reshape(heads, length)
+        step_grad = decay_own[:, None] * log_grad + sums[2].reshape(heads, length)
+        raw_grad = step_grad * jax.nn.sigmoid(step_logits)
+        step_bias_grad = jnp.sum(raw_grad, axis=1)
+        decay_grad = jnp.sum(step_sizes * log_grad, axis=1) * decay_own
+        small_grad = jnp.concatenate([shared_grad, raw_grad * head_mask[:, None]], axis=0).astype(bf16)
+        small_raw = scatter_rows(
+            lax.dot_general(
+                normed, small_grad, (((0,), (1,)), ((), ())), preferred_element_type=f32
+            ).astype(bf16),
+            "dp",
+        )
+
+        def in_back(grad, weight, grad_dim=1):
+            return lax.dot_general(
+                grad, weight, (((grad_dim,), (1,)), ((), ())), preferred_element_type=f32
+            )
+
+        normed_grad = halved(
+            (
+                in_back(gate_grad, weight_gate)
+                + in_back(x_grad, weight_x)
+                + in_back(small_grad, weight_shared, 0)
+            )
+            .astype(bf16)
+            .reshape(fsdp, tokens.shape[0], D),
+            "fsdp",
+        )
+        pulled = normed_grad * norm_gain[None, :]
+        input_grad = inverse_in * pulled - inputs * (
+            inverse_in**3 * jnp.mean(pulled * inputs, axis=-1, keepdims=True)
+        )
+        token_grad = (cotangent.astype(f32) + input_grad).astype(bf16)
+        norm_gain_grad = jnp.sum(normed_grad * inputs * inverse_in, axis=0)
+
+        head_row = jnp.concatenate(
+            [jnp.pad(step_bias_grad, (0, PAIR - heads)), jnp.pad(decay_grad, (0, PAIR - heads))]
+        )
+        shared_rows = jnp.concatenate([taps_shared_grad, bias_shared_grad[None]])
+        vector_rows = jnp.concatenate(
+            [
+                gain_grad[0:1],
+                channel_grad[: CONV + 2],
+                norm_gain_grad.reshape(-1, inner),
+                jnp.zeros((15 - CONV - 3 - D // inner, inner), f32),
+                jnp.pad(head_row, (0, inner - 2 * PAIR))[None],
+                jnp.pad(shared_rows, ((0, 7 - CONV), (0, inner - shared))),
+            ]
+        )
+        vector_rows = spread_small(summed_in_steps(vector_rows, "dp"), "fsdp")
+        squares = (
+            jnp.sum(gate_raw * gate_raw)
+            + jnp.sum(x_raw * x_raw)
+            + jnp.sum(small_raw * small_raw)
+            + jnp.sum(out_raw * out_raw)
+        )
+        squares = summed(summed(jnp.broadcast_to(squares, (8, 128)), "fsdp"), "dp")[0, 0]
 
     def joined_channels(v):
         return v.reshape(fsdp, pairs, PAIR).transpose(1, 0, 2).reshape(INNER)
@@ -1427,69 +1891,68 @@
     def joined_heads(v):
         return v.reshape(fsdp, pairs, 2).transpose(1, 0, 2).reshape(HEADS)
 
-    head_all = vector_rows[:, CONV + 2]
-    taps_shared_all = (
-        head_all[:, 3 * heads + shared : 3 * heads + 5 * shared]
-        .reshape(fsdp, CONV, shared)
-        .transpose(1, 0, 2)
-        .reshape(CONV, 2 * STATE)
-    )
+    shared_all = vector_rows[:, 16 : 17 + CONV, :shared]
+    bias_shared_all = shared_all[:, CONV].reshape(-1)
     taps_all = [
-        jnp.concatenate([joined_channels(vector_rows[:, 1 + k]), taps_shared_all[k]])
+        jnp.concatenate([joined_channels(vector_rows[:, 1 + k]), shared_all[:, k].reshape(-1)])
         for k in range(CONV)
     ]
-    bias_all = jnp.concatenate(
-        [
-            joined_channels(vector_rows[:, CONV + 1]),
-            head_all[:, 3 * heads : 3 * heads + shared].reshape(-1),
-        ]
-    )
+    bias_all = jnp.concatenate([joined_channels(vector_rows[:, CONV + 1]), bias_shared_all])
     norm_rows = vector_rows[:, CONV + 3 : CONV + 3 + D // inner].reshape(fsdp, D)
     norm_all = norm_rows[0]
     for member in range(1, fsdp):
         norm_all = norm_all + norm_rows[member]
+    skip_all = vector_rows[:, CONV + 2].reshape(fsdp * heads, HEAD_DIM).sum(axis=1)
     vector_raw = jnp.concatenate(
         [norm_all, joined_channels(vector_rows[:, 0])]
         + taps_all
-        + [bias_all]
-        + [joined_heads(head_all[:, i * heads : (i + 1) * heads]) for i in range(3)]
-    )
-
-    squares = (
-        jnp.sum(gate_raw * gate_raw)
-        + jnp.sum(x_raw * x_raw)
-        + jnp.sum(small_raw * small_raw)
-        + jnp.sum(out_raw * out_raw)
-    )
-    squares = summed(summed(jnp.broadcast_to(squares, (8, 128)), "fsdp"), "dp")[0, 0]
+        + [
+            bias_all,
+            joined_heads(vector_rows[:, 15, :heads]),
+            joined_heads(vector_rows[:, 15, PAIR : PAIR + heads]),
+            joined_heads(skip_all),
+        ]
+    )
+
     grad_norm = jnp.sqrt(squares + jnp.sum(vector_raw * vector_raw))
     factor = jnp.minimum(1.0, clip_norm / (grad_norm + 1e-06))
-
-    def returned(raw):
-        return exchanged(raw.astype(bf16).reshape(fsdp, rows_in, raw.shape[1]), "fsdp")
-
-    def joined_columns(part):
-        return (
-            part.reshape(fsdp, rows_in, pairs, PAIR).transpose(1, 2, 0, 3).reshape(rows_in, INNER)
-        )
-
-    small_back = returned(small_raw)
-    in_raw = jnp.concatenate(
-        [
-            joined_columns(returned(gate_raw)),
-            joined_columns(returned(x_raw)),
-            small_back[:, :, :shared].transpose(1, 0, 2).reshape(rows_in, 2 * STATE),
-            small_back[:, :, shared:]
-            .reshape(fsdp, rows_in, pairs, 2)
-            .transpose(1, 2, 0, 3)
-            .reshape(rows_in, HEADS),
-        ],
-        axis=1,
-    ).astype(f32)
-    in_grad = in_raw * factor
+    if in_kernels:
+        in_grad, in_moment, in_square, in_master, in_rounded = step_in(
+            jnp.broadcast_to(factor, (8, PAIR)), gate_back, x_back, small_back,
+            in_weight, in_first, in_second,
+        )
+    else:
+
+        def returned(raw):
+            return exchanged(raw.astype(bf16).reshape(fsdp, rows_in, raw.shape[1]), "fsdp")
+
+        def joined_columns(part):
+            return (
+                part.reshape(fsdp, rows_in, pairs, PAIR)
+                .transpose(1, 2, 0, 3)
+                .reshape(rows_in, INNER)
+            )
+
+        small_back = returned(small_raw)
+        in_raw = jnp.concatenate(
+            [
+                joined_columns(returned(gate_raw)),
+                joined_columns(returned(x_raw)),
+                small_back[:, :, :shared].transpose(1, 0, 2).reshape(rows_in, 2 * STATE),
+                small_back[:, :, shared:]
+                .reshape(fsdp, rows_in, pairs, 2)
+                .transpose(1, 2, 0, 3)
+                .reshape(rows_in, HEADS),
+            ],
+            axis=1,
+        ).astype(f32)
+        in_grad = in_raw * factor
+        in_moment, in_square, in_master = adamw(
+            in_weight, in_first, in_second, in_grad, rate_in_proj
+        )
+        in_rounded = in_master.astype(bf16)
     out_grad = out_raw * factor
     vector_grad = vector_raw * factor
-    in_moment, in_square, in_master = adamw(in_weight, in_first, in_second, in_grad, rate_in_proj)
     out_moment, out_square, out_master = adamw(
         out_weight, out_first, out_second, out_grad, rate_out_proj
     )
@@ -1506,7 +1969,7 @@
         in_moment,
         in_square,
         in_master,
-        in_master.astype(bf16),
+        in_rounded,
         out_moment,
         out_square,
         out_master,

time: 743 us -> 528 us (0.71); the launches traced: 730 us -> 526 us
  local copies, waits for them, and re-layouts: 212 us -> 63.2 us
  Pallas kernels: 304 us -> 414 us
  starting transfers between devices: 53.7 us -> 3.72 us
  other arithmetic: 60.6 us -> 22.5 us
  matrix products: 40.7 us -> 4.45 us
  waiting for transfers between devices: 41 us -> 13 us
  between operations: 18.7 us -> 4.66 us
    dynamic_update_slice x20 -> x3, local copies, waits for them, and re-layouts: 104 us -> 4.7 us  [placed(): lax.dynamic_update_index_in_dim(whole, part, lax.bitwise_xor(me, flip), 0)]
    pallas_call x0 -> x2, Pallas kernels: none -> 95.9 us  [the longest x1 81.1 us: last_scatter(): pl.pallas_call(last_scatter_kernel, in_specs=[whole_spec()] * 2 + any_spe...]
    dot_general x7 -> x0, matrix products: 36.7 us -> none  [the longest x3 26.8 us: in_back(): lax.dot_general(grad, weight, (((grad_dim,), (1,)), ((), ())), preferred_...]
    ppermute x37 -> x6, starting transfers between devices: 35.9 us -> 3.72 us  [swapped(): return lax.ppermute(value, axis, [(i, i ^ flip) for i in range(count)])]
    convert_element_type x13 -> x2, other arithmetic: 24.5 us -> 1.99 us  [the longest x1 0.99 us: last_scatter(): head_pick = (jnp.arange(width)[:, None] // HEAD_DIM == jnp.arange(PAIR)[N...]
    broadcast_in_dim x8 -> x2, local copies, waits for them, and re-layouts: 19.4 us -> 0.59 us  [the longest x1 0.59 us: on_device(): jnp.broadcast_to(factor, (8, PAIR))]
    ppermute x16 -> x0, starting transfers between devices: 17.8 us -> none  [the longest x6 6.99 us: scatter_rows(): going_right = lax.ppermute(to_right.astype(bf16), axis, right)]
    ppermute x16 -> x0, waiting for transfers between devices: 16.3 us -> none  [the longest x6 12.8 us: scatter_rows(): going_right = lax.ppermute(to_right.astype(bf16), axis, right)]
  transfers between devices with their start and end apart: 53 -> 6, of which waited for: 12 -> 2; matrix products, arithmetic and copies ran while one was open for 33% -> 6% of each run, Pallas kernels for 0% -> 0%
where the time goes in v3:
time: 528 us; the launch traced here: 526 us
  Pallas kernels  414 us (78%)
  local copies, waits for them, and re-layouts  63.2 us (12%)
  other arithmetic  22.5 us (4%)
  waiting for transfers between devices  13 us (2%)
    pallas_call x1, Pallas kernels, scan_gather(): pl.pallas_call(scan_gather_kernel, grid=(width // LANES,), in_specs=[whol...  109 us
    pallas_call x1, Pallas kernels, scan_scatter(): pl.pallas_call(scan_scatter_kernel, grid=(groups,), in_specs=head_specs(l...  96.4 us
    pallas_call x1, Pallas kernels, last_scatter(): pl.pallas_call(last_scatter_kernel, in_specs=[whole_spec()] * 2 + any_spe...  81.1 us
    pallas_call x1, Pallas kernels, gather_first(): pl.pallas_call(gather_first_kernel, in_specs=any_specs(4), out_specs=any_...  73 us
    pallas_call x1, Pallas kernels, gate_forward(): pl.pallas_call(gate_kernel, grid=(length // ROW_TILE,), in_specs=[rows(D)...  30.8 us
    pallas_call x1, Pallas kernels, step_in(): pl.pallas_call(step_in_kernel, grid=(2 * tiles + 1,), in_specs=[whole_spe...  14.8 us
    ppermute x6, waiting for transfers between devices, swapped(): return lax.ppermute(value, axis, [(i, i ^ flip) for i in range(count)])  13 us
  transfers between devices with their start and end apart: 6, of which 2 were waited for; matrix products, arithmetic and copies ran while one was open for 6% of the time, Pallas kernels for 0%

profile of v3, /device:TPU:0, one launch (start us, length us, event | category | flops | bytes accessed | tf_op | source)
XLA Modules:
  0.0 526.0 jit_solution(16332359342277120550)
XLA Ops:
  0.7 3.4 copy.111
  5.4 1.7 copy.116
  10.4 73.0 %gather_first.1 = (bf16[2048,128]{1,0:T(8,128)(2,1)}, bf16[2048,1024]{1,0:T(8,128)(2,1)}, bf16[1024,2048]{1,0:T(8,128)(2,1)}, bf16[1024,2048]{1,0:T(8,128)(2,1)}) custom-call(bf16[4,64,128]{2,1,0:T(8,128)(2,1)} %fusion.34.small_cut, bf16[4,64,1024]{2,1,0:T(8,128)(2,1)} %reshape.942.x_cut, bf16[256,2048]{1,0:T(8,128)(2,1)} %fusion.2.normed_own, ...), custom_call_target="tpu_custom_call" | custom-call | tf_op jit(solution)/shard_map/gather_first/pallas_call | solution.py:859
  83.4 3.9 fusion.75
  90.0 1.4 collective-permute-start.1
  102.5 1.8 copy.146.column_ref
  109.5 1.6 bitcast_dynamic-update-slice_fusion.2
  111.1 1.6 bitcast_dynamic-update-slice_fusion.1
  112.6 1.6 bitcast_dynamic-update-slice_fusion
  117.0 109.4 %scan_gather.1 = (f32[1024,1024]{1,0:T(8,128)}, f32[1024,1024]{1,0:T(8,128)}, bf16[8,128,1024]{2,1,0:T(8,128)(2,1)}, bf16[2048,1024]{1,0:T(8,128)(2,1)}, bf16[1024,2048]{1,0:T(8,128)(2,1)}) custom-call(bf16[1024,2048]{1,0:T(8,128)(2,1)} %get-tuple-element.54.normed_ref, bf16[2048,1024]{1,0:T(8,128)(2,1)} %get-tuple-element.55.weight_ref.weight_x_hbm, ...), custom_call_target="tpu_custom_call" | custom-call | tf_op jit(solution)/shard_map/scan_gather/pallas_call | solution.py:949
  226.4 30.8 %gate_forward.1 = (f32[1024,1024]{1,0:T(8,128)}, f32[1024,1024]{1,0:T(8,128)}, f32[1024,128]{1,0:T(8,128)}) custom-call(bf16[1024,2048]{1,0:T(8,128)(2,1)} %get-tuple-element.54.normed_ref, bf16[2048,1024]{1,0:T(8,128)(2,1)} %get-tuple-element.59.weight_ref.weight_gate_hbm, bf16[1024,2048]{1,0:T(8,128)(2,1)} %get-tuple-element.60.cotangent_ref, ...), custom_call_target="tpu_custom_call" | custom-call | flops 8999999488 | bytes 28000000 | tf_op jit(solution)/shard_map/gate_forward/pallas_call | solution.py:544
  257.2 1.9 slice_bitcast_fusion
  259.1 1.4 collective-permute-start.4
  261.5 6.5 %copy.128 = bf16[1024,2048]{0,1:T(8,128)(2,1)} copy(bf16[1024,2048]{1,0:T(8,128)(2,1)} %get-tuple-element.54.normed_ref) | data formatting | bytes 8388608 | tf_op jit(solution)/shard_map/gather_first/pallas_call | solution.py:859
  268.0 2.1 stack.9.pick_ref
  271.5 2.5 collective-permute-done.4
  274.0 10.5 %collective-permute-done.5 = f32[2,1024]{0,1:T(8,128)S(1)} collective-permute-done((f32[2,1024]{0,1:T(8,128)}, f32[2,1024]{0,1:T(8,128)S(1)}, u32[]{:S(2)}, u32[]{:S(2)}) %collective-permute-start.5) | collective-permute-done | bytes 8224 | tf_op jit(solution)/shard_map/ppermute | solution.py:126
  286.1 9.0 %norm_back.1 = (bf16[1024,1024]{1,0:T(8,128)(2,1)}, bf16[1024,1024]{1,0:T(8,128)(2,1)}, bf16[1024,1024]{1,0:T(8,128)(2,1)}, f32[8,1024]{1,0:T(8,128)}) custom-call(f32[1024,1024]{1,0:T(8,128)} %get-tuple-element.58.y_ref, f32[1024,1024]{1,0:T(8,128)} %get-tuple-element.62.gate_part_ref, f32[1024,1024]{1,0:T(8,128)} %get-tuple-element.63.gated_grad_ref, ...), custom_call_target="tpu_custom_call" | custom-call | flops 30000000 | bytes 18000000 | tf_op jit(solution)/shard_map/norm_back/pallas_call | solution.py:591
  295.1 3.9 copy.129
  299.0 96.4 %scan_scatter.1 = (bf16[1024,1024]{1,0:T(8,128)(2,1)}, f32[1024,128]{1,0:T(8,128)}, f32[1024,128]{1,0:T(8,128)}, f32[1024,128]{1,0:T(8,128)}, f32[8,1,1024]{2,1,...) custom-call(f32[1024,1024]{1,0:T(8,128)} %get-tuple-element.57.x_ref, ...), custom_call_target="tpu_custom_call" | custom-call | tf_op jit(solution)/shard_map/scan_scatter/pallas_call | solution.py:1088
  395.5 1.4 copy.157
  396.8 81.1 %last_scatter.1 = (bf16[4,64,1024]{2,1,0:T(8,128)(2,1)}, bf16[4,64,1024]{2,1,0:T(8,128)(2,1)}, bf16[4,64,128]{2,1,0:T(8,128)(2,1)}, bf16[256,2048]{1,0:T(8,128)(...) custom-call(bf16[1024,1024]{1,0:T(8,128)(2,1)} %get-tuple-element.70.x_grad_ref, bf16[2048,1024]{1,0:T(8,128)(2,1)} %bitcast.109, ...), custom_call_target="tpu_custom_call" | custom-call | tf_op jit(solution)/shard_map/last_scatter/pallas_call | solution.py:1451
  478.0 1.5 slice_reduce_fusion.5
  479.5 1.3 fusion.72
  480.9 1.5 add_bitcast_fusion
  482.4 1.5 slice_reduce_fusion.6
  490.5 1.3 reshape_squeeze.44
  491.8 1.3 reshape_squeeze.46
  494.5 1.3 reshape_squeeze.50
  501.2 1.7 multiply_subtract_fusion.1
  502.9 3.8 fusion.66
  507.3 14.8 %step_in.1 = (f32[64,8512]{1,0:T(8,128)}, f32[64,8512]{1,0:T(8,128)}, f32[64,8512]{1,0:T(8,128)}, f32[64,8512]{1,0:T(8,128)}, bf16[64,8512]{1,0:T(8,128)(2,1)}) custom-call(f32[8,128]{1,0:T(8,128)} %broadcast_in_dim.58.factor_ref, bf16[4,64,1024]{2,1,0:T(8,128)(2,1)} %get-tuple-element.82.gate_ref, bf16[4,64,1024]{2,1,0:T(8,128)(2,1)} %get-tuple-element.83.x_ref, ...), custom_call_target="tpu_custom_call" | custom-call | tf_op jit(solution)/shard_map/step_in/pallas_call | solution.py:1564
  (166 shorter events, 44.5 us)
Async XLA Ops:
  4.0 1.1 copy-start.11
  5.2 3.0 copy-start
  5.2 5.3 copy-start.15
  83.4 4.0 slice-start
  83.4 4.4 slice-start.1
  87.3 5.1 copy-start.12
  87.4 7.9 %copy-start.2 = (f32[64,1024]{1,0:T(8,128)}, f32[64,1024]{1,0:T(8,128)S(1)}, u32[]{:S(2)}) copy-start(f32[64,1024]{1,0:T(8,128)S(1)} %slice.246.shared_part_ref) | copy-start | bytes 786436
  89.9 19.6 %collective-permute-start = (bf16[64,1024]{1,0:T(8,128)(2,1)}, bf16[64,1024]{1,0:T(8,128)(2,1)}, u32[]{:S(2)}, u32[]{:S(2)}) collective-permute-start(bf16[64,1024]{1,0:T(8,128)(2,1)} %get-tuple-element.112), channel_id=1, source_target_pairs={{0,1},{1,0},{2,3},{3,2},{4,5},{5,4},{6,7},{7,6},{8,9},{9,8},{10,11... | collective-permute-start | bytes 393224 | tf_op jit(solution)/shard_map/ppermute | solution.py:126
  90.0 21.1 %collective-permute-start.1 = (bf16[64,1024]{1,0:T(8,128)(2,1)}, bf16[64,1024]{1,0:T(8,128)(2,1)}, u32[]{:S(2)}, u32[]{:S(2)}) collective-permute-start(bf16[64,1024]{1,0:T(8,128)(2,1)} %get-tuple-element.112), channel_id=1, source_target_pairs={{0,2},{1,3},{2,0},{3,1},{4,6},{5,7},{6,4},{7,5},{8,10},{9,11},{10,... | collective-permute-start | bytes 393224 | tf_op jit(solution)/shard_map/ppermute | solution.py:126
  91.4 21.2 %collective-permute-start.2 = (bf16[64,1024]{1,0:T(8,128)(2,1)}, bf16[64,1024]{1,0:T(8,128)(2,1)}, u32[]{:S(2)}, u32[]{:S(2)}) collective-permute-start(bf16[64,1024]{1,0:T(8,128)(2,1)} %get-tuple-element.112), channel_id=1, source_target_pairs={{0,3},{1,2},{2,1},{3,0},{4,7},{5,6},{6,5},{7,4},{8,11},{9,10},{10,... | collective-permute-start | bytes 393224 | tf_op jit(solution)/shard_map/ppermute | solution.py:126
  101.3 1.0 copy-start.10
  104.3 3.6 copy-start.1
  115.3 1.7 copy-start.4
  115.3 111.1 %copy-start.3 = (bf16[2,64,1024]{2,1,0:T(8,128)(2,1)}, bf16[2,64,1024]{2,1,0:T(8,128)(2,1)S(1)}, u32[]{:S(2)}) copy-start(bf16[2,64,1024]{2,1,0:T(8,128)(2,1)S(1)} %get-tuple-element.120) | copy-start | bytes 786436
  259.1 12.4 %collective-permute-start.3 = (f32[2,1024]{0,1:T(8,128)}, f32[2,1024]{0,1:T(8,128)S(1)}, u32[]{:S(2)}, u32[]{:S(2)}) collective-permute-start(f32[2,1024]{0,1:T(8,128)} %slice_bitcast_fusion), channel_id=1, source_target_pairs={{0,1},{1,0},{2,3},{3,2},{4,5},{5,4},{6,7},{7,6},{8,9},{9,8},{10,11... | collective-permute-start | bytes 24584 | tf_op jit(solution)/shard_map/ppermute | solution.py:126
  259.1 14.9 %collective-permute-start.4 = (f32[2,1024]{0,1:T(8,128)}, f32[2,1024]{0,1:T(8,128)S(1)}, u32[]{:S(2)}, u32[]{:S(2)}) collective-permute-start(f32[2,1024]{0,1:T(8,128)} %slice_bitcast_fusion), channel_id=1, source_target_pairs={{0,2},{1,3},{2,0},{3,1},{4,6},{5,7},{6,4},{7,5},{8,10},{9,11},{10,... | collective-permute-start | bytes 24584 | tf_op jit(solution)/shard_map/ppermute | solution.py:126
  260.5 24.0 %collective-permute-start.5 = (f32[2,1024]{0,1:T(8,128)}, f32[2,1024]{0,1:T(8,128)S(1)}, u32[]{:S(2)}, u32[]{:S(2)}) collective-permute-start(f32[2,1024]{0,1:T(8,128)} %slice_bitcast_fusion), channel_id=1, source_target_pairs={{0,3},{1,2},{2,1},{3,0},{4,7},{5,6},{6,5},{7,4},{8,11},{9,10},{10,... | collective-permute-start | bytes 24584 | tf_op jit(solution)/shard_map/ppermute | solution.py:126
  261.5 22.9 %copy-start.5 = (f32[1024,128]{1,0:T(8,128)S(1)}, f32[1024,128]{1,0:T(8,128)}, u32[]{:S(2)}) copy-start(f32[1024,128]{1,0:T(8,128)} %get-tuple-element.64) | copy-start | bytes 1572868
  396.8 104.3 %copy-start.13 = (f32[28096]{0:T(1024)S(1)}, f32[28096]{0:T(1024)}, u32[]{:S(2)}) copy-start(f32[28096]{0:T(1024)} %param.21) | copy-start | bytes 337156
  396.8 104.4 %copy-start.14 = (f32[28096]{0:T(1024)S(1)}, f32[28096]{0:T(1024)}, u32[]{:S(2)}) copy-start(f32[28096]{0:T(1024)} %param.23) | copy-start | bytes 337156
  478.0 24.9 %copy-start.6 = (f32[128,2048]{1,0:T(8,128)S(1)}, f32[128,2048]{1,0:T(8,128)}, u32[]{:S(2)}) copy-start(f32[128,2048]{1,0:T(8,128)} %param.20) | copy-start | bytes 3145732
  478.0 24.9 %copy-start.7 = (f32[128,2048]{1,0:T(8,128)S(1)}, f32[128,2048]{1,0:T(8,128)}, u32[]{:S(2)}) copy-start(f32[128,2048]{1,0:T(8,128)} %param.19) | copy-start | bytes 3145732
  507.3 14.8 %copy-start.8 = (bf16[256,2048]{1,0:T(8,128)(2,1)S(1)}, bf16[256,2048]{1,0:T(8,128)(2,1)}, u32[]{:S(2)}) copy-start(bf16[256,2048]{1,0:T(8,128)(2,1)} %get-tuple-element.173) | copy-start | bytes 3145732
  522.1 1.6 copy-start.9
